TPU v7x, 256 devices: a whole 4x4x8 slice. The times are simulated.
256 devices in a mesh: row: 4 (over z_hi), col: 8 (over y, core), dep: 8 (over z_lo, x).
Axes of the slice: x: 4, y: 4, z: 8 (z_hi: 4, z_lo: 2; z = z_hi * 2 + z_lo), core: 2. Of those that a mesh axis runs over, the one named last changes fastest.
Arguments:
- activations: bfloat16 [512, 5120], P(('col', 'dep'), 'row'), may hold values from -30 to 30
- out_weight: bfloat16 [5120, 151936], P('row', ('col', 'dep')), may hold values from -1 to 1
- teacher_ids: int32 [512, 64], replicated, may hold values from 0 to 151935, as said below
- teacher_values: float32 [512, 64], replicated, may hold values from -8 to 310
Outputs:
- grad_activations: bfloat16 [512, 5120], P(('col', 'dep'), 'row')
- grad_weight: bfloat16 [5120, 151936], P('row', ('col', 'dep'))
Inputs may be any that keep to these rules, and one draw needn't show every extreme that they name: `teacher_ids`: each row names 64 different token ids.
All inputs are finite; a program needn't handle non-finite values.
Results may differ from a plain program's by a relative error of at most 0.0046.
Values may be sent and summed in bfloat16 or wider, within the bound.
No kernel may reach another device: no remote copies, remote signals or barrier semaphores. Data moves between devices by JAX's collectives and lax.ppermute only.
A program may use at most 128 MiB of HBM per device.

v0:
```python
import jax
import jax.numpy as jnp
from jax import lax
from jax.sharding import PartitionSpec as P

loss_scale = 64.0


def teacher_table(teacher_ids, teacher_values, first_col, shard_width):
    teacher_peak = jnp.max(teacher_values, axis=1, keepdims=True)
    teacher_exp = jnp.exp(teacher_values - teacher_peak)
    teacher = teacher_exp / jnp.sum(teacher_exp, axis=1, keepdims=True)
    local_col = teacher_ids - first_col
    inside = (local_col >= 0) & (local_col < shard_width)
    local_col = jnp.where(inside, local_col, shard_width)
    row_index = jnp.broadcast_to(
        jnp.arange(teacher_ids.shape[0], dtype=jnp.int32)[:, None], teacher_ids.shape
    )
    empty_table = jnp.zeros((teacher_ids.shape[0], shard_width), jnp.float32)
    return empty_table.at[row_index, local_col].add(teacher, mode="drop")


def logit_grad(logits, teacher_ids, teacher_values, first_col):
    row_peak = lax.pmax(jnp.max(logits, axis=1), ("col", "dep"))
    own_total = jnp.sum(jnp.exp(logits - row_peak[:, None]), axis=1)
    row_total = lax.psum(own_total, ("col", "dep"))
    student = jnp.exp(logits - row_peak[:, None]) / row_total[:, None]
    teacher_dense = teacher_table(teacher_ids, teacher_values, first_col, logits.shape[1])
    return (loss_scale * (student - teacher_dense)).astype(jnp.bfloat16)


def local(activations, out_weight, teacher_ids, teacher_values):
    shard_width = out_weight.shape[1]
    first_col = lax.axis_index(("col", "dep")) * shard_width
    gathered = lax.all_gather(activations, ("col", "dep"), axis=0, tiled=True)
    partial_logits = jnp.dot(gathered, out_weight, preferred_element_type=jnp.float32)
    logits = lax.psum(partial_logits, "row")
    grad_logits = logit_grad(logits, teacher_ids, teacher_values, first_col)
    grad_weight = lax.dot_general(
        gathered, grad_logits, (((0,), (0,)), ((), ())), preferred_element_type=jnp.float32
    ).astype(jnp.bfloat16)
    grad_inputs = lax.psum_scatter(
        lax.dot_general(
            grad_logits, out_weight, (((1,), (1,)), ((), ())), preferred_element_type=jnp.float32
        ),
        ("col", "dep"),
        scatter_dimension=0,
        tiled=True,
    ).astype(jnp.bfloat16)
    return (grad_inputs, grad_weight)


def solution(mesh):
    in_specs = (P(("col", "dep"), "row"), P("row", ("col", "dep")), P(), P())
    out_specs = (P(("col", "dep"), "row"), P("row", ("col", "dep")))
    return jax.shard_map(local, mesh=mesh, in_specs=in_specs, out_specs=out_specs, check_vma=False)
```

profile of v0, /device:TPU:2, one launch (start us, length us, event | category | flops | bytes accessed | tf_op | source)
XLA Modules:
  0.0 959.4 jit_solution(9128805454825943547)
XLA Ops:
  7.2 0.0 all-gather.2.cloned.1.call-start
  7.2 0.7 all-gather.2.cloned.1.call-update
  7.9 0.0 all-reduce.2.cloned.1.call-start
  7.9 162.5 %all-gather.2.cloned.1.call-done = bf16[512,1280]{1,0:T(8,128)(2,1)} async-done(((bf16[8,1280]{1,0:T(8,128)(2,1)}), bf16[512,1280]{1,0:T(8,128)(2,1)}) %all-gather.2.cloned.1.call-update) | async-done | bytes 1310736 | tf_op jit(solution)/shard_map/all_gather | solution.py:35
  170.4 8.8 fusion.9
  179.2 0.0 copy-start.1
  179.2 0.0 copy-start.3
  179.2 0.0 copy-start.2
  179.2 0.0 all-reduce.2.cloned.1.call-update
  179.2 0.0 reduce-scatter.2.cloned.1.call-start
  179.3 0.8 copy-done.1
  180.2 0.0 copy-done.3
  180.2 0.1 multiply_reduce_fusion
  180.3 0.0 copy-done.2
  180.3 0.1 and_reduce_fusion
  180.4 0.1 copy.7
  180.5 0.1 reshape.24
  180.7 0.0 copy-done
  180.8 0.1 copy.8
  180.9 0.1 reshape.26
  181.0 173.5 %scatter_custom_fusion = f32[1215488]{0:T(1024)} fusion(s32[32768]{0:T(1024)S(1)} %reshape.24, f32[32768]{0:T(1024)S(1)} %reshape.26, f32[]{:T(128)} %constant.9.clone.1), kind=kCustom, calls=%fused_computation.8 | custom fusion | flops 32768 | bytes 4861956
  354.5 6.2 reshape.22
  360.7 2.8 reduce_max.18
  363.5 147.3 %pmax.7 = f32[512]{0:T(512)S(1)} all-reduce(f32[512]{0:T(512)S(1)} %reduce_max.18), channel_id=1, replica_groups=mesh['row'=4,'col'=8,'dep'=8] {'col','dep'}, use_global_device_ids=true, to_apply=%region_2.0 | all-reduce | flops 512 | bytes 4096 | tf_op jit(solution)/shard_map/pmax | solution.py:24
  510.7 3.1 fusion.3
  513.8 144.0 %psum.15 = f32[512]{0:T(512)S(1)} all-reduce(f32[512]{0:T(512)S(1)} %fusion.3), channel_id=1, replica_groups=mesh['row'=4,'col'=8,'dep'=8] {'col','dep'}, use_global_device_ids=true, to_apply=%region_4.0 | all-reduce | flops 512 | bytes 4096 | tf_op jit(solution)/shard_map/psum | solution.py:26
  657.8 5.2 fusion.2
  663.0 7.8 fusion.10
  670.8 0.0 reduce-scatter.2.cloned.1.call-update
  670.9 6.5 fusion
  677.3 274.1 %reduce-scatter.2.cloned.1.call-done = f32[8,1280]{1,0:T(8,128)} async-done(((f32[512,1280]{1,0:T(8,128)}), f32[8,1280]{1,0:T(8,128)}) %reduce-scatter.2.cloned.1.call-update) | async-done | bytes 40976 | tf_op jit(solution)/shard_map/reduce_scatter | solution.py:42
  951.4 1.4 convert_element_type.13
  (8 shorter events, 0.2 us)
Async XLA Ops:
  7.2 163.3 %all-gather.2.cloned.1.call-start = ((), (), s32[]{:S(2)}) async-start(), calls=%async_computation.1 | async-start | bytes 1331200 | tf_op jit(solution)/shard_map/all_gather | solution.py:35
  7.9 352.8 %all-reduce.2.cloned.1.call-start = ((), (), s32[]{:S(2)}) async-start(), calls=%async_computation.2 | async-start | bytes 9732096 | tf_op jit(solution)/shard_map/psum | solution.py:37
  179.2 0.9 copy-start.1
  179.2 1.0 copy-start.3
  179.2 1.1 copy-start.2
  179.2 1.5 copy-start
  179.2 772.2 %reduce-scatter.2.cloned.1.call-start = ((), (), s32[]{:S(2)}) async-start(), calls=%async_computation.3 | async-start | bytes 2662400 | tf_op jit(solution)/shard_map/reduce_scatter | solution.py:42
Sparse Core Ops, SparseCore 0:
  9.8 160.5 all-gather.1
  179.3 178.2 all-reduce.1
  671.0 280.4 reduce-scatter.1
where the time goes:
time: 963 us; the launch traced here: 959 us
  waiting for transfers between devices  437 us (45%)
  blocking collectives  291 us (30%)
  other arithmetic  186 us (19%)
  matrix products  23.1 us (2%)
  between operations  13.8 us (1%)
    reduce_scatter x1, waiting for transfers between devices, local(): lax.psum_scatter(lax.dot_general(grad_logits, out_weight, (((1,), (1,)),...  274 us
    unnamed x4, other arithmetic  174 us
    all_gather x1, waiting for transfers between devices, local(): gathered = lax.all_gather(activations, ('col', 'dep'), axis=0, tiled=True)  162 us
    pmax x1, blocking collectives, logit_grad(): row_peak = lax.pmax(jnp.max(logits, axis=1), ('col', 'dep'))  147 us
    psum x1, blocking collectives, logit_grad(): row_total = lax.psum(own_total, ('col', 'dep'))  144 us
  transfers between devices with their start and end apart: 3, of which 2 were waited for; matrix products, arithmetic and copies ran while one was open for 19% of the time, Pallas kernels for 0%

commit v1 on v0

v1 whole, which is shorter than its diff:
```python
import functools

import jax
import jax.numpy as jnp
from jax import lax
from jax.experimental import pallas as pl
from jax.experimental.pallas import tpu as pltpu
from jax.sharding import Mesh, PartitionSpec as P

LOSS_SCALE = 64.0
CODE_SCALE = 65535.0
CODE_OFFSET = 32768.0
F32 = jnp.float32
BF16 = jnp.bfloat16
I16 = jnp.int16
I32 = jnp.int32
VMEM = pl.BlockSpec(memory_space=pltpu.VMEM)
SMEM = pl.BlockSpec(memory_space=pltpu.SMEM)
PARAMS = pltpu.CompilerParams(vmem_limit_bytes=20 * 1024 * 1024)
CHIP = ("y", "z_lo", "x")
SHARD = ("y", "core", "z_lo", "x")


def cost(flops, bytes_accessed, exps=0):
    return pl.CostEstimate(flops=flops, bytes_accessed=bytes_accessed, transcendentals=exps)


def lanes_of(shape):
    return lax.broadcasted_iota(I32, shape, 1)


def encode(x, width):
    lane = lanes_of(x.shape)
    inside = lane < width
    high = jnp.max(jnp.where(inside, x, -jnp.inf), axis=1, keepdims=True)
    low = jnp.min(jnp.where(inside, x, jnp.inf), axis=1, keepdims=True)
    size = jnp.maximum(jnp.abs(high), jnp.abs(low))
    step = jnp.maximum(jnp.maximum((high - low) * (1.0 / 65000.0), size * 2.0**-22), 1e-30)
    power = jnp.ceil(jnp.log2(step))
    inverse = jnp.exp2(-power)
    middle = jnp.round((0.5 * high + 0.5 * low) * inverse)
    upper = jnp.floor(middle * (1.0 / 4096.0))
    lower = middle - upper * 4096.0
    code = jnp.clip(jnp.round(x * inverse) - middle, -32767.0, 32767.0)
    code = jnp.where(lane == width, power, code)
    code = jnp.where(lane == width + 1, upper, code)
    code = jnp.where(lane == width + 2, lower, code)
    return code.astype(I32).astype(I16)


def decode(code, width):
    value = code.astype(I32).astype(F32)
    step = jnp.exp2(value[:, width : width + 1])
    middle = value[:, width + 1 : width + 2] * 4096.0 + value[:, width + 2 : width + 3]
    return (value + middle) * step


def logits_kernel(width, row_ref, act_ref, weight_ref, own_ref, right_ref, left_ref, merge_right_ref, merge_left_ref, acc_ref):
    tokens = act_ref.shape[0]
    quarter, half = tokens // 4, tokens // 8
    padded = acc_ref.shape[1]
    tail = padded - 128
    acc_ref[:, tail:padded] = jnp.zeros((tokens, 128), F32)
    act = act_ref[...]
    for start in range(0, width, 512):
        stop = min(start + 512, width)
        acc_ref[:, start:stop] = lax.dot_general(
            act, weight_ref[start:stop, :], (((1,), (1,)), ((), ())), preferred_element_type=F32
        )
    row = row_ref[0]

    def piece(distance, which):
        first = lax.rem(row + distance, 4) * quarter + which * half
        return acc_ref[pl.ds(pl.multiple_of(first, half), half), :]

    own_ref[0:half, :] = piece(0, 0)
    own_ref[half:quarter, :] = piece(0, 1)
    right_ref[0:half, :] = encode(piece(1, 1), width)
    right_ref[half:quarter, :] = encode(piece(2, 0), width)
    left_ref[0:half, :] = encode(piece(3, 0), width)
    left_ref[half:quarter, :] = encode(piece(2, 1), width)
    merge_right_ref[...] = piece(1, 0)
    merge_left_ref[...] = piece(3, 1)


def merge_kernel(width, from_left_ref, from_right_ref, merge_right_ref, merge_left_ref, right_ref, left_ref):
    half = merge_right_ref.shape[0]
    right_ref[...] = encode(merge_right_ref[...] + decode(from_left_ref[half : 2 * half, :], width), width)
    left_ref[...] = encode(merge_left_ref[...] + decode(from_right_ref[half : 2 * half, :], width), width)


def column_to_row(column, offset):
    shape = (column.shape[0], 128)
    here = lax.broadcasted_iota(I32, shape, 0) + offset == lanes_of(shape)
    return jnp.sum(jnp.where(here, column, 0.0), axis=0, keepdims=True)


def row_to_column(row, count, offset):
    shape = (count, 128)
    here = lax.broadcasted_iota(I32, shape, 0) + offset == lanes_of(shape)
    return jnp.sum(jnp.where(here, row, 0.0), axis=1, keepdims=True)


def chunk_of(place_ref, which_chunk):
    core = place_ref[1]
    return core if which_chunk == 0 else 1 - core


def total_kernel(width, which_chunk, place_ref, own_ref, left_one_ref, right_one_ref, left_two_ref, right_two_ref, before_ref, code_ref, stats_ref):
    half, padded = left_two_ref.shape
    offset = chunk_of(place_ref, which_chunk) * (2 * half)
    inside = lanes_of((half, padded)) < width
    peaks, totals = [], []
    for which, one_ref, two_ref in ((0, right_one_ref, left_two_ref), (1, left_one_ref, right_two_ref)):
        rows = slice(which * half, (which + 1) * half)
        logits = own_ref[rows, :] + decode(one_ref[0:half, :], width) + decode(two_ref[...], width)
        logits = jnp.where(inside, logits, -jnp.inf)
        peak = jnp.max(logits, axis=1, keepdims=True)
        weight = jnp.exp(logits - peak)
        code_ref[rows, :] = (jnp.round(weight * CODE_SCALE) - CODE_OFFSET).astype(I32).astype(I16)
        peaks.append(column_to_row(peak, offset + which * half))
        totals.append(column_to_row(jnp.sum(weight, axis=1, keepdims=True), offset + which * half))
    peak, total = peaks[0] + peaks[1], totals[0] + totals[1]
    stats_ref[...] = before_ref[...] + jnp.concatenate([peak, total, jnp.zeros((6, 128), F32)], axis=0)


def teacher_kernel(width, place_ref, ids_ref, values_ref, dense_ref):
    groups, pairs = ids_ref.shape
    tiles = dense_ref.shape[1] // 128
    key_row = lax.broadcasted_iota(I32, (tiles * 8, pairs), 0)
    low_row = lax.broadcasted_iota(I32, (128, pairs), 0)
    token = lax.broadcasted_iota(I32, (1, pairs), 1) // (pairs // 8)
    lane = lax.broadcasted_iota(I32, (8, 128), 1)
    contract = (((1,), (1,)), ((), ()))

    def group(g, _):
        ids = ids_ref[pl.ds(g, 1), :] - place_ref[0]
        value = values_ref[pl.ds(g, 1), :]
        coarse = value.astype(BF16).astype(F32)
        key = lax.shift_right_arithmetic(ids, 7) * 8 + token
        here = key_row == key
        one_hot = jnp.where(low_row == (ids & 127), 1.0, 0.0).astype(BF16)
        dense = lax.dot_general(
            jnp.where(here, coarse, 0.0).astype(BF16), one_hot, contract, preferred_element_type=F32
        )
        dense += lax.dot_general(
            jnp.where(here, value - coarse, 0.0).astype(BF16), one_hot, contract, preferred_element_type=F32
        )
        rows = pl.ds(pl.multiple_of(g * 8, 8), 8)
        for tile in range(tiles):
            block = dense[tile * 8 : tile * 8 + 8, :]
            if tile == tiles - 1:
                block = jnp.where(lane + tile * 128 < width, block, 0.0)
            dense_ref[rows, tile * 128 : tile * 128 + 128] = block
        return 0

    lax.fori_loop(0, groups, group, 0)


def scale_kernel(stats_ref, own_ref, scale_ref):
    peaks = stats_ref[:, 0, :]
    peak = jnp.max(peaks, axis=0, keepdims=True)
    total = jnp.sum(jnp.exp(peaks - peak) * stats_ref[:, 1, :], axis=0, keepdims=True)
    scale = jnp.exp(own_ref[0:1, :] - peak) / total * (LOSS_SCALE / CODE_SCALE)
    scale_ref[...] = jnp.broadcast_to(scale, scale_ref.shape)


def hidden_kernel(
    width, which_chunk, place_ref, own_ref, left_ref, right_ref, left_two_ref, right_two_ref,
    scale_own_ref, scale_left_ref, scale_right_ref, scale_far_ref, dense_ref, weight_ref,
    hidden_ref, grad_ref, last_ref,
):
    quarter, padded = own_ref.shape
    half = quarter // 2
    row, chunk = place_ref[0], chunk_of(place_ref, which_chunk)

    def put(distance, which, code_ref, scale_ref):
        owner = lax.rem(row + distance, 4)
        count = code_ref.shape[0]
        first = pl.multiple_of(owner * quarter + which * half, half)
        token = pl.multiple_of((2 * owner + chunk) * quarter + which * half, half)
        scale = row_to_column(scale_ref[0:1, :], count, chunk * quarter + which * half)
        student = (code_ref[...].astype(I32).astype(F32) + CODE_OFFSET) * scale
        grad = student - LOSS_SCALE * dense_ref[pl.ds(token, count), :]
        grad_ref[pl.ds(first, count), :] = grad.astype(BF16)

    put(0, 0, own_ref, scale_own_ref)
    put(3, 0, left_ref, scale_left_ref)
    put(1, 0, right_ref, scale_right_ref)
    put(2, 0, left_two_ref, scale_far_ref)
    put(2, 1, right_two_ref, scale_far_ref)
    tail = padded - 128
    last_ref[...] = jnp.zeros(last_ref.shape, BF16)
    last_ref[0 : width - tail, :] = weight_ref[tail:width, :]
    total = jnp.dot(grad_ref[:, 0:tail], weight_ref[0:tail, :], preferred_element_type=F32)
    total += jnp.dot(grad_ref[:, tail:padded], last_ref[...], preferred_element_type=F32)
    hidden_ref[...] = total.astype(hidden_ref.dtype)


def weight_kernel(act_a_ref, act_b_ref, grad_a_ref, grad_b_ref, out_ref):
    contract = (((0,), (0,)), ((), ()))
    total = lax.dot_general(grad_a_ref[...], act_a_ref[...], contract, preferred_element_type=F32)
    total += lax.dot_general(grad_b_ref[...], act_b_ref[...], contract, preferred_element_type=F32)
    out_ref[...] = total.astype(BF16)


def pair_kernel(keep_ref, received_ref, sum_ref):
    sum_ref[...] = (keep_ref[...] + received_ref[...]).astype(BF16)


def forward_kernel(a_left_ref, a_right_ref, b_left_ref, b_right_ref, a_first_ref, a_second_ref, b_first_ref, b_second_ref):
    half = a_first_ref.shape[0]
    a_first_ref[...] = a_left_ref[0:half, :]
    a_second_ref[...] = a_right_ref[half : 2 * half, :]
    b_first_ref[...] = b_left_ref[0:half, :]
    b_second_ref[...] = b_right_ref[half : 2 * half, :]


def finish_kernel(part_ref, out_ref):
    out_ref[...] = jnp.sum(part_ref[...].astype(F32), axis=0).astype(BF16)


def shape(dims, dtype):
    return jax.ShapeDtypeStruct(dims, dtype)


def ring(x, step):
    return lax.ppermute(x, "row", [(i, (i + step) % 4) for i in range(4)])


def swap(x):
    return lax.ppermute(x, "core", [(0, 1), (1, 0)])


def local(activations, out_weight, teacher_ids, teacher_values):
    own_tokens, depth = activations.shape
    width = out_weight.shape[1]
    padded = (width + 127) // 128 * 128
    row, core = lax.axis_index("row"), lax.axis_index("core")
    chips = 32
    tokens = chips * own_tokens
    quarter, half = tokens // 4, tokens // 8
    first_col = lax.axis_index(SHARD) * width
    places = jnp.stack([row, core]).astype(I32)

    mine = lax.all_to_all(jnp.broadcast_to(activations[None], (chips, own_tokens, depth)), CHIP, 0, 0)
    mine = mine.reshape(tokens, depth)
    acts = [mine, swap(mine)]
    weight = out_weight.T

    def call(kernel, outs, ins, estimate, scratch=(), after=()):
        count = len(ins)
        ordered = count + len(after)

        def body(*refs):
            kernel(*refs[:count], *refs[ordered:])

        return pl.pallas_call(
            body,
            out_shape=outs,
            in_specs=[SMEM if x.ndim == 1 else VMEM for x in ins] + [pl.BlockSpec(memory_space=pl.ANY)] * len(after),
            out_specs=jax.tree.map(lambda _: VMEM, outs),
            scratch_shapes=scratch,
            compiler_params=PARAMS,
            cost_estimate=estimate,
        )(*ins, *after)

    matmul_flops = 2 * tokens * depth * width
    weight_bytes = depth * padded * 2

    def partial_logits(chunk, after):
        return call(
            functools.partial(logits_kernel, width),
            (
                shape((quarter, padded), F32),
                shape((quarter, padded), I16),
                shape((quarter, padded), I16),
                shape((half, padded), F32),
                shape((half, padded), F32),
            ),
            (places, acts[chunk], weight),
            cost(1, 1),
            [pltpu.VMEM((tokens, padded), F32)],
            after,
        )

    def merge(parts, received, after):
        return call(
            functools.partial(merge_kernel, width),
            (shape((half, padded), I16), shape((half, padded), I16)),
            (*received, parts[3], parts[4]),
            cost(1, 1),
            (),
            after,
        )

    def total(chunk, parts, one, two, before, after):
        return call(
            functools.partial(total_kernel, width, chunk),
            (shape((quarter, padded), I16), shape((8, 128), F32)),
            (places, parts[0], *one, *two, before),
            cost(1, 1),
            (),
            after,
        )

    def hidden(chunk, own, near, far, after):
        return call(
            functools.partial(hidden_kernel, width, chunk),
            (shape((tokens, depth), F32), shape((tokens, padded), BF16)),
            (places, own, *near, *far, *scales, dense, weight),
            cost(1, 1),
            [pltpu.VMEM((128, depth), BF16)],
            after,
        )

    def both_ways(right, left):
        return ring(right, 1), ring(left, 3)

    def all_stats(stats):
        return lax.all_to_all(jnp.broadcast_to(stats[None], (64, 8, 128)), SHARD, 0, 0)

    parts_a = partial_logits(0, ())
    one_a = both_ways(parts_a[1], parts_a[2])
    parts_b = partial_logits(1, parts_a[3:4])
    one_b = both_ways(parts_b[1], parts_b[2])
    merged_a = merge(parts_a, one_a, parts_b[3:4])
    two_a = both_ways(*merged_a)
    merged_b = merge(parts_b, one_b, merged_a[:1])
    two_b = both_ways(*merged_b)
    code_a, stats_a = total(0, parts_a, one_a, two_a, jnp.zeros((8, 128), F32), merged_b[:1])
    near_a = both_ways(code_a, code_a)
    code_b, stats = total(1, parts_b, one_b, two_b, stats_a, (code_a,))
    near_b = both_ways(code_b, code_b)

    pairs = 8 * teacher_ids.shape[1]
    teacher = jax.nn.softmax(teacher_values, axis=1)
    dense = call(
        functools.partial(teacher_kernel, width),
        shape((2 * tokens, padded), F32),
        (jnp.stack([first_col, row]).astype(I32), teacher_ids.reshape(-1, pairs), teacher.reshape(-1, pairs)),
        cost(1, 1),
        (),
        (code_b,),
    )
    scale = call(scale_kernel, shape((8, 128), F32), (all_stats(stats), stats), cost(1, 1), (), (dense,))
    scales = (scale, ring(scale, 1), ring(scale, 3), ring(scale, 2))

    forward = call(
        forward_kernel, (shape((half, padded), I16),) * 4, (*near_a, *near_b), cost(1, 1), (), (scale,)
    )
    far_b = both_ways(forward[2], forward[3])
    far_a = both_ways(forward[0], forward[1])
    hidden_b, full_b = hidden(1, code_b, near_b, far_b, (forward[0],))
    received = swap(hidden_b)
    hidden_a, full_a = hidden(0, code_a, near_a, far_a, (full_b,))
    summed = call(pair_kernel, shape((tokens, depth), BF16), (hidden_a, received), cost(1, 1))
    partial = lax.all_to_all(summed.reshape(chips, own_tokens, depth), CHIP, 0, 0)

    tile = 512
    whole = pl.BlockSpec((tokens, depth), lambda i: (0, 0))
    columns = pl.BlockSpec((tokens, tile), lambda i: (0, i))
    grad_weight = pl.pallas_call(
        weight_kernel,
        out_shape=shape((width, depth), BF16),
        grid=(pl.cdiv(width, tile),),
        in_specs=[whole, whole, columns, columns],
        out_specs=pl.BlockSpec((tile, depth), lambda i: (i, 0)),
        compiler_params=pltpu.CompilerParams(vmem_limit_bytes=58 * 1024 * 1024),
        cost_estimate=cost(2 * matmul_flops, weight_bytes),
    )(acts[0], acts[1], full_a, full_b)

    grad_inputs = call(
        finish_kernel, shape((own_tokens, depth), BF16), (partial,), cost(1, 1), (), (grad_weight,)
    )
    return (grad_inputs, grad_weight.T)


def solution(mesh):
    fine = Mesh(mesh.devices.reshape(4, 4, 2, 2, 4), ("row", "y", "core", "z_lo", "x"))
    specs = (P(SHARD, "row"), P("row", SHARD))
    return jax.shard_map(local, mesh=fine, in_specs=specs + (P(), P()), out_specs=specs, check_vma=False)
```

time: 963 us -> 180 us (0.19)
  waiting for transfers between devices: 437 us -> 39.5 us
  blocking collectives: 291 us -> 20.9 us
  other arithmetic: 186 us -> 0.26 us
  starting transfers between devices: 0.12 us -> 60.6 us
  Pallas kernels: 0 us -> 42 us
  matrix products: 23.1 us -> 0 us
  between operations: 13.8 us -> 0.91 us
    reduce_scatter x1 -> x0, waiting for transfers between devices: 274 us -> none  [local(): lax.psum_scatter(lax.dot_general(grad_logits, out_weight, (((1,), (1,)),...]
    unnamed x4 -> x0, other arithmetic: 174 us -> none
    all_gather x1 -> x0, waiting for transfers between devices: 162 us -> none  [local(): gathered = lax.all_gather(activations, ('col', 'dep'), axis=0, tiled=True)]
    pmax x1 -> x0, blocking collectives: 147 us -> none  [logit_grad(): row_peak = lax.pmax(jnp.max(logits, axis=1), ('col', 'dep'))]
    psum x1 -> x0, blocking collectives: 144 us -> none  [logit_grad(): row_total = lax.psum(own_total, ('col', 'dep'))]
    ppermute x0 -> x21, starting transfers between devices: none -> 42.1 us  [the longest x19 42 us: ring(): return lax.ppermute(x, 'row', [(i, (i + step) % 4) for i in range(4)])]
    pallas_call x0 -> x14, Pallas kernels: none -> 42 us  [the longest x13 34 us: call(): pl.pallas_call(body, out_shape=outs, in_specs=[SMEM if x.ndim == 1 else V...]
    ppermute x0 -> x21, waiting for transfers between devices: none -> 35.1 us  [the longest x19 35.1 us: ring(): return lax.ppermute(x, 'row', [(i, (i + step) % 4) for i in range(4)])]
  transfers between devices with their start and end apart: 3 -> 23, of which waited for: 2 -> 10; matrix products, arithmetic and copies ran while one was open for 19% -> 0% of each run, Pallas kernels for 0% -> 20%
where the time goes in v1:
time: 180 us; the launch traced here: 179 us
  starting transfers between devices  60.6 us (34%)
  Pallas kernels  42 us (23%)
  waiting for transfers between devices  39.5 us (22%)
  blocking collectives  20.9 us (12%)
  local copies, waits for them, and re-layouts  15.2 us (8%)
    ppermute x19, starting transfers between devices, ring(): return lax.ppermute(x, 'row', [(i, (i + step) % 4) for i in range(4)])  42 us
    ppermute x19, waiting for transfers between devices, ring(): return lax.ppermute(x, 'row', [(i, (i + step) % 4) for i in range(4)])  35.1 us
    pallas_call x13, Pallas kernels, call(): pl.pallas_call(body, out_shape=outs, in_specs=[SMEM if x.ndim == 1 else V...  34 us
    all_to_all x1, blocking collectives, local(): lax.all_to_all(jnp.broadcast_to(activations[None], (chips, own_tokens, de...  20.9 us
    unnamed x27, local copies, waits for them, and re-layouts  13.4 us
    all_to_all x1, starting transfers between devices, local(): lax.all_to_all(summed.reshape(chips, own_tokens, depth), CHIP, 0, 0)  11.7 us
    pallas_call x1, Pallas kernels, local(): pl.pallas_call(weight_kernel, out_shape=shape((width, depth), BF16), grid...  7.99 us
    all_to_all x1, starting transfers between devices, all_stats(): lax.all_to_all(jnp.broadcast_to(stats[None], (64, 8, 128)), SHARD, 0, 0)  6.86 us
  transfers between devices with their start and end apart: 23, of which 10 were waited for; matrix products, arithmetic and copies ran while one was open for 0% of the time, Pallas kernels for 20%

profile of v1, /device:TPU:2, one launch (start us, length us, event | category | flops | bytes accessed | tf_op | source)
XLA Modules:
  0.0 179.4 jit_solution(12586917017240887579)
XLA Ops:
  1.4 20.9 %all_to_all.15 = bf16[32,8,1280]{2,1,0:T(8,128)(2,1)S(1)} all-to-all(bf16[32,8,1280]{2,1,0:T(8,128)(2,1)S(1)} %broadcast_in_dim.6), channel_id=1, replica_groups=mesh['row'=4,'y'=4,'core'=2,'z_lo'=2,'x'=4] {'y','z_lo','x'}, dimensions={0} | all-to-all | bytes 1310720 | tf_op jit(solution)/shard_map/all_to_all | solution.py:246
  22.4 2.9 %copy-done = bf16[1280,2374]{0,1:T(8,128)(2,1)S(1)} copy-done((bf16[1280,2374]{0,1:T(8,128)(2,1)S(1)}, bf16[1280,2374]{0,1:T(8,128)(2,1)}, u32[]{:S(2)}) %copy-start) | copy-done | bytes 6077464
  25.3 3.1 %shard_map.59 = (f32[64,2432]{1,0:T(8,128)S(1)}, s16[64,2432]{1,0:T(8,128)(2,1)S(1)}, s16[64,2432]{1,0:T(8,128)(2,1)S(1)}, f32[32,2432]{1,0:T(8,128)S(1)}, f32[32,2432]{1,0:T(8,128)S(1)}) custom-call(s32[2]{0:T(128)S(1)} %pad_add_fusion.refs_0_, bf16[256,1280]{1,0:T(8,128)(2,1)S(1)} %bitcast.13, bf16[2374,1280]{1,0:T(8,128)(2,1)S(1)} %bitcast.7), custom_call_target="tpu_custom_call" | custom-call | flops 1 | bytes 1 | tf_op jit(solution)/shard_map/pallas_call | solution.py:258
  28.4 3.3 %collective-permute-start = (s16[64,2432]{1,0:T(8,128)(2,1)S(1)}, s16[64,2432]{1,0:T(8,128)(2,1)S(1)}, u32[]{:S(2)}, u32[]{:S(2)}) collective-permute-start(s16[64,2432]{1,0:T(8,128)(2,1)S(1)} %get-tuple-element.29), channel_id=1, source_target_pairs={{0,64},{64,128},{128,192},{192,0},{1,65},{65,129},{129,193},{193,1... | collective-permute-start | bytes 933896 | tf_op jit(solution)/shard_map/ppermute | solution.py:228
  31.8 2.2 %collective-permute-start.1 = (s16[64,2432]{1,0:T(8,128)(2,1)S(1)}, s16[64,2432]{1,0:T(8,128)(2,1)S(1)}, u32[]{:S(2)}, u32[]{:S(2)}) collective-permute-start(s16[64,2432]{1,0:T(8,128)(2,1)S(1)} %get-tuple-element.30), channel_id=1, source_target_pairs={{0,192},{64,0},{128,64},{192,128},{1,193},{65,1},{129,65},{193,129... | collective-permute-start | bytes 933896 | tf_op jit(solution)/shard_map/ppermute | solution.py:228
  34.0 3.1 %shard_map.60 = (f32[64,2432]{1,0:T(8,128)S(1)}, s16[64,2432]{1,0:T(8,128)(2,1)S(1)}, s16[64,2432]{1,0:T(8,128)(2,1)S(1)}, f32[32,2432]{1,0:T(8,128)S(1)}, f32[32,2432]{1,0:T(8,128)S(1)}) custom-call(s32[2]{0:T(128)S(1)} %pad_add_fusion.refs_0_, bf16[256,1280]{1,0:T(8,128)(2,1)S(1)} %collective-permute-done.2.refs_1_.act_b_ref, ...), custom_call_target="tpu_custom_call" | custom-call | flops 1 | bytes 1 | tf_op jit(solution)/shard_map/pallas_call | solution.py:258
  38.6 2.8 %collective-permute-start.6 = (s16[64,2432]{1,0:T(8,128)(2,1)S(1)}, s16[64,2432]{1,0:T(8,128)(2,1)S(1)}, u32[]{:S(2)}, u32[]{:S(2)}) collective-permute-start(s16[64,2432]{1,0:T(8,128)(2,1)S(1)} %get-tuple-element.37), channel_id=1, source_target_pairs={{0,192},{64,0},{128,64},{192,128},{1,193},{65,1},{129,65},{193,129... | collective-permute-start | bytes 933896 | tf_op jit(solution)/shard_map/ppermute | solution.py:228
  41.3 5.3 %collective-permute-done.refs_0_.refs_2_ = s16[64,2432]{1,0:T(8,128)(2,1)S(1)} collective-permute-done((s16[64,2432]{1,0:T(8,128)(2,1)S(1)}, s16[64,2432]{1,0:T(8,128)(2,1)S(1)}, u32[]{:S(2)}, u32[]{:S(2)}) %collective-permute-start) | collective-permute-done | bytes 311328 | tf_op jit(solution)/shard_map/ppermute | solution.py:228
  46.7 10.9 %collective-permute-done.1.refs_1_.refs_3_ = s16[64,2432]{1,0:T(8,128)(2,1)S(1)} collective-permute-done((s16[64,2432]{1,0:T(8,128)(2,1)S(1)}, s16[64,2432]{1,0:T(8,128)(2,1)S(1)}, u32[]{:S(2)}, u32[]{:S(2)}) %collective-permute-start.1) | collective-permute-done | bytes 311328 | tf_op jit(solution)/shard_map/ppermute | solution.py:228
  58.0 2.8 %collective-permute-start.4 = (s16[32,2432]{1,0:T(8,128)(2,1)S(1)}, s16[32,2432]{1,0:T(8,128)(2,1)S(1)}, u32[]{:S(2)}, u32[]{:S(2)}) collective-permute-start(s16[32,2432]{1,0:T(8,128)(2,1)S(1)} %get-tuple-element.35), channel_id=1, source_target_pairs={{0,192},{64,0},{128,64},{192,128},{1,193},{65,1},{129,65},{193,129... | collective-permute-start | bytes 466952 | tf_op jit(solution)/shard_map/ppermute | solution.py:228
  62.3 3.8 %collective-permute-done.6.refs_1_.refs_3_ = s16[64,2432]{1,0:T(8,128)(2,1)S(1)} collective-permute-done((s16[64,2432]{1,0:T(8,128)(2,1)S(1)}, s16[64,2432]{1,0:T(8,128)(2,1)S(1)}, u32[]{:S(2)}, u32[]{:S(2)}) %collective-permute-start.6) | collective-permute-done | bytes 311328 | tf_op jit(solution)/shard_map/ppermute | solution.py:228
  66.6 1.9 %collective-permute-start.10 = (s16[32,2432]{1,0:T(8,128)(2,1)S(1)}, s16[32,2432]{1,0:T(8,128)(2,1)S(1)}, u32[]{:S(2)}, u32[]{:S(2)}) collective-permute-start(s16[32,2432]{1,0:T(8,128)(2,1)S(1)} %get-tuple-element.42), channel_id=1, source_target_pairs={{0,192},{64,0},{128,64},{192,128},{1,193},{65,1},{129,65},{193,129... | collective-permute-start | bytes 466952 | tf_op jit(solution)/shard_map/ppermute | solution.py:228
  71.4 5.0 %collective-permute-done.10.refs_5_ = s16[32,2432]{1,0:T(8,128)(2,1)S(1)} collective-permute-done((s16[32,2432]{1,0:T(8,128)(2,1)S(1)}, s16[32,2432]{1,0:T(8,128)(2,1)S(1)}, u32[]{:S(2)}, u32[]{:S(2)}) %collective-permute-start.10) | collective-permute-done | bytes 155680 | tf_op jit(solution)/shard_map/ppermute | solution.py:228
  79.5 6.9 %all-to-all-start.1 = ((f32[64,8,128]{2,1,0:T(8,128)}), f32[64,8,128]{2,1,0:T(8,128)S(1)}, u32[]{:S(2)}, u32[]{:S(2)}) async-start(f32[64,8,128]{2,1,0:T(8,128)} %broadcast_in_dim.8), calls=%async_computation.1 | async-start | bytes 524288 | tf_op jit(solution)/shard_map/all_to_all | solution.py:321
  86.4 2.4 %collective-permute-start.8 = (s16[64,2432]{1,0:T(8,128)(2,1)S(1)}, s16[64,2432]{1,0:T(8,128)(2,1)S(1)}, u32[]{:S(2)}, u32[]{:S(2)}) collective-permute-start(s16[64,2432]{1,0:T(8,128)(2,1)S(1)} %get-tuple-element.40.refs_7_.refs_1_), channel_id=1, source_target_pairs={{0,192},{64,0},{128,64},{192,128},{1,193},{65,1},{129,65},{193,129... | collective-permute-start | bytes 933896 | tf_op jit(solution)/shard_map/ppermute | solution.py:228
  89.4 3.5 %collective-permute-start.12 = (s16[64,2432]{1,0:T(8,128)(2,1)S(1)}, s16[64,2432]{1,0:T(8,128)(2,1)S(1)}, u32[]{:S(2)}, u32[]{:S(2)}) collective-permute-start(s16[64,2432]{1,0:T(8,128)(2,1)S(1)} %get-tuple-element.44.refs_3_.refs_1_), channel_id=1, source_target_pairs={{0,192},{64,0},{128,64},{192,128},{1,193},{65,1},{129,65},{193,129... | collective-permute-start | bytes 933896 | tf_op jit(solution)/shard_map/ppermute | solution.py:228
  93.6 17.0 %shard_map.65.refs_2_.refs_10_ = f32[512,2432]{1,0:T(8,128)S(1)} custom-call(s32[2]{0:T(128)S(1)} %pad_add_fusion.1.refs_0_, s32[64,512]{1,0:T(8,128)S(1)} %reshape.21.refs_1_, f32[64,512]{1,0:T(8,128)S(1)} %reshape.22.refs_2_, s16[64,2432]{1,0:T(8,128)(2,1)S(1)} %get-tuple-element.44.refs_3_.refs_1_), custom_call_target="tpu_custom_call" | custom-call | flops 1 | bytes 1 | tf_op jit(solution)/shard_map/pallas_call | solution.py:258
  110.6 2.3 %copy-done.3 = f32[512,2432]{1,0:T(8,128)} copy-done((f32[512,2432]{1,0:T(8,128)}, f32[512,2432]{1,0:T(8,128)S(1)}, u32[]{:S(2)}) %copy-start.3) | copy-done | bytes 4980760
  112.8 2.4 %copy-done.4 = f32[512,2432]{1,0:T(8,128)S(1)} copy-done((f32[512,2432]{1,0:T(8,128)S(1)}, f32[512,2432]{1,0:T(8,128)}, u32[]{:S(2)}) %copy-start.4) | copy-done | bytes 4980760
  115.4 3.2 %collective-permute-start.18 = (s16[32,2432]{1,0:T(8,128)(2,1)S(1)}, s16[32,2432]{1,0:T(8,128)(2,1)S(1)}, u32[]{:S(2)}, u32[]{:S(2)}) collective-permute-start(s16[32,2432]{1,0:T(8,128)(2,1)S(1)} %get-tuple-element.48), channel_id=1, source_target_pairs={{0,64},{64,128},{128,192},{192,0},{1,65},{65,129},{129,193},{193,1... | collective-permute-start | bytes 466952 | tf_op jit(solution)/shard_map/ppermute | solution.py:228
  119.7 7.3 %collective-permute-start.17 = (f32[8,128]{1,0:T(8,128)S(1)}, f32[8,128]{1,0:T(8,128)S(1)}, u32[]{:S(2)}, u32[]{:S(2)}) collective-permute-start(f32[8,128]{1,0:T(8,128)S(1)} %shard_map.66.refs_4_.refs_6_), channel_id=1, source_target_pairs={{0,128},{64,192},{128,0},{192,64},{1,129},{65,193},{129,1},{193,65... | collective-permute-start | bytes 12296 | tf_op jit(solution)/shard_map/ppermute | solution.py:228
  127.1 2.9 %collective-permute-start.15 = (f32[8,128]{1,0:T(8,128)S(1)}, f32[8,128]{1,0:T(8,128)S(1)}, u32[]{:S(2)}, u32[]{:S(2)}) collective-permute-start(f32[8,128]{1,0:T(8,128)S(1)} %shard_map.66.refs_4_.refs_6_), channel_id=1, source_target_pairs={{0,64},{64,128},{128,192},{192,0},{1,65},{65,129},{129,193},{193,1... | collective-permute-start | bytes 12296 | tf_op jit(solution)/shard_map/ppermute | solution.py:228
  132.8 2.7 %copy-done.2 = bf16[1280,2374]{0,1:T(8,128)(2,1)S(1)} copy-done((bf16[1280,2374]{0,1:T(8,128)(2,1)S(1)}, bf16[1280,2374]{0,1:T(8,128)(2,1)}, u32[]{:S(2)}) %copy-start.2) | copy-done | bytes 6077464
  135.5 2.9 %shard_map.68 = (f32[256,1280]{1,0:T(8,128)S(1)}, bf16[256,2432]{1,0:T(8,128)(2,1)S(1)}) custom-call(s32[2]{0:T(128)S(1)} %pad_add_fusion.refs_0_, s16[64,2432]{1,0:T(8,128)(2,1)S(1)} %get-tuple-element.44.refs_3_.refs_1_, s16[64,2432]{1,0:T(8,128)(2,1)S(1)} %collective-permute-done.11.refs_2_, s16[64,2432]{1,0:T(8,128)(2,1)S(1)} %collective-permute-done.12.refs_3_, ...), custom_call_target="tpu_custom_call" | custom-call | flops 1 | bytes 1 | tf_op jit(solution)/shard_map/pallas_call | solution.py:258
  139.7 2.0 %collective-permute-start.13 = (s16[32,2432]{1,0:T(8,128)(2,1)S(1)}, s16[32,2432]{1,0:T(8,128)(2,1)S(1)}, u32[]{:S(2)}, u32[]{:S(2)}) collective-permute-start(s16[32,2432]{1,0:T(8,128)(2,1)S(1)} %get-tuple-element.46.refs_12_), channel_id=1, source_target_pairs={{0,64},{64,128},{128,192},{192,0},{1,65},{65,129},{129,193},{193,1... | collective-permute-start | bytes 466952 | tf_op jit(solution)/shard_map/ppermute | solution.py:228
  141.7 4.2 %collective-permute-done.14.refs_5_ = s16[32,2432]{1,0:T(8,128)(2,1)S(1)} collective-permute-done((s16[32,2432]{1,0:T(8,128)(2,1)S(1)}, s16[32,2432]{1,0:T(8,128)(2,1)S(1)}, u32[]{:S(2)}, u32[]{:S(2)}) %collective-permute-start.14) | collective-permute-done | bytes 155680 | tf_op jit(solution)/shard_map/ppermute | solution.py:228
  145.9 1.9 %collective-permute-done.13.refs_4_ = s16[32,2432]{1,0:T(8,128)(2,1)S(1)} collective-permute-done((s16[32,2432]{1,0:T(8,128)(2,1)S(1)}, s16[32,2432]{1,0:T(8,128)(2,1)S(1)}, u32[]{:S(2)}, u32[]{:S(2)}) %collective-permute-start.13) | collective-permute-done | bytes 155680 | tf_op jit(solution)/shard_map/ppermute | solution.py:228
  147.8 2.9 %shard_map.69 = (f32[256,1280]{1,0:T(8,128)S(1)}, bf16[256,2432]{1,0:T(8,128)(2,1)S(1)}) custom-call(s32[2]{0:T(128)S(1)} %pad_add_fusion.refs_0_, s16[64,2432]{1,0:T(8,128)(2,1)S(1)} %get-tuple-element.40.refs_7_.refs_1_, s16[64,2432]{1,0:T(8,128)(2,1)S(1)} %collective-permute-done.7.refs_0_.refs_2_, ...), custom_call_target="tpu_custom_call" | custom-call | flops 1 | bytes 1 | tf_op jit(solution)/shard_map/pallas_call | solution.py:258
  152.0 11.7 %all-to-all-start.2 = ((bf16[32,8,1280]{2,1,0:T(8,128)(2,1)}), bf16[32,8,1280]{2,1,0:T(8,128)(2,1)S(1)}, u32[]{:S(2)}, u32[]{:S(2)}) async-start(bf16[32,8,1280]{2,1,0:T(8,128)(2,1)} %bitcast.5), calls=%async_computation.2 | async-start | bytes 1310720 | tf_op jit(solution)/shard_map/all_to_all | solution.py:358
  163.6 8.0 %shard_map.71.refs_1_ = bf16[2374,1280]{1,0:T(8,128)(2,1)} custom-call(bf16[256,1280]{1,0:T(8,128)(2,1)} %bitcast.14, bf16[256,1280]{1,0:T(8,128)(2,1)} %copy-done.9, bf16[256,2432]{1,0:T(8,128)(2,1)} %copy-done.10, bf16[256,2432]{1,0:T(8,128)(2,1)} %copy-done.8), custom_call_target="tpu_custom_call" | custom-call | flops 3111649280 | bytes 6225920 | tf_op jit(solution)/shard_map/pallas_call | solution.py:363
  171.6 4.4 %all-to-all-done.2.refs_0_ = bf16[32,8,1280]{2,1,0:T(8,128)(2,1)S(1)} async-done(((bf16[32,8,1280]{2,1,0:T(8,128)(2,1)}), bf16[32,8,1280]{2,1,0:T(8,128)(2,1)S(1)}, u32[]{:S(2)}, u32[]{:S(2)}) %all-to-all-start.2) | async-done | bytes 655392 | tf_op jit(solution)/shard_map/all_to_all | solution.py:358
  176.0 2.7 %copy-done.6 = bf16[2374,1280]{1,0:T(8,128)(2,1)S(1)} copy-done((bf16[2374,1280]{1,0:T(8,128)(2,1)S(1)}, bf16[2374,1280]{1,0:T(8,128)(2,1)}, u32[]{:S(2)}) %copy-start.6) | copy-done | bytes 6077464
  (67 shorter events, 19.3 us)
Async XLA Ops:
  22.3 6.1 %copy-start.7 = (bf16[32,8,1280]{2,1,0:T(8,128)(2,1)}, bf16[32,8,1280]{2,1,0:T(8,128)(2,1)S(1)}, u32[]{:S(2)}) copy-start(bf16[32,8,1280]{2,1,0:T(8,128)(2,1)S(1)} %all_to_all.15) | copy-start | bytes 1966084
  22.3 11.7 %collective-permute-start.2 = (bf16[256,1280]{1,0:T(8,128)(2,1)S(1)}, bf16[256,1280]{1,0:T(8,128)(2,1)S(1)}, u32[]{:S(2)}, u32[]{:S(2)}) collective-permute-start(bf16[256,1280]{1,0:T(8,128)(2,1)S(1)} %bitcast.12), channel_id=1, source_target_pairs={{0,8},{8,0},{1,9},{9,1},{2,10},{10,2},{3,11},{11,3},{4,12},{12,4},... | collective-permute-start | bytes 1966088 | tf_op jit(solution)/shard_map/ppermute | solution.py:232
  22.4 2.9 %copy-start = (bf16[1280,2374]{0,1:T(8,128)(2,1)S(1)}, bf16[1280,2374]{0,1:T(8,128)(2,1)}, u32[]{:S(2)}) copy-start(bf16[1280,2374]{0,1:T(8,128)(2,1)} %param.5) | copy-start | bytes 18232324
  25.3 8.7 %copy-start.1 = (bf16[1280,2374]{0,1:T(8,128)(2,1)S(1)}, bf16[1280,2374]{0,1:T(8,128)(2,1)}, u32[]{:S(2)}) copy-start(bf16[1280,2374]{0,1:T(8,128)(2,1)} %param.5) | copy-start | bytes 18232324
  28.4 18.2 %collective-permute-start = (s16[64,2432]{1,0:T(8,128)(2,1)S(1)}, s16[64,2432]{1,0:T(8,128)(2,1)S(1)}, u32[]{:S(2)}, u32[]{:S(2)}) collective-permute-start(s16[64,2432]{1,0:T(8,128)(2,1)S(1)} %get-tuple-element.29), channel_id=1, source_target_pairs={{0,64},{64,128},{128,192},{192,0},{1,65},{65,129},{129,193},{193,1... | collective-permute-start | bytes 933896 | tf_op jit(solution)/shard_map/ppermute | solution.py:228
  31.8 25.8 %collective-permute-start.1 = (s16[64,2432]{1,0:T(8,128)(2,1)S(1)}, s16[64,2432]{1,0:T(8,128)(2,1)S(1)}, u32[]{:S(2)}, u32[]{:S(2)}) collective-permute-start(s16[64,2432]{1,0:T(8,128)(2,1)S(1)} %get-tuple-element.30), channel_id=1, source_target_pairs={{0,192},{64,0},{128,64},{192,128},{1,193},{65,1},{129,65},{193,129... | collective-permute-start | bytes 933896 | tf_op jit(solution)/shard_map/ppermute | solution.py:228
  34.0 3.1 %copy-start.9 = (bf16[256,1280]{1,0:T(8,128)(2,1)}, bf16[256,1280]{1,0:T(8,128)(2,1)S(1)}, u32[]{:S(2)}) copy-start(bf16[256,1280]{1,0:T(8,128)(2,1)S(1)} %collective-permute-done.2.refs_1_.act_b_ref) | copy-start | bytes 1966084
  37.1 25.2 %collective-permute-start.5 = (s16[64,2432]{1,0:T(8,128)(2,1)S(1)}, s16[64,2432]{1,0:T(8,128)(2,1)S(1)}, u32[]{:S(2)}, u32[]{:S(2)}) collective-permute-start(s16[64,2432]{1,0:T(8,128)(2,1)S(1)} %get-tuple-element.36), channel_id=1, source_target_pairs={{0,64},{64,128},{128,192},{192,0},{1,65},{65,129},{129,193},{193,1... | collective-permute-start | bytes 933896 | tf_op jit(solution)/shard_map/ppermute | solution.py:228
  38.6 27.6 %collective-permute-start.6 = (s16[64,2432]{1,0:T(8,128)(2,1)S(1)}, s16[64,2432]{1,0:T(8,128)(2,1)S(1)}, u32[]{:S(2)}, u32[]{:S(2)}) collective-permute-start(s16[64,2432]{1,0:T(8,128)(2,1)S(1)} %get-tuple-element.37), channel_id=1, source_target_pairs={{0,192},{64,0},{128,64},{192,128},{1,193},{65,1},{129,65},{193,129... | collective-permute-start | bytes 933896 | tf_op jit(solution)/shard_map/ppermute | solution.py:228
  58.0 12.2 %collective-permute-start.4 = (s16[32,2432]{1,0:T(8,128)(2,1)S(1)}, s16[32,2432]{1,0:T(8,128)(2,1)S(1)}, u32[]{:S(2)}, u32[]{:S(2)}) collective-permute-start(s16[32,2432]{1,0:T(8,128)(2,1)S(1)} %get-tuple-element.35), channel_id=1, source_target_pairs={{0,192},{64,0},{128,64},{192,128},{1,193},{65,1},{129,65},{193,129... | collective-permute-start | bytes 466952 | tf_op jit(solution)/shard_map/ppermute | solution.py:228
  60.8 9.4 %collective-permute-start.3 = (s16[32,2432]{1,0:T(8,128)(2,1)S(1)}, s16[32,2432]{1,0:T(8,128)(2,1)S(1)}, u32[]{:S(2)}, u32[]{:S(2)}) collective-permute-start(s16[32,2432]{1,0:T(8,128)(2,1)S(1)} %get-tuple-element.34.refs_4_), channel_id=1, source_target_pairs={{0,64},{64,128},{128,192},{192,0},{1,65},{65,129},{129,193},{193,1... | collective-permute-start | bytes 466952 | tf_op jit(solution)/shard_map/ppermute | solution.py:228
  66.6 9.7 %collective-permute-start.10 = (s16[32,2432]{1,0:T(8,128)(2,1)S(1)}, s16[32,2432]{1,0:T(8,128)(2,1)S(1)}, u32[]{:S(2)}, u32[]{:S(2)}) collective-permute-start(s16[32,2432]{1,0:T(8,128)(2,1)S(1)} %get-tuple-element.42), channel_id=1, source_target_pairs={{0,192},{64,0},{128,64},{192,128},{1,193},{65,1},{129,65},{193,129... | collective-permute-start | bytes 466952 | tf_op jit(solution)/shard_map/ppermute | solution.py:228
  68.6 9.0 %collective-permute-start.9 = (s16[32,2432]{1,0:T(8,128)(2,1)S(1)}, s16[32,2432]{1,0:T(8,128)(2,1)S(1)}, u32[]{:S(2)}, u32[]{:S(2)}) collective-permute-start(s16[32,2432]{1,0:T(8,128)(2,1)S(1)} %get-tuple-element.39.refs_7_), channel_id=1, source_target_pairs={{0,64},{64,128},{128,192},{192,0},{1,65},{65,129},{129,193},{193,1... | collective-permute-start | bytes 466952 | tf_op jit(solution)/shard_map/ppermute | solution.py:228
  77.6 8.8 %copy-start.11 = (f32[512,64]{0,1:T(8,128)S(1)}, f32[512,64]{0,1:T(8,128)}, u32[]{:S(2)}) copy-start(f32[512,64]{0,1:T(8,128)} %param.7) | copy-start | bytes 393220
  78.7 14.5 %copy-start.12 = (s32[512,64]{0,1:T(8,128)S(1)}, s32[512,64]{0,1:T(8,128)}, u32[]{:S(2)}) copy-start(s32[512,64]{0,1:T(8,128)} %param.6) | copy-start | bytes 393220
  79.5 33.4 %all-to-all-start.1 = ((f32[64,8,128]{2,1,0:T(8,128)}), f32[64,8,128]{2,1,0:T(8,128)S(1)}, u32[]{:S(2)}, u32[]{:S(2)}) async-start(f32[64,8,128]{2,1,0:T(8,128)} %broadcast_in_dim.8), calls=%async_computation.1 | async-start | bytes 524288 | tf_op jit(solution)/shard_map/all_to_all | solution.py:321
  86.4 28.9 %collective-permute-start.8 = (s16[64,2432]{1,0:T(8,128)(2,1)S(1)}, s16[64,2432]{1,0:T(8,128)(2,1)S(1)}, u32[]{:S(2)}, u32[]{:S(2)}) collective-permute-start(s16[64,2432]{1,0:T(8,128)(2,1)S(1)} %get-tuple-element.40.refs_7_.refs_1_), channel_id=1, source_target_pairs={{0,192},{64,0},{128,64},{192,128},{1,193},{65,1},{129,65},{193,129... | collective-permute-start | bytes 933896 | tf_op jit(solution)/shard_map/ppermute | solution.py:228
  88.8 26.5 %collective-permute-start.7 = (s16[64,2432]{1,0:T(8,128)(2,1)S(1)}, s16[64,2432]{1,0:T(8,128)(2,1)S(1)}, u32[]{:S(2)}, u32[]{:S(2)}) collective-permute-start(s16[64,2432]{1,0:T(8,128)(2,1)S(1)} %get-tuple-element.40.refs_7_.refs_1_), channel_id=1, source_target_pairs={{0,64},{64,128},{128,192},{192,0},{1,65},{65,129},{129,193},{193,1... | collective-permute-start | bytes 933896 | tf_op jit(solution)/shard_map/ppermute | solution.py:228
  89.4 25.9 %collective-permute-start.12 = (s16[64,2432]{1,0:T(8,128)(2,1)S(1)}, s16[64,2432]{1,0:T(8,128)(2,1)S(1)}, u32[]{:S(2)}, u32[]{:S(2)}) collective-permute-start(s16[64,2432]{1,0:T(8,128)(2,1)S(1)} %get-tuple-element.44.refs_3_.refs_1_), channel_id=1, source_target_pairs={{0,192},{64,0},{128,64},{192,128},{1,193},{65,1},{129,65},{193,129... | collective-permute-start | bytes 933896 | tf_op jit(solution)/shard_map/ppermute | solution.py:228
  92.9 22.4 %collective-permute-start.11 = (s16[64,2432]{1,0:T(8,128)(2,1)S(1)}, s16[64,2432]{1,0:T(8,128)(2,1)S(1)}, u32[]{:S(2)}, u32[]{:S(2)}) collective-permute-start(s16[64,2432]{1,0:T(8,128)(2,1)S(1)} %get-tuple-element.44.refs_3_.refs_1_), channel_id=1, source_target_pairs={{0,64},{64,128},{128,192},{192,0},{1,65},{65,129},{129,193},{193,1... | collective-permute-start | bytes 933896 | tf_op jit(solution)/shard_map/ppermute | solution.py:228
  115.2 17.5 %copy-start.5 = (f32[512,2432]{1,0:T(8,128)S(1)}, f32[512,2432]{1,0:T(8,128)}, u32[]{:S(2)}) copy-start(f32[512,2432]{1,0:T(8,128)} %copy-done.3) | copy-start | bytes 14942212
  115.4 17.4 %collective-permute-start.18 = (s16[32,2432]{1,0:T(8,128)(2,1)S(1)}, s16[32,2432]{1,0:T(8,128)(2,1)S(1)}, u32[]{:S(2)}, u32[]{:S(2)}) collective-permute-start(s16[32,2432]{1,0:T(8,128)(2,1)S(1)} %get-tuple-element.48), channel_id=1, source_target_pairs={{0,64},{64,128},{128,192},{192,0},{1,65},{65,129},{129,193},{193,1... | collective-permute-start | bytes 466952 | tf_op jit(solution)/shard_map/ppermute | solution.py:228
  118.6 14.2 %collective-permute-start.19 = (s16[32,2432]{1,0:T(8,128)(2,1)S(1)}, s16[32,2432]{1,0:T(8,128)(2,1)S(1)}, u32[]{:S(2)}, u32[]{:S(2)}) collective-permute-start(s16[32,2432]{1,0:T(8,128)(2,1)S(1)} %get-tuple-element.49), channel_id=1, source_target_pairs={{0,192},{64,0},{128,64},{192,128},{1,193},{65,1},{129,65},{193,129... | collective-permute-start | bytes 466952 | tf_op jit(solution)/shard_map/ppermute | solution.py:228
  119.7 10.3 %collective-permute-start.17 = (f32[8,128]{1,0:T(8,128)S(1)}, f32[8,128]{1,0:T(8,128)S(1)}, u32[]{:S(2)}, u32[]{:S(2)}) collective-permute-start(f32[8,128]{1,0:T(8,128)S(1)} %shard_map.66.refs_4_.refs_6_), channel_id=1, source_target_pairs={{0,128},{64,192},{128,0},{192,64},{1,129},{65,193},{129,1},{193,65... | collective-permute-start | bytes 12296 | tf_op jit(solution)/shard_map/ppermute | solution.py:228
  127.1 4.5 %collective-permute-start.16 = (f32[8,128]{1,0:T(8,128)S(1)}, f32[8,128]{1,0:T(8,128)S(1)}, u32[]{:S(2)}, u32[]{:S(2)}) collective-permute-start(f32[8,128]{1,0:T(8,128)S(1)} %shard_map.66.refs_4_.refs_6_), channel_id=1, source_target_pairs={{0,192},{64,0},{128,64},{192,128},{1,193},{65,1},{129,65},{193,129... | collective-permute-start | bytes 12296 | tf_op jit(solution)/shard_map/ppermute | solution.py:228
  127.1 5.7 %collective-permute-start.15 = (f32[8,128]{1,0:T(8,128)S(1)}, f32[8,128]{1,0:T(8,128)S(1)}, u32[]{:S(2)}, u32[]{:S(2)}) collective-permute-start(f32[8,128]{1,0:T(8,128)S(1)} %shard_map.66.refs_4_.refs_6_), channel_id=1, source_target_pairs={{0,64},{64,128},{128,192},{192,0},{1,65},{65,129},{129,193},{193,1... | collective-permute-start | bytes 12296 | tf_op jit(solution)/shard_map/ppermute | solution.py:228
  132.8 2.7 %copy-start.2 = (bf16[1280,2374]{0,1:T(8,128)(2,1)S(1)}, bf16[1280,2374]{0,1:T(8,128)(2,1)}, u32[]{:S(2)}) copy-start(bf16[1280,2374]{0,1:T(8,128)(2,1)} %param.5) | copy-start | bytes 18232324
  138.4 12.3 %copy-start.8 = (bf16[256,2432]{1,0:T(8,128)(2,1)}, bf16[256,2432]{1,0:T(8,128)(2,1)S(1)}, u32[]{:S(2)}) copy-start(bf16[256,2432]{1,0:T(8,128)(2,1)S(1)} %get-tuple-element.50.refs_12_.grad_b_ref) | copy-start | bytes 3735556
  138.4 12.3 %collective-permute-start.20 = (f32[256,1280]{1,0:T(8,128)S(1)}, f32[256,1280]{1,0:T(8,128)S(1)}, u32[]{:S(2)}, u32[]{:S(2)}) collective-permute-start(f32[256,1280]{1,0:T(8,128)S(1)} %get-tuple-element.52), channel_id=1, source_target_pairs={{0,8},{8,0},{1,9},{9,1},{2,10},{10,2},{3,11},{11,3},{4,12},{12,4},... | collective-permute-start | bytes 3932168 | tf_op jit(solution)/shard_map/ppermute | solution.py:232
  138.5 7.4 %collective-permute-start.14 = (s16[32,2432]{1,0:T(8,128)(2,1)S(1)}, s16[32,2432]{1,0:T(8,128)(2,1)S(1)}, u32[]{:S(2)}, u32[]{:S(2)}) collective-permute-start(s16[32,2432]{1,0:T(8,128)(2,1)S(1)} %get-tuple-element.47), channel_id=1, source_target_pairs={{0,192},{64,0},{128,64},{192,128},{1,193},{65,1},{129,65},{193,129... | collective-permute-start | bytes 466952 | tf_op jit(solution)/shard_map/ppermute | solution.py:228
  139.7 8.1 %collective-permute-start.13 = (s16[32,2432]{1,0:T(8,128)(2,1)S(1)}, s16[32,2432]{1,0:T(8,128)(2,1)S(1)}, u32[]{:S(2)}, u32[]{:S(2)}) collective-permute-start(s16[32,2432]{1,0:T(8,128)(2,1)S(1)} %get-tuple-element.46.refs_12_), channel_id=1, source_target_pairs={{0,64},{64,128},{128,192},{192,0},{1,65},{65,129},{129,193},{193,1... | collective-permute-start | bytes 466952 | tf_op jit(solution)/shard_map/ppermute | solution.py:228
  152.0 24.0 %all-to-all-start.2 = ((bf16[32,8,1280]{2,1,0:T(8,128)(2,1)}), bf16[32,8,1280]{2,1,0:T(8,128)(2,1)S(1)}, u32[]{:S(2)}, u32[]{:S(2)}) async-start(bf16[32,8,1280]{2,1,0:T(8,128)(2,1)} %bitcast.5), calls=%async_computation.2 | async-start | bytes 1310720 | tf_op jit(solution)/shard_map/all_to_all | solution.py:358
  (4 other events, 8.7 us)

commit v2 on v1

v2 whole, which is shorter than its diff:
```python
import functools

import jax
import jax.numpy as jnp
from jax import lax
from jax.experimental import pallas as pl
from jax.experimental.pallas import tpu as pltpu
from jax.sharding import Mesh, PartitionSpec as P

LOSS_SCALE = 64.0
CODE_SCALE = 65535.0
CODE_OFFSET = 32768.0
F32 = jnp.float32
BF16 = jnp.bfloat16
I16 = jnp.int16
I32 = jnp.int32
VMEM = pl.BlockSpec(memory_space=pltpu.VMEM)
SMEM = pl.BlockSpec(memory_space=pltpu.SMEM)
ANY = pl.BlockSpec(memory_space=pl.ANY)
PARAMS = pltpu.CompilerParams(vmem_limit_bytes=20 * 1024 * 1024)
CHIP = ("y", "z_lo", "x")
SHARD = ("y", "core", "z_lo", "x")


def lanes_of(shape):
    return lax.broadcasted_iota(I32, shape, 1)


def encode(x, width):
    lane = lanes_of(x.shape)
    inside = lane < width
    high = jnp.max(jnp.where(inside, x, -jnp.inf), axis=1, keepdims=True)
    low = jnp.min(jnp.where(inside, x, jnp.inf), axis=1, keepdims=True)
    size = jnp.maximum(jnp.abs(high), jnp.abs(low))
    step = jnp.maximum(jnp.maximum((high - low) * (1.0 / 65000.0), size * 2.0**-22), 1e-30)
    power = jnp.ceil(jnp.log2(step))
    inverse = jnp.exp2(-power)
    middle = jnp.round((0.5 * high + 0.5 * low) * inverse)
    upper = jnp.floor(middle * (1.0 / 4096.0))
    lower = middle - upper * 4096.0
    code = jnp.clip(jnp.round(x * inverse) - middle, -32767.0, 32767.0)
    code = jnp.where(lane == width, power, code)
    code = jnp.where(lane == width + 1, upper, code)
    code = jnp.where(lane == width + 2, lower, code)
    return code.astype(I32).astype(I16)


def decode(code, width):
    value = code.astype(I32).astype(F32)
    step = jnp.exp2(value[:, width : width + 1])
    middle = value[:, width + 1 : width + 2] * 4096.0 + value[:, width + 2 : width + 3]
    return (value + middle) * step


def first_logits_kernel(
    width, row_ref, act_ref, rest_ref, weight_hbm, own_ref, right_ref, left_ref, merge_right_ref, merge_left_ref,
    weight_ref, acc_ref, sems,
):
    padded = weight_ref.shape[0]
    rest = rest_ref.shape[0]
    copied = width // rest * rest
    copies = []
    for i, start in enumerate(range(0, copied, 512)):
        rows = pl.ds(start, min(512, copied - start))
        copies.append(pltpu.make_async_copy(weight_hbm.at[rows], weight_ref.at[rows], sems.at[i]))
        copies[-1].start()
    weight_ref[copied : copied + rest, :] = rest_ref[...]
    weight_ref[copied + rest : padded, :] = jnp.zeros((padded - copied - rest, weight_ref.shape[1]), BF16)
    logits_kernel(
        width, row_ref, act_ref, weight_ref, own_ref, right_ref, left_ref, merge_right_ref, merge_left_ref, acc_ref, copies
    )


def logits_kernel(
    width, row_ref, act_ref, weight_ref, own_ref, right_ref, left_ref, merge_right_ref, merge_left_ref, acc_ref, copies=()
):
    tokens = act_ref.shape[0]
    quarter, half = tokens // 4, tokens // 8
    padded = acc_ref.shape[1]
    act = act_ref[...]
    for i, start in enumerate(range(0, padded, 512)):
        stop = min(start + 512, padded)
        if copies:
            copies[i].wait()
        acc_ref[:, start:stop] = lax.dot_general(
            act, weight_ref[start:stop, :], (((1,), (1,)), ((), ())), preferred_element_type=F32
        )
    row = row_ref[0]

    def piece(distance, which):
        first = lax.rem(row + distance, 4) * quarter + which * half
        return acc_ref[pl.ds(pl.multiple_of(first, half), half), :]

    own_ref[0:half, :] = piece(0, 0)
    own_ref[half:quarter, :] = piece(0, 1)
    right_ref[0:half, :] = encode(piece(1, 1), width)
    right_ref[half:quarter, :] = encode(piece(2, 0), width)
    left_ref[0:half, :] = encode(piece(3, 0), width)
    left_ref[half:quarter, :] = encode(piece(2, 1), width)
    merge_right_ref[...] = piece(1, 0)
    merge_left_ref[...] = piece(3, 1)


def merge_kernel(width, from_left_ref, from_right_ref, merge_right_ref, merge_left_ref, right_ref, left_ref):
    half = merge_right_ref.shape[0]
    right_ref[...] = encode(merge_right_ref[...] + decode(from_left_ref[half : 2 * half, :], width), width)
    left_ref[...] = encode(merge_left_ref[...] + decode(from_right_ref[half : 2 * half, :], width), width)


def column_to_row(column, offset):
    shape = (column.shape[0], 128)
    here = lax.broadcasted_iota(I32, shape, 0) + offset == lanes_of(shape)
    return jnp.sum(jnp.where(here, column, 0.0), axis=0, keepdims=True)


def row_to_column(row, count, offset):
    shape = (count, 128)
    here = lax.broadcasted_iota(I32, shape, 0) + offset == lanes_of(shape)
    return jnp.sum(jnp.where(here, row, 0.0), axis=1, keepdims=True)


def chunk_of(place_ref, which_chunk):
    core = place_ref[1]
    return core if which_chunk == 0 else 1 - core


def total_kernel(width, which_chunk, place_ref, own_ref, left_one_ref, right_one_ref, left_two_ref, right_two_ref, before_ref, code_ref, stats_ref):
    half, padded = left_two_ref.shape
    offset = chunk_of(place_ref, which_chunk) * (2 * half)
    inside = lanes_of((half, padded)) < width
    peaks, totals = [], []
    for which, one_ref, two_ref in ((0, right_one_ref, left_two_ref), (1, left_one_ref, right_two_ref)):
        rows = slice(which * half, (which + 1) * half)
        logits = own_ref[rows, :] + decode(one_ref[0:half, :], width) + decode(two_ref[...], width)
        logits = jnp.where(inside, logits, -jnp.inf)
        peak = jnp.max(logits, axis=1, keepdims=True)
        weight = jnp.exp(logits - peak)
        code_ref[rows, :] = (jnp.round(weight * CODE_SCALE) - CODE_OFFSET).astype(I32).astype(I16)
        peaks.append(column_to_row(peak, offset + which * half))
        totals.append(column_to_row(jnp.sum(weight, axis=1, keepdims=True), offset + which * half))
    peak, total = peaks[0] + peaks[1], totals[0] + totals[1]
    stats_ref[...] = before_ref[...] + jnp.concatenate([peak, total, jnp.zeros((6, 128), F32)], axis=0)


def teacher_kernel(width, place_ref, ids_ref, values_ref, dense_ref, teacher_ref):
    tokens, entries = ids_ref.shape
    pairs = 8 * entries
    tiles = dense_ref.shape[1] // 128
    values = values_ref[...]
    weight = jnp.exp(values - jnp.max(values, axis=1, keepdims=True))
    teacher_ref[...] = weight / jnp.sum(weight, axis=1, keepdims=True)
    key_row = lax.broadcasted_iota(I32, (tiles * 8, pairs), 0)
    low_row = lax.broadcasted_iota(I32, (128, pairs), 0)
    token = lax.broadcasted_iota(I32, (1, pairs), 1) // entries
    lane = lax.broadcasted_iota(I32, (8, 128), 1)
    contract = (((1,), (1,)), ((), ()))

    def flat(block):
        return jnp.concatenate([block[n : n + 1, :] for n in range(8)], axis=1)

    def group(g, _):
        rows = pl.ds(pl.multiple_of(g * 8, 8), 8)
        ids = flat(ids_ref[rows, :]) - place_ref[0]
        value = flat(teacher_ref[rows, :])
        coarse = value.astype(BF16).astype(F32)
        key = lax.shift_right_arithmetic(ids, 7) * 8 + token
        here = key_row == key
        one_hot = jnp.where(low_row == (ids & 127), 1.0, 0.0).astype(BF16)
        dense = lax.dot_general(
            jnp.where(here, coarse, 0.0).astype(BF16), one_hot, contract, preferred_element_type=F32
        )
        dense += lax.dot_general(
            jnp.where(here, value - coarse, 0.0).astype(BF16), one_hot, contract, preferred_element_type=F32
        )
        for tile in range(tiles):
            block = dense[tile * 8 : tile * 8 + 8, :]
            if tile == tiles - 1:
                block = jnp.where(lane + tile * 128 < width, block, 0.0)
            dense_ref[rows, tile * 128 : tile * 128 + 128] = block
        return 0

    lax.fori_loop(0, tokens // 8, group, 0, unroll=4)


def pair_stats_kernel(mine_ref, other_ref, out_ref):
    peak_a, peak_b = mine_ref[0:1, :], other_ref[0:1, :]
    peak = jnp.maximum(peak_a, peak_b)
    total = jnp.exp(peak_a - peak) * mine_ref[1:2, :] + jnp.exp(peak_b - peak) * other_ref[1:2, :]
    out_ref[...] = jnp.concatenate([peak, total, jnp.zeros((6, 128), F32)], axis=0)


def scale_kernel(stats_ref, own_ref, scale_ref):
    peaks = stats_ref[:, 0, :]
    peak = jnp.max(peaks, axis=0, keepdims=True)
    total = jnp.sum(jnp.exp(peaks - peak) * stats_ref[:, 1, :], axis=0, keepdims=True)
    scale = jnp.exp(own_ref[0:1, :] - peak) / total * (LOSS_SCALE / CODE_SCALE)
    scale_ref[...] = jnp.broadcast_to(scale, scale_ref.shape)


def grad_rows(code, scale_ref, dense_ref, place_ref, which_chunk, distance, which):
    chunk = chunk_of(place_ref, which_chunk)
    owner = lax.rem(place_ref[0] + distance, 4)
    count = code.shape[0]
    quarter = dense_ref.shape[0] // 8
    first = owner * quarter + which * (quarter // 2)
    token = pl.multiple_of((2 * owner + chunk) * quarter + which * (quarter // 2), quarter // 2)
    scale = row_to_column(scale_ref[0:1, :], count, chunk * quarter + which * (quarter // 2))
    student = (code.astype(I32).astype(F32) + CODE_OFFSET) * scale
    grad = student - LOSS_SCALE * dense_ref[pl.ds(token, count), :]
    return grad.astype(BF16), pl.multiple_of(first, quarter // 2)


def hidden_kernel(
    which_chunk, place_ref, own_ref, left_ref, right_ref, left_two_ref, right_two_ref,
    scale_own_ref, scale_left_ref, scale_right_ref, scale_far_ref, dense_ref, weight_ref, hidden_ref, grad_ref,
):
    half = own_ref.shape[0] // 2
    far = slice(which_chunk * half, (which_chunk + 1) * half)
    for distance, which, code_ref, rows, scale_ref in (
        (0, 0, own_ref, slice(None), scale_own_ref),
        (3, 0, left_ref, slice(None), scale_left_ref),
        (1, 0, right_ref, slice(None), scale_right_ref),
        (2, 0, left_two_ref, far, scale_far_ref),
        (2, 1, right_two_ref, far, scale_far_ref),
    ):
        grad, first = grad_rows(code_ref[rows, :], scale_ref, dense_ref, place_ref, which_chunk, distance, which)
        grad_ref[pl.ds(first, grad.shape[0]), :] = grad
    hidden_ref[...] = jnp.dot(grad_ref[...], weight_ref[...], preferred_element_type=F32)


def weight_kernel(act_a_ref, act_b_ref, grad_a_ref, grad_b_ref, out_ref, token_ref):
    contract = (((0,), (0,)), ((), ()))
    total = lax.dot_general(grad_a_ref[...], act_a_ref[...], contract, preferred_element_type=F32)
    total += lax.dot_general(grad_b_ref[...], act_b_ref[...], contract, preferred_element_type=F32)
    out_ref[...] = total.astype(BF16)
    token_ref[...] = jnp.zeros(token_ref.shape, F32)


def pair_kernel(keep_ref, received_ref, sum_ref):
    sum_ref[...] = (keep_ref[...] + received_ref[...]).astype(BF16)


def forward_kernel(a_left_ref, a_right_ref, b_left_ref, b_right_ref, right_ref, left_ref):
    half = right_ref.shape[0] // 2
    right_ref[0:half, :] = a_left_ref[0:half, :]
    right_ref[half : 2 * half, :] = b_left_ref[0:half, :]
    left_ref[0:half, :] = a_right_ref[half : 2 * half, :]
    left_ref[half : 2 * half, :] = b_right_ref[half : 2 * half, :]


def finish_kernel(part_ref, out_ref):
    out_ref[...] = jnp.sum(part_ref[...].astype(F32), axis=0).astype(BF16)


def pin(x, space=pltpu.VMEM):
    return pltpu.with_memory_space_constraint(x, space)


def ring(x, step):
    return lax.ppermute(x, "row", [(i, (i + step) % 4) for i in range(4)])


def swap(x):
    return lax.ppermute(x, "core", [(0, 1), (1, 0)])


def local(activations, out_weight, teacher_ids, teacher_values):
    own_tokens, depth = activations.shape
    width = out_weight.shape[1]
    padded = (width + 127) // 128 * 128
    row, core = lax.axis_index("row"), lax.axis_index("core")
    chips = 32
    tokens = chips * own_tokens
    quarter, half = tokens // 4, tokens // 8
    first_col = lax.axis_index(SHARD) * width
    places = jnp.stack([row, core]).astype(I32)

    mine = lax.all_to_all(jnp.broadcast_to(activations[None], (chips, own_tokens, depth)), CHIP, 0, 0)
    mine = mine.reshape(tokens, depth)
    acts = [mine, swap(mine)]

    def call(kernel, outs, ins, scratch=(), after=()):
        count, ordered = len(ins), len(ins) + len(after)
        outs = tuple(outs)

        def body(*refs):
            kernel(*refs[:count], *refs[ordered : ordered + len(outs)], *refs[ordered + len(outs) + 1 :])
            refs[ordered + len(outs)][...] = jnp.zeros((8, 128), F32)

        specs = [SMEM if x.ndim == 1 else ANY if x.shape == (width, depth) else VMEM for x in ins]
        ins = [x if x.ndim == 1 else pin(x, pltpu.HBM) if x.shape == (width, depth) else pin(x) for x in ins]
        return pl.pallas_call(
            body,
            out_shape=tuple(pltpu.VMEM(dims, dtype) for dims, dtype in outs) + (pltpu.VMEM((8, 128), F32),),
            in_specs=specs + [ANY] * len(after),
            out_specs=(VMEM,) * (len(outs) + 1),
            scratch_shapes=scratch,
            compiler_params=PARAMS,
            cost_estimate=pl.CostEstimate(flops=1, bytes_accessed=1, transcendentals=0),
        )(*ins, *after)

    def both_ways(right, left):
        return ring(right, 1), ring(left, 3)

    part_outs = (
        ((quarter, padded), F32),
        ((quarter, padded), I16),
        ((quarter, padded), I16),
        ((half, padded), F32),
        ((half, padded), F32),
    )
    acc = pltpu.VMEM((tokens, padded), F32)

    def merge(parts, received, after):
        return call(
            functools.partial(merge_kernel, width),
            (((half, padded), I16), ((half, padded), I16)),
            (*received, parts[3], parts[4]),
            after=after,
        )

    def total(chunk, parts, one, two, before, after):
        return call(
            functools.partial(total_kernel, width, chunk),
            (((quarter, padded), I16), ((8, 128), F32)),
            (places, parts[0], *one, *two, before),
            after=after,
        )

    def hidden(chunk, own, received, after):
        return call(
            functools.partial(hidden_kernel, chunk),
            (((tokens, depth), F32), ((tokens, padded), BF16)),
            (places, own, *received, *codes_far, *scales, dense, weight),
            after=after,
        )

    weight = out_weight.T
    copied = width // 16 * 16
    rest = jnp.pad(weight[copied:], ((0, 16 - (width - copied)), (0, 0)))
    *parts_a, weight, done = call(
        functools.partial(first_logits_kernel, width),
        part_outs + (((padded, depth), BF16),),
        (places, mine, rest, weight),
        (acc, pltpu.SemaphoreType.DMA((8,))),
    )
    one_a = both_ways(parts_a[1], parts_a[2])
    *parts_b, done = call(
        functools.partial(logits_kernel, width), part_outs, (places, acts[1], weight), (acc,), (done,)
    )
    one_b = both_ways(parts_b[1], parts_b[2])
    dense, done = call(
        functools.partial(teacher_kernel, width),
        (((2 * tokens, padded), F32),),
        (jnp.stack([first_col, row]).astype(I32), teacher_ids, teacher_values),
        (pltpu.VMEM(teacher_values.shape, F32),),
        (done,),
    )
    *merged_a, done = merge(parts_a, one_a, (done,))
    two_a = both_ways(*merged_a)
    *merged_b, done = merge(parts_b, one_b, (done,))
    two_b = both_ways(*merged_b)
    code_a, stats, done = total(0, parts_a, one_a, two_a, jnp.zeros((8, 128), F32), (done,))
    near_a = both_ways(code_a, code_a)
    code_b, stats, done = total(1, parts_b, one_b, two_b, stats, (done,))
    near_b = both_ways(code_b, code_b)

    paired, done = call(pair_stats_kernel, (((8, 128), F32),), (stats, swap(stats)), after=(done,))
    gathered = lax.all_to_all(jnp.broadcast_to(paired[None], (chips, 8, 128)), CHIP, 0, 0)
    scale, done = call(scale_kernel, (((8, 128), F32),), (gathered, stats), after=(done,))
    scales = (scale, ring(scale, 1), ring(scale, 3), ring(scale, 2))
    *forward, done = call(
        forward_kernel, (((quarter, padded), I16),) * 2, (*near_a, *near_b), after=(done,)
    )
    codes_far = both_ways(*forward)

    hidden_b, grad_b, done = hidden(1, code_b, near_b, (done,))
    received = swap(hidden_b)
    hidden_a, grad_a, done = hidden(0, code_a, near_a, (done,))
    summed, done = call(pair_kernel, (((tokens, depth), BF16),), (hidden_a, received), after=(done,))
    partial = lax.all_to_all(summed.reshape(chips, own_tokens, depth), CHIP, 0, 0)

    tile = 512
    whole = pl.BlockSpec((tokens, depth), lambda i: (0, 0))
    columns = pl.BlockSpec((tokens, tile), lambda i: (0, i))
    grad_weight, done = pl.pallas_call(
        weight_kernel,
        out_shape=(pltpu.HBM((width, depth), BF16), pltpu.VMEM((8, 128), F32)),
        grid=(pl.cdiv(width, tile),),
        in_specs=[whole, whole, columns, columns],
        out_specs=(pl.BlockSpec((tile, depth), lambda i: (i, 0)), pl.BlockSpec((8, 128), lambda i: (0, 0))),
        compiler_params=PARAMS,
        cost_estimate=pl.CostEstimate(flops=4 * tokens * depth * width, bytes_accessed=1, transcendentals=0),
    )(acts[0], acts[1], grad_a, grad_b)

    grad_inputs, _ = call(finish_kernel, (((own_tokens, depth), BF16),), (partial,), after=(done,))
    return (grad_inputs, grad_weight.T)


def solution(mesh):
    fine = Mesh(mesh.devices.reshape(4, 4, 2, 2, 4), ("row", "y", "core", "z_lo", "x"))
    specs = (P(SHARD, "row"), P("row", SHARD))
    return jax.shard_map(local, mesh=fine, in_specs=specs + (P(), P()), out_specs=specs, check_vma=False)
```

time: 180 us -> 160 us (0.89)
  blocking collectives: 20.9 us -> 43.3 us
  starting transfers between devices: 60.6 us -> 42.5 us
  waiting for transfers between devices: 39.5 us -> 23.4 us
  local copies, waits for them, and re-layouts: 15.2 us -> 11.1 us
  Pallas kernels: 42 us -> 38.2 us
    all_to_all x0 -> x1, blocking collectives: none -> 22.4 us  [local(): lax.all_to_all(jnp.broadcast_to(paired[None], (chips, 8, 128)), CHIP, 0, 0)]
    ppermute x19 -> x17, waiting for transfers between devices: 35.1 us -> 17.9 us  [ring(): return lax.ppermute(x, 'row', [(i, (i + step) % 4) for i in range(4)])]
    ppermute x19 -> x17, starting transfers between devices: 42 us -> 34.6 us  [ring(): return lax.ppermute(x, 'row', [(i, (i + step) % 4) for i in range(4)])]
    all_to_all x1 -> x0, starting transfers between devices: 6.86 us -> none  [all_stats(): lax.all_to_all(jnp.broadcast_to(stats[None], (64, 8, 128)), SHARD, 0, 0)]
    unnamed x27 -> x39, local copies, waits for them, and re-layouts: 13.4 us -> 9.58 us
    pallas_call x14 -> x15, Pallas kernels: 42 us -> 38.2 us  [the longest x14 32.4 us: call(): pl.pallas_call(body, out_shape=tuple((pltpu.VMEM(dims, dtype) for dims, d...]
    all_to_all x1, starting transfers between devices: 11.7 us -> 7.94 us  [local(): lax.all_to_all(summed.reshape(chips, own_tokens, depth), CHIP, 0, 0)]
  transfers between devices with their start and end apart: 23 -> 21, of which waited for: 10 -> 8; matrix products, arithmetic and copies ran while one was open for 0% -> 1% of each run, Pallas kernels for 20% -> 21%
where the time goes in v2:
time: 160 us
  blocking collectives  43.3 us (27%)
  starting transfers between devices  42.5 us (27%)
  Pallas kernels  38.2 us (24%)
  waiting for transfers between devices  23.4 us (15%)
  local copies, waits for them, and re-layouts  11.1 us (7%)
    ppermute x17, starting transfers between devices, ring(): return lax.ppermute(x, 'row', [(i, (i + step) % 4) for i in range(4)])  34.6 us
    pallas_call x14, Pallas kernels, call(): pl.pallas_call(body, out_shape=tuple((pltpu.VMEM(dims, dtype) for dims, d...  32.4 us
    all_to_all x1, blocking collectives, local(): lax.all_to_all(jnp.broadcast_to(paired[None], (chips, 8, 128)), CHIP, 0, 0)  22.4 us
    all_to_all x1, blocking collectives, local(): lax.all_to_all(jnp.broadcast_to(activations[None], (chips, own_tokens, de...  20.9 us
    ppermute x17, waiting for transfers between devices, ring(): return lax.ppermute(x, 'row', [(i, (i + step) % 4) for i in range(4)])  17.9 us
    unnamed x39, local copies, waits for them, and re-layouts  9.58 us
    all_to_all x1, starting transfers between devices, local(): lax.all_to_all(summed.reshape(chips, own_tokens, depth), CHIP, 0, 0)  7.94 us
    pallas_call x1, Pallas kernels, local(): pl.pallas_call(weight_kernel, out_shape=(pltpu.HBM((width, depth), BF16),...  5.89 us
  transfers between devices with their start and end apart: 21, of which 8 were waited for; matrix products, arithmetic and copies ran while one was open for 1% of the time, Pallas kernels for 21%

profile of v2, /device:TPU:2, one launch (start us, length us, event | category | flops | bytes accessed | tf_op | source)
XLA Modules:
  0.0 159.7 jit_solution(14635954927417588344)
XLA Ops:
  1.4 20.9 %all_to_all.15 = bf16[32,8,1280]{2,1,0:T(8,128)(2,1)S(1)} all-to-all(bf16[32,8,1280]{2,1,0:T(8,128)(2,1)S(1)} %broadcast_in_dim.6), channel_id=1, replica_groups=mesh['row'=4,'y'=4,'core'=2,'z_lo'=2,'x'=4] {'y','z_lo','x'}, dimensions={0} | all-to-all | bytes 1310720 | tf_op jit(solution)/shard_map/all_to_all | solution.py:278
  23.2 6.0 %shard_map.59 = (f32[64,2432]{1,0:T(8,128)S(1)}, s16[64,2432]{1,0:T(8,128)(2,1)}, s16[64,2432]{1,0:T(8,128)(2,1)}, f32[32,2432]{1,0:T(8,128)S(1)}, f32[32,2432]{...) custom-call(s32[2]{0:T(128)S(1)} %pad_add_fusion.refs_0_, bf16[256,1280]{1,0:T(8,128)(2,1)S(1)} %bitcast.8, ...), custom_call_target="tpu_custom_call" | custom-call | flops 1 | bytes 1 | tf_op jit(solution)/shard_map/pallas_call | solution.py:292
  30.6 3.3 %collective-permute-start = (s16[64,2432]{1,0:T(8,128)(2,1)}, s16[64,2432]{1,0:T(8,128)(2,1)S(1)}, u32[]{:S(2)}, u32[]{:S(2)}) collective-permute-start(s16[64,2432]{1,0:T(8,128)(2,1)} %get-tuple-element.47), channel_id=1, source_target_pairs={{0,64},{64,128},{128,192},{192,0},{1,65},{65,129},{129,193},{193,1... | collective-permute-start | bytes 933896 | tf_op jit(solution)/shard_map/ppermute | solution.py:260
  33.9 2.1 %collective-permute-start.1 = (s16[64,2432]{1,0:T(8,128)(2,1)}, s16[64,2432]{1,0:T(8,128)(2,1)S(1)}, u32[]{:S(2)}, u32[]{:S(2)}) collective-permute-start(s16[64,2432]{1,0:T(8,128)(2,1)} %get-tuple-element.48), channel_id=1, source_target_pairs={{0,192},{64,0},{128,64},{192,128},{1,193},{65,1},{129,65},{193,129... | collective-permute-start | bytes 933896 | tf_op jit(solution)/shard_map/ppermute | solution.py:260
  36.0 3.9 %shard_map.60 = (f32[64,2432]{1,0:T(8,128)S(1)}, s16[64,2432]{1,0:T(8,128)(2,1)}, s16[64,2432]{1,0:T(8,128)(2,1)}, f32[32,2432]{1,0:T(8,128)S(1)}, f32[32,2432]{1,0:T(8,128)S(1)}, /*index=5*/f32[8,128]{1,0:T(8,128)S(1)}) custom-call(s32[2]{0:T(128)S(1)} %pad_add_fusion.refs_0_, bf16[256,1280]{1,0:T(8,128)(2,1)S(1)} %collective-permute-done.2.refs_1_.act_b_ref, ...), custom_call_target="tpu_custom_call" | custom-call | flops 1 | bytes 1 | tf_op jit(solution)/shard_map/pallas_call | solution.py:292
  41.5 1.5 collective-permute-start.5
  43.0 2.7 %collective-permute-start.6 = (s16[64,2432]{1,0:T(8,128)(2,1)}, s16[64,2432]{1,0:T(8,128)(2,1)S(1)}, u32[]{:S(2)}, u32[]{:S(2)}) collective-permute-start(s16[64,2432]{1,0:T(8,128)(2,1)} %get-tuple-element.58), channel_id=1, source_target_pairs={{0,192},{64,0},{128,64},{192,128},{1,193},{65,1},{129,65},{193,129... | collective-permute-start | bytes 933896 | tf_op jit(solution)/shard_map/ppermute | solution.py:260
  46.0 11.6 %shard_map.61 = (f32[512,2432]{1,0:T(8,128)S(1)}, f32[8,128]{1,0:T(8,128)S(1)}) custom-call(s32[2]{0:T(128)S(1)} %pad_add_fusion.1.refs_0_, s32[512,64]{1,0:T(8,128)S(1)} %copy.6.refs_1_, f32[512,64]{1,0:T(8,128)S(1)} %copy.7.refs_2_, f32[8,128]{1,0:T(8,128)S(1)} %get-tuple-element.53.refs_3_), custom_call_target="tpu_custom_call" | custom-call | flops 1 | bytes 1 | tf_op jit(solution)/shard_map/pallas_call | solution.py:292
  60.1 1.5 collective-permute-start.3
  61.6 2.7 %collective-permute-start.4 = (s16[32,2432]{1,0:T(8,128)(2,1)S(1)}, s16[32,2432]{1,0:T(8,128)(2,1)S(1)}, u32[]{:S(2)}, u32[]{:S(2)}) collective-permute-start(s16[32,2432]{1,0:T(8,128)(2,1)S(1)} %get-tuple-element.56), channel_id=1, source_target_pairs={{0,192},{64,0},{128,64},{192,128},{1,193},{65,1},{129,65},{193,129... | collective-permute-start | bytes 466952 | tf_op jit(solution)/shard_map/ppermute | solution.py:260
  64.3 1.2 collective-permute-done.6.refs_1_.refs_3_
  66.0 2.8 %collective-permute-start.9 = (s16[32,2432]{1,0:T(8,128)(2,1)S(1)}, s16[32,2432]{1,0:T(8,128)(2,1)S(1)}, u32[]{:S(2)}, u32[]{:S(2)}) collective-permute-start(s16[32,2432]{1,0:T(8,128)(2,1)S(1)} %get-tuple-element.65), channel_id=1, source_target_pairs={{0,64},{64,128},{128,192},{192,0},{1,65},{65,129},{129,193},{193,1... | collective-permute-start | bytes 466952 | tf_op jit(solution)/shard_map/ppermute | solution.py:260
  68.8 1.6 collective-permute-start.10
  70.4 2.1 %collective-permute-done.3.refs_4_ = s16[32,2432]{1,0:T(8,128)(2,1)S(1)} collective-permute-done((s16[32,2432]{1,0:T(8,128)(2,1)S(1)}, s16[32,2432]{1,0:T(8,128)(2,1)S(1)}, u32[]{:S(2)}, u32[]{:S(2)}) %collective-permute-start.3) | collective-permute-done | bytes 155680 | tf_op jit(solution)/shard_map/ppermute | solution.py:260
  73.6 2.1 %collective-permute-start.8 = (s16[64,2432]{1,0:T(8,128)(2,1)S(1)}, s16[64,2432]{1,0:T(8,128)(2,1)S(1)}, u32[]{:S(2)}, u32[]{:S(2)}) collective-permute-start(s16[64,2432]{1,0:T(8,128)(2,1)S(1)} %get-tuple-element.63.refs_1_), channel_id=1, source_target_pairs={{0,192},{64,0},{128,64},{192,128},{1,193},{65,1},{129,65},{193,129... | collective-permute-start | bytes 933896 | tf_op jit(solution)/shard_map/ppermute | solution.py:260
  75.7 2.0 %collective-permute-start.7 = (s16[64,2432]{1,0:T(8,128)(2,1)S(1)}, s16[64,2432]{1,0:T(8,128)(2,1)S(1)}, u32[]{:S(2)}, u32[]{:S(2)}) collective-permute-start(s16[64,2432]{1,0:T(8,128)(2,1)S(1)} %get-tuple-element.63.refs_1_), channel_id=1, source_target_pairs={{0,64},{64,128},{128,192},{192,0},{1,65},{65,129},{129,193},{193,1... | collective-permute-start | bytes 933896 | tf_op jit(solution)/shard_map/ppermute | solution.py:260
  77.7 1.6 %collective-permute-done.9.refs_4_ = s16[32,2432]{1,0:T(8,128)(2,1)S(1)} collective-permute-done((s16[32,2432]{1,0:T(8,128)(2,1)S(1)}, s16[32,2432]{1,0:T(8,128)(2,1)S(1)}, u32[]{:S(2)}, u32[]{:S(2)}) %collective-permute-start.9) | collective-permute-done | bytes 155680 | tf_op jit(solution)/shard_map/ppermute | solution.py:260
  79.3 3.9 %collective-permute-done.10.refs_5_ = s16[32,2432]{1,0:T(8,128)(2,1)S(1)} collective-permute-done((s16[32,2432]{1,0:T(8,128)(2,1)S(1)}, s16[32,2432]{1,0:T(8,128)(2,1)S(1)}, u32[]{:S(2)}, u32[]{:S(2)}) %collective-permute-start.10) | collective-permute-done | bytes 155680 | tf_op jit(solution)/shard_map/ppermute | solution.py:260
  85.3 2.0 %collective-permute-start.11 = (s16[64,2432]{1,0:T(8,128)(2,1)S(1)}, s16[64,2432]{1,0:T(8,128)(2,1)S(1)}, u32[]{:S(2)}, u32[]{:S(2)}) collective-permute-start(s16[64,2432]{1,0:T(8,128)(2,1)S(1)} %get-tuple-element.69.refs_1_), channel_id=1, source_target_pairs={{0,64},{64,128},{128,192},{192,0},{1,65},{65,129},{129,193},{193,1... | collective-permute-start | bytes 933896 | tf_op jit(solution)/shard_map/ppermute | solution.py:260
  88.5 22.4 %all_to_all.16.refs_0_ = f32[32,8,128]{2,1,0:T(8,128)S(1)} all-to-all(f32[32,8,128]{2,1,0:T(8,128)S(1)} %broadcast_in_dim.8), channel_id=1, replica_groups=mesh['row'=4,'y'=4,'core'=2,'z_lo'=2,'x'=4] {'y','z_lo','x'}, dimensions={0} | all-to-all | bytes 262144 | tf_op jit(solution)/shard_map/all_to_all | solution.py:369
  111.0 1.9 %collective-permute-start.14 = (s16[64,2432]{1,0:T(8,128)(2,1)S(1)}, s16[64,2432]{1,0:T(8,128)(2,1)S(1)}, u32[]{:S(2)}, u32[]{:S(2)}) collective-permute-start(s16[64,2432]{1,0:T(8,128)(2,1)S(1)} %get-tuple-element.75), channel_id=1, source_target_pairs={{0,64},{64,128},{128,192},{192,0},{1,65},{65,129},{129,193},{193,1... | collective-permute-start | bytes 933896 | tf_op jit(solution)/shard_map/ppermute | solution.py:260
  113.0 2.3 %collective-permute-start.15 = (s16[64,2432]{1,0:T(8,128)(2,1)S(1)}, s16[64,2432]{1,0:T(8,128)(2,1)S(1)}, u32[]{:S(2)}, u32[]{:S(2)}) collective-permute-start(s16[64,2432]{1,0:T(8,128)(2,1)S(1)} %get-tuple-element.76), channel_id=1, source_target_pairs={{0,192},{64,0},{128,64},{192,128},{1,193},{65,1},{129,65},{193,129... | collective-permute-start | bytes 933896 | tf_op jit(solution)/shard_map/ppermute | solution.py:260
  115.2 2.3 %collective-permute-start.18 = (f32[8,128]{1,0:T(8,128)S(1)}, f32[8,128]{1,0:T(8,128)S(1)}, u32[]{:S(2)}, u32[]{:S(2)}) collective-permute-start(f32[8,128]{1,0:T(8,128)S(1)} %get-tuple-element.77.refs_6_), channel_id=1, source_target_pairs={{0,128},{64,192},{128,0},{192,64},{1,129},{65,193},{129,1},{193,65... | collective-permute-start | bytes 12296 | tf_op jit(solution)/shard_map/ppermute | solution.py:260
  117.5 1.9 %collective-permute-start.17 = (f32[8,128]{1,0:T(8,128)S(1)}, f32[8,128]{1,0:T(8,128)S(1)}, u32[]{:S(2)}, u32[]{:S(2)}) collective-permute-start(f32[8,128]{1,0:T(8,128)S(1)} %get-tuple-element.77.refs_6_), channel_id=1, source_target_pairs={{0,192},{64,0},{128,64},{192,128},{1,193},{65,1},{129,65},{193,129... | collective-permute-start | bytes 12296 | tf_op jit(solution)/shard_map/ppermute | solution.py:260
  120.4 9.1 %collective-permute-done.18.refs_9_ = f32[8,128]{1,0:T(8,128)S(1)} collective-permute-done((f32[8,128]{1,0:T(8,128)S(1)}, f32[8,128]{1,0:T(8,128)S(1)}, u32[]{:S(2)}, u32[]{:S(2)}) %collective-permute-start.18) | collective-permute-done | bytes 4128 | tf_op jit(solution)/shard_map/ppermute | solution.py:260
  129.6 2.9 %shard_map.69 = (f32[256,1280]{1,0:T(8,128)S(1)}, bf16[256,2432]{1,0:T(8,128)(2,1)S(1)}, f32[8,128]{1,0:T(8,128)S(1)}) custom-call(s32[2]{0:T(128)S(1)} %pad_add_fusion.refs_0_, s16[64,2432]{1,0:T(8,128)(2,1)S(1)} %get-tuple-element.69.refs_1_, s16[64,2432]{1,0:T(8,128)(2,1)S(1)} %collective-permute-done.11.refs_2_, ...), custom_call_target="tpu_custom_call" | custom-call | flops 1 | bytes 1 | tf_op jit(solution)/shard_map/pallas_call | solution.py:292
  133.6 2.9 %shard_map.70 = (f32[256,1280]{1,0:T(8,128)S(1)}, bf16[256,2432]{1,0:T(8,128)(2,1)S(1)}, f32[8,128]{1,0:T(8,128)S(1)}) custom-call(s32[2]{0:T(128)S(1)} %pad_add_fusion.refs_0_, s16[64,2432]{1,0:T(8,128)(2,1)S(1)} %get-tuple-element.63.refs_1_, s16[64,2432]{1,0:T(8,128)(2,1)S(1)} %collective-permute-done.7.refs_0_.refs_2_, ...), custom_call_target="tpu_custom_call" | custom-call | flops 1 | bytes 1 | tf_op jit(solution)/shard_map/pallas_call | solution.py:292
  137.8 7.9 %all-to-all-start.2 = ((bf16[32,8,1280]{2,1,0:T(8,128)(2,1)}), bf16[32,8,1280]{2,1,0:T(8,128)(2,1)S(1)}, u32[]{:S(2)}, u32[]{:S(2)}) async-start(bf16[32,8,1280]{2,1,0:T(8,128)(2,1)} %bitcast.5), calls=%async_computation.2 | async-start | bytes 1310720 | tf_op jit(solution)/shard_map/all_to_all | solution.py:381
  145.7 1.3 copy-done.13
  147.0 1.3 copy-done.15
  148.3 5.9 %shard_map.72 = (bf16[2374,1280]{1,0:T(8,128)(2,1)}, f32[8,128]{1,0:T(8,128)S(1)}) custom-call(bf16[256,1280]{1,0:T(8,128)(2,1)S(1)} %bitcast.9, bf16[256,1280]{1,0:T(8,128)(2,1)S(1)} %collective-permute-done.2.refs_1_.act_b_ref, bf16[256,2432]{1,0:T(8,128)(2,1)S(1)} %copy-done.15, bf16[256,2432]{1,0:T(8,128)(2,1)S(1)} %copy-done.13), custom_call_target="tpu_custom_call" | custom-call | flops 3111649280 | bytes 1 | tf_op jit(solution)/shard_map/pallas_call | solution.py:386
  154.2 4.3 %all-to-all-done.2.refs_0_ = bf16[32,8,1280]{2,1,0:T(8,128)(2,1)S(1)} async-done(((bf16[32,8,1280]{2,1,0:T(8,128)(2,1)}), bf16[32,8,1280]{2,1,0:T(8,128)(2,1)S(1)}, u32[]{:S(2)}, u32[]{:S(2)}) %all-to-all-start.2) | async-done | bytes 655392 | tf_op jit(solution)/shard_map/all_to_all | solution.py:381
  (73 shorter events, 17.0 us)
Async XLA Ops:
  22.3 13.7 %collective-permute-start.2 = (bf16[256,1280]{1,0:T(8,128)(2,1)S(1)}, bf16[256,1280]{1,0:T(8,128)(2,1)S(1)}, u32[]{:S(2)}, u32[]{:S(2)}) collective-permute-start(bf16[256,1280]{1,0:T(8,128)(2,1)S(1)} %bitcast.7), channel_id=1, source_target_pairs={{0,8},{8,0},{1,9},{9,1},{2,10},{10,2},{3,11},{11,3},{4,12},{12,4},... | collective-permute-start | bytes 1966088 | tf_op jit(solution)/shard_map/ppermute | solution.py:264
  30.6 9.3 %copy-start = (bf16[2432,1280]{1,0:T(8,128)(2,1)}, bf16[2432,1280]{1,0:T(8,128)(2,1)S(1)}, u32[]{:S(2)}) copy-start(bf16[2432,1280]{1,0:T(8,128)(2,1)S(1)} %get-tuple-element.51.refs_2_.refs_11_) | copy-start | bytes 18677764
  30.6 9.3 %copy-start.4 = (f32[64,2432]{1,0:T(8,128)}, f32[64,2432]{1,0:T(8,128)S(1)}, u32[]{:S(2)}) copy-start(f32[64,2432]{1,0:T(8,128)S(1)} %get-tuple-element.46.refs_1_) | copy-start | bytes 1867780
  30.6 27.0 %collective-permute-start = (s16[64,2432]{1,0:T(8,128)(2,1)}, s16[64,2432]{1,0:T(8,128)(2,1)S(1)}, u32[]{:S(2)}, u32[]{:S(2)}) collective-permute-start(s16[64,2432]{1,0:T(8,128)(2,1)} %get-tuple-element.47), channel_id=1, source_target_pairs={{0,64},{64,128},{128,192},{192,0},{1,65},{65,129},{129,193},{193,1... | collective-permute-start | bytes 933896 | tf_op jit(solution)/shard_map/ppermute | solution.py:260
  33.9 23.7 %collective-permute-start.1 = (s16[64,2432]{1,0:T(8,128)(2,1)}, s16[64,2432]{1,0:T(8,128)(2,1)S(1)}, u32[]{:S(2)}, u32[]{:S(2)}) collective-permute-start(s16[64,2432]{1,0:T(8,128)(2,1)} %get-tuple-element.48), channel_id=1, source_target_pairs={{0,192},{64,0},{128,64},{192,128},{1,193},{65,1},{129,65},{193,129... | collective-permute-start | bytes 933896 | tf_op jit(solution)/shard_map/ppermute | solution.py:260
  36.0 9.6 %copy-start.16 = (s32[512,64]{0,1:T(8,128)S(1)}, s32[512,64]{0,1:T(8,128)}, u32[]{:S(2)}) copy-start(s32[512,64]{0,1:T(8,128)} %param.6) | copy-start | bytes 393220
  36.0 9.7 %copy-start.17 = (f32[512,64]{0,1:T(8,128)S(1)}, f32[512,64]{0,1:T(8,128)}, u32[]{:S(2)}) copy-start(f32[512,64]{0,1:T(8,128)} %param.7) | copy-start | bytes 393220
  41.5 22.8 %collective-permute-start.5 = (s16[64,2432]{1,0:T(8,128)(2,1)}, s16[64,2432]{1,0:T(8,128)(2,1)S(1)}, u32[]{:S(2)}, u32[]{:S(2)}) collective-permute-start(s16[64,2432]{1,0:T(8,128)(2,1)} %get-tuple-element.57), channel_id=1, source_target_pairs={{0,64},{64,128},{128,192},{192,0},{1,65},{65,129},{129,193},{193,1... | collective-permute-start | bytes 933896 | tf_op jit(solution)/shard_map/ppermute | solution.py:260
  43.0 22.6 %collective-permute-start.6 = (s16[64,2432]{1,0:T(8,128)(2,1)}, s16[64,2432]{1,0:T(8,128)(2,1)S(1)}, u32[]{:S(2)}, u32[]{:S(2)}) collective-permute-start(s16[64,2432]{1,0:T(8,128)(2,1)} %get-tuple-element.58), channel_id=1, source_target_pairs={{0,192},{64,0},{128,64},{192,128},{1,193},{65,1},{129,65},{193,129... | collective-permute-start | bytes 933896 | tf_op jit(solution)/shard_map/ppermute | solution.py:260
  45.9 19.6 %copy-start.7 = (f32[32,2432]{1,0:T(8,128)S(1)}, f32[32,2432]{1,0:T(8,128)}, u32[]{:S(2)}) copy-start(f32[32,2432]{1,0:T(8,128)} %copy-done.6) | copy-start | bytes 933892
  57.6 14.9 %copy-start.5 = (f32[64,2432]{1,0:T(8,128)S(1)}, f32[64,2432]{1,0:T(8,128)}, u32[]{:S(2)}) copy-start(f32[64,2432]{1,0:T(8,128)} %copy-done.4) | copy-start | bytes 1867780
  59.6 23.5 %copy-start.3 = (f32[64,2432]{1,0:T(8,128)S(1)}, f32[64,2432]{1,0:T(8,128)}, u32[]{:S(2)}) copy-start(f32[64,2432]{1,0:T(8,128)} %copy-done.2) | copy-start | bytes 1867780
  60.1 12.4 %collective-permute-start.3 = (s16[32,2432]{1,0:T(8,128)(2,1)S(1)}, s16[32,2432]{1,0:T(8,128)(2,1)S(1)}, u32[]{:S(2)}, u32[]{:S(2)}) collective-permute-start(s16[32,2432]{1,0:T(8,128)(2,1)S(1)} %get-tuple-element.55), channel_id=1, source_target_pairs={{0,64},{64,128},{128,192},{192,0},{1,65},{65,129},{129,193},{193,1... | collective-permute-start | bytes 466952 | tf_op jit(solution)/shard_map/ppermute | solution.py:260
  61.6 67.9 %copy-start.1 = (bf16[2432,1280]{1,0:T(8,128)(2,1)S(1)}, bf16[2432,1280]{1,0:T(8,128)(2,1)}, u32[]{:S(2)}) copy-start(bf16[2432,1280]{1,0:T(8,128)(2,1)} %copy-done) | copy-start | bytes 18677764
  61.6 10.8 %collective-permute-start.4 = (s16[32,2432]{1,0:T(8,128)(2,1)S(1)}, s16[32,2432]{1,0:T(8,128)(2,1)S(1)}, u32[]{:S(2)}, u32[]{:S(2)}) collective-permute-start(s16[32,2432]{1,0:T(8,128)(2,1)S(1)} %get-tuple-element.56), channel_id=1, source_target_pairs={{0,192},{64,0},{128,64},{192,128},{1,193},{65,1},{129,65},{193,129... | collective-permute-start | bytes 466952 | tf_op jit(solution)/shard_map/ppermute | solution.py:260
  66.0 13.3 %collective-permute-start.9 = (s16[32,2432]{1,0:T(8,128)(2,1)S(1)}, s16[32,2432]{1,0:T(8,128)(2,1)S(1)}, u32[]{:S(2)}, u32[]{:S(2)}) collective-permute-start(s16[32,2432]{1,0:T(8,128)(2,1)S(1)} %get-tuple-element.65), channel_id=1, source_target_pairs={{0,64},{64,128},{128,192},{192,0},{1,65},{65,129},{129,193},{193,1... | collective-permute-start | bytes 466952 | tf_op jit(solution)/shard_map/ppermute | solution.py:260
  68.8 14.4 %collective-permute-start.10 = (s16[32,2432]{1,0:T(8,128)(2,1)S(1)}, s16[32,2432]{1,0:T(8,128)(2,1)S(1)}, u32[]{:S(2)}, u32[]{:S(2)}) collective-permute-start(s16[32,2432]{1,0:T(8,128)(2,1)S(1)} %get-tuple-element.66), channel_id=1, source_target_pairs={{0,192},{64,0},{128,64},{192,128},{1,193},{65,1},{129,65},{193,129... | collective-permute-start | bytes 466952 | tf_op jit(solution)/shard_map/ppermute | solution.py:260
  73.6 37.3 %collective-permute-start.8 = (s16[64,2432]{1,0:T(8,128)(2,1)S(1)}, s16[64,2432]{1,0:T(8,128)(2,1)S(1)}, u32[]{:S(2)}, u32[]{:S(2)}) collective-permute-start(s16[64,2432]{1,0:T(8,128)(2,1)S(1)} %get-tuple-element.63.refs_1_), channel_id=1, source_target_pairs={{0,192},{64,0},{128,64},{192,128},{1,193},{65,1},{129,65},{193,129... | collective-permute-start | bytes 933896 | tf_op jit(solution)/shard_map/ppermute | solution.py:260
  75.7 35.2 %collective-permute-start.7 = (s16[64,2432]{1,0:T(8,128)(2,1)S(1)}, s16[64,2432]{1,0:T(8,128)(2,1)S(1)}, u32[]{:S(2)}, u32[]{:S(2)}) collective-permute-start(s16[64,2432]{1,0:T(8,128)(2,1)S(1)} %get-tuple-element.63.refs_1_), channel_id=1, source_target_pairs={{0,64},{64,128},{128,192},{192,0},{1,65},{65,129},{129,193},{193,1... | collective-permute-start | bytes 933896 | tf_op jit(solution)/shard_map/ppermute | solution.py:260
  84.3 26.6 %collective-permute-start.12 = (s16[64,2432]{1,0:T(8,128)(2,1)S(1)}, s16[64,2432]{1,0:T(8,128)(2,1)S(1)}, u32[]{:S(2)}, u32[]{:S(2)}) collective-permute-start(s16[64,2432]{1,0:T(8,128)(2,1)S(1)} %get-tuple-element.69.refs_1_), channel_id=1, source_target_pairs={{0,192},{64,0},{128,64},{192,128},{1,193},{65,1},{129,65},{193,129... | collective-permute-start | bytes 933896 | tf_op jit(solution)/shard_map/ppermute | solution.py:260
  85.3 25.6 %collective-permute-start.11 = (s16[64,2432]{1,0:T(8,128)(2,1)S(1)}, s16[64,2432]{1,0:T(8,128)(2,1)S(1)}, u32[]{:S(2)}, u32[]{:S(2)}) collective-permute-start(s16[64,2432]{1,0:T(8,128)(2,1)S(1)} %get-tuple-element.69.refs_1_), channel_id=1, source_target_pairs={{0,64},{64,128},{128,192},{192,0},{1,65},{65,129},{129,193},{193,1... | collective-permute-start | bytes 933896 | tf_op jit(solution)/shard_map/ppermute | solution.py:260
  87.3 1.2 collective-permute-start.13
  111.0 18.5 %collective-permute-start.14 = (s16[64,2432]{1,0:T(8,128)(2,1)S(1)}, s16[64,2432]{1,0:T(8,128)(2,1)S(1)}, u32[]{:S(2)}, u32[]{:S(2)}) collective-permute-start(s16[64,2432]{1,0:T(8,128)(2,1)S(1)} %get-tuple-element.75), channel_id=1, source_target_pairs={{0,64},{64,128},{128,192},{192,0},{1,65},{65,129},{129,193},{193,1... | collective-permute-start | bytes 933896 | tf_op jit(solution)/shard_map/ppermute | solution.py:260
  113.0 16.6 %collective-permute-start.15 = (s16[64,2432]{1,0:T(8,128)(2,1)S(1)}, s16[64,2432]{1,0:T(8,128)(2,1)S(1)}, u32[]{:S(2)}, u32[]{:S(2)}) collective-permute-start(s16[64,2432]{1,0:T(8,128)(2,1)S(1)} %get-tuple-element.76), channel_id=1, source_target_pairs={{0,192},{64,0},{128,64},{192,128},{1,193},{65,1},{129,65},{193,129... | collective-permute-start | bytes 933896 | tf_op jit(solution)/shard_map/ppermute | solution.py:260
  115.2 14.3 %collective-permute-start.18 = (f32[8,128]{1,0:T(8,128)S(1)}, f32[8,128]{1,0:T(8,128)S(1)}, u32[]{:S(2)}, u32[]{:S(2)}) collective-permute-start(f32[8,128]{1,0:T(8,128)S(1)} %get-tuple-element.77.refs_6_), channel_id=1, source_target_pairs={{0,128},{64,192},{128,0},{192,64},{1,129},{65,193},{129,1},{193,65... | collective-permute-start | bytes 12296 | tf_op jit(solution)/shard_map/ppermute | solution.py:260
  117.5 12.0 %collective-permute-start.17 = (f32[8,128]{1,0:T(8,128)S(1)}, f32[8,128]{1,0:T(8,128)S(1)}, u32[]{:S(2)}, u32[]{:S(2)}) collective-permute-start(f32[8,128]{1,0:T(8,128)S(1)} %get-tuple-element.77.refs_6_), channel_id=1, source_target_pairs={{0,192},{64,0},{128,64},{192,128},{1,193},{65,1},{129,65},{193,129... | collective-permute-start | bytes 12296 | tf_op jit(solution)/shard_map/ppermute | solution.py:260
  119.5 10.1 %collective-permute-start.16 = (f32[8,128]{1,0:T(8,128)S(1)}, f32[8,128]{1,0:T(8,128)S(1)}, u32[]{:S(2)}, u32[]{:S(2)}) collective-permute-start(f32[8,128]{1,0:T(8,128)S(1)} %get-tuple-element.77.refs_6_), channel_id=1, source_target_pairs={{0,64},{64,128},{128,192},{192,0},{1,65},{65,129},{129,193},{193,1... | collective-permute-start | bytes 12296 | tf_op jit(solution)/shard_map/ppermute | solution.py:260
  133.6 3.0 %collective-permute-start.19 = (f32[256,1280]{1,0:T(8,128)S(1)}, f32[256,1280]{1,0:T(8,128)S(1)}, u32[]{:S(2)}, u32[]{:S(2)}) collective-permute-start(f32[256,1280]{1,0:T(8,128)S(1)} %get-tuple-element.82), channel_id=1, source_target_pairs={{0,8},{8,0},{1,9},{9,1},{2,10},{10,2},{3,11},{11,3},{4,12},{12,4},... | collective-permute-start | bytes 3932168 | tf_op jit(solution)/shard_map/ppermute | solution.py:264
  136.5 1.3 copy-start.14
  137.8 20.7 %all-to-all-start.2 = ((bf16[32,8,1280]{2,1,0:T(8,128)(2,1)}), bf16[32,8,1280]{2,1,0:T(8,128)(2,1)S(1)}, u32[]{:S(2)}, u32[]{:S(2)}) async-start(bf16[32,8,1280]{2,1,0:T(8,128)(2,1)} %bitcast.5), calls=%async_computation.2 | async-start | bytes 1310720 | tf_op jit(solution)/shard_map/all_to_all | solution.py:381
  145.7 1.3 copy-start.13
  147.0 1.3 copy-start.15
  (7 other events, 6.1 us)

commit v3 on v2

--- a/solution.py
+++ b/solution.py
@@ -179,7 +179,7 @@
             dense_ref[rows, tile * 128 : tile * 128 + 128] = block
         return 0
 
-    lax.fori_loop(0, tokens // 8, group, 0, unroll=4)
+    lax.fori_loop(0, tokens // 8, group, 0, unroll=8)
 
 
 def pair_stats_kernel(mine_ref, other_ref, out_ref):
@@ -279,7 +279,7 @@
     mine = mine.reshape(tokens, depth)
     acts = [mine, swap(mine)]
 
-    def call(kernel, outs, ins, scratch=(), after=()):
+    def call(kernel, outs, ins, scratch=(), after=(), micros=0):
         count, ordered = len(ins), len(ins) + len(after)
         outs = tuple(outs)
 
@@ -291,12 +291,12 @@
         ins = [x if x.ndim == 1 else pin(x, pltpu.HBM) if x.shape == (width, depth) else pin(x) for x in ins]
         return pl.pallas_call(
             body,
-            out_shape=tuple(pltpu.VMEM(dims, dtype) for dims, dtype in outs) + (pltpu.VMEM((8, 128), F32),),
+            out_shape=tuple((pltpu.HBM if space else pltpu.VMEM)(dims, dtype) for dims, dtype, *space in outs) + (pltpu.VMEM((8, 128), F32),),
             in_specs=specs + [ANY] * len(after),
             out_specs=(VMEM,) * (len(outs) + 1),
             scratch_shapes=scratch,
             compiler_params=PARAMS,
-            cost_estimate=pl.CostEstimate(flops=1, bytes_accessed=1, transcendentals=0),
+            cost_estimate=pl.CostEstimate(flops=1 + micros * 1_150_000_000, bytes_accessed=1, transcendentals=0),
         )(*ins, *after)
 
     def both_ways(right, left):
@@ -330,7 +330,7 @@
     def hidden(chunk, own, received, after):
         return call(
             functools.partial(hidden_kernel, chunk),
-            (((tokens, depth), F32), ((tokens, padded), BF16)),
+            (((tokens, depth), F32), ((tokens, padded), BF16, pltpu.HBM)),
             (places, own, *received, *codes_far, *scales, dense, weight),
             after=after,
         )

time: 160 us -> 158 us (0.988)
  starting transfers between devices: 42.5 us -> 39 us
  waiting for transfers between devices: 23.4 us -> 26.8 us
  Pallas kernels: 38.2 us -> 36 us
    ppermute x17, waiting for transfers between devices: 17.9 us -> 21.1 us  [ring(): return lax.ppermute(x, 'row', [(i, (i + step) % 4) for i in range(4)])]
    all_to_all x1, starting transfers between devices: 7.94 us -> 4.94 us  [local(): lax.all_to_all(summed.reshape(chips, own_tokens, depth), CHIP, 0, 0)]
    pallas_call x14, Pallas kernels: 32.4 us -> 30.2 us  [call(): pl.pallas_call(body, out_shape=tuple(((pltpu.HBM if space else pltpu.VMEM...]
    unnamed x39 -> x35, local copies, waits for them, and re-layouts: 9.58 us -> 8.39 us
  transfers between devices with their start and end apart: 21 -> 21, of which waited for: 8 -> 8; matrix products, arithmetic and copies ran while one was open for 1% -> 1% of each run, Pallas kernels for 21% -> 20%
where the time goes in v3:
time: 158 us; the launch traced here: 157 us
  blocking collectives  44.2 us (28%)
  starting transfers between devices  39 us (25%)
  Pallas kernels  36 us (23%)
  waiting for transfers between devices  26.8 us (17%)
  local copies, waits for them, and re-layouts  9.91 us (6%)
    ppermute x17, starting transfers between devices, ring(): return lax.ppermute(x, 'row', [(i, (i + step) % 4) for i in range(4)])  33.7 us
    pallas_call x14, Pallas kernels, call(): pl.pallas_call(body, out_shape=tuple(((pltpu.HBM if space else pltpu.VMEM...  30.2 us
    all_to_all x1, blocking collectives, local(): lax.all_to_all(jnp.broadcast_to(paired[None], (chips, 8, 128)), CHIP, 0, 0)  23.3 us
    ppermute x17, waiting for transfers between devices, ring(): return lax.ppermute(x, 'row', [(i, (i + step) % 4) for i in range(4)])  21.1 us
    all_to_all x1, blocking collectives, local(): lax.all_to_all(jnp.broadcast_to(activations[None], (chips, own_tokens, de...  20.9 us
    unnamed x35, local copies, waits for them, and re-layouts  8.39 us
    pallas_call x1, Pallas kernels, local(): pl.pallas_call(weight_kernel, out_shape=(pltpu.HBM((width, depth), BF16),...  5.89 us
    all_to_all x1, starting transfers between devices, local(): lax.all_to_all(summed.reshape(chips, own_tokens, depth), CHIP, 0, 0)  4.94 us
  transfers between devices with their start and end apart: 21, of which 8 were waited for; matrix products, arithmetic and copies ran while one was open for 1% of the time, Pallas kernels for 20%

profile of v3, /device:TPU:2, one launch (start us, length us, event | category | flops | bytes accessed | tf_op | source)
XLA Modules:
  0.0 157.0 jit_solution(7971318472961249931)
XLA Ops:
  1.4 20.9 %all_to_all.15 = bf16[32,8,1280]{2,1,0:T(8,128)(2,1)S(1)} all-to-all(bf16[32,8,1280]{2,1,0:T(8,128)(2,1)S(1)} %broadcast_in_dim.6), channel_id=1, replica_groups=mesh['row'=4,'y'=4,'core'=2,'z_lo'=2,'x'=4] {'y','z_lo','x'}, dimensions={0} | all-to-all | bytes 1310720 | tf_op jit(solution)/shard_map/all_to_all | solution.py:278
  23.2 6.0 %shard_map.59 = (f32[64,2432]{1,0:T(8,128)S(1)}, s16[64,2432]{1,0:T(8,128)(2,1)}, s16[64,2432]{1,0:T(8,128)(2,1)}, f32[32,2432]{1,0:T(8,128)S(1)}, f32[32,2432]{...) custom-call(s32[2]{0:T(128)S(1)} %pad_add_fusion.refs_0_, bf16[256,1280]{1,0:T(8,128)(2,1)S(1)} %bitcast.8, ...), custom_call_target="tpu_custom_call" | custom-call | flops 1 | bytes 1 | tf_op jit(solution)/shard_map/pallas_call | solution.py:292
  30.6 3.3 %collective-permute-start = (s16[64,2432]{1,0:T(8,128)(2,1)}, s16[64,2432]{1,0:T(8,128)(2,1)S(1)}, u32[]{:S(2)}, u32[]{:S(2)}) collective-permute-start(s16[64,2432]{1,0:T(8,128)(2,1)} %get-tuple-element.47), channel_id=1, source_target_pairs={{0,64},{64,128},{128,192},{192,0},{1,65},{65,129},{129,193},{193,1... | collective-permute-start | bytes 933896 | tf_op jit(solution)/shard_map/ppermute | solution.py:260
  33.9 2.1 %collective-permute-start.1 = (s16[64,2432]{1,0:T(8,128)(2,1)}, s16[64,2432]{1,0:T(8,128)(2,1)S(1)}, u32[]{:S(2)}, u32[]{:S(2)}) collective-permute-start(s16[64,2432]{1,0:T(8,128)(2,1)} %get-tuple-element.48), channel_id=1, source_target_pairs={{0,192},{64,0},{128,64},{192,128},{1,193},{65,1},{129,65},{193,129... | collective-permute-start | bytes 933896 | tf_op jit(solution)/shard_map/ppermute | solution.py:260
  36.0 3.9 %shard_map.60 = (f32[64,2432]{1,0:T(8,128)S(1)}, s16[64,2432]{1,0:T(8,128)(2,1)}, s16[64,2432]{1,0:T(8,128)(2,1)}, f32[32,2432]{1,0:T(8,128)S(1)}, f32[32,2432]{1,0:T(8,128)S(1)}, /*index=5*/f32[8,128]{1,0:T(8,128)S(1)}) custom-call(s32[2]{0:T(128)S(1)} %pad_add_fusion.refs_0_, bf16[256,1280]{1,0:T(8,128)(2,1)S(1)} %collective-permute-done.2.refs_1_.act_b_ref, ...), custom_call_target="tpu_custom_call" | custom-call | flops 1 | bytes 1 | tf_op jit(solution)/shard_map/pallas_call | solution.py:292
  41.4 1.5 collective-permute-start.5
  42.9 2.7 %collective-permute-start.6 = (s16[64,2432]{1,0:T(8,128)(2,1)}, s16[64,2432]{1,0:T(8,128)(2,1)S(1)}, u32[]{:S(2)}, u32[]{:S(2)}) collective-permute-start(s16[64,2432]{1,0:T(8,128)(2,1)} %get-tuple-element.58), channel_id=1, source_target_pairs={{0,192},{64,0},{128,64},{192,128},{1,193},{65,1},{129,65},{193,129... | collective-permute-start | bytes 933896 | tf_op jit(solution)/shard_map/ppermute | solution.py:260
  46.0 9.6 %shard_map.61 = (f32[512,2432]{1,0:T(8,128)S(1)}, f32[8,128]{1,0:T(8,128)S(1)}) custom-call(s32[2]{0:T(128)S(1)} %pad_add_fusion.1.refs_0_, s32[512,64]{1,0:T(8,128)S(1)} %copy.6.refs_1_, f32[512,64]{1,0:T(8,128)S(1)} %copy.7.refs_2_, f32[8,128]{1,0:T(8,128)S(1)} %get-tuple-element.53.refs_3_), custom_call_target="tpu_custom_call" | custom-call | flops 1 | bytes 1 | tf_op jit(solution)/shard_map/pallas_call | solution.py:292
  58.4 2.2 %collective-permute-start.3 = (s16[32,2432]{1,0:T(8,128)(2,1)S(1)}, s16[32,2432]{1,0:T(8,128)(2,1)S(1)}, u32[]{:S(2)}, u32[]{:S(2)}) collective-permute-start(s16[32,2432]{1,0:T(8,128)(2,1)S(1)} %get-tuple-element.55), channel_id=1, source_target_pairs={{0,64},{64,128},{128,192},{192,0},{1,65},{65,129},{129,193},{193,1... | collective-permute-start | bytes 466952 | tf_op jit(solution)/shard_map/ppermute | solution.py:260
  60.6 2.0 %collective-permute-start.4 = (s16[32,2432]{1,0:T(8,128)(2,1)S(1)}, s16[32,2432]{1,0:T(8,128)(2,1)S(1)}, u32[]{:S(2)}, u32[]{:S(2)}) collective-permute-start(s16[32,2432]{1,0:T(8,128)(2,1)S(1)} %get-tuple-element.56), channel_id=1, source_target_pairs={{0,192},{64,0},{128,64},{192,128},{1,193},{65,1},{129,65},{193,129... | collective-permute-start | bytes 466952 | tf_op jit(solution)/shard_map/ppermute | solution.py:260
  62.6 3.5 %collective-permute-done.6.refs_1_.refs_3_ = s16[64,2432]{1,0:T(8,128)(2,1)S(1)} collective-permute-done((s16[64,2432]{1,0:T(8,128)(2,1)}, s16[64,2432]{1,0:T(8,128)(2,1)S(1)}, u32[]{:S(2)}, u32[]{:S(2)}) %collective-permute-start.6) | collective-permute-done | bytes 311328 | tf_op jit(solution)/shard_map/ppermute | solution.py:260
  66.6 2.4 %collective-permute-start.9 = (s16[32,2432]{1,0:T(8,128)(2,1)S(1)}, s16[32,2432]{1,0:T(8,128)(2,1)S(1)}, u32[]{:S(2)}, u32[]{:S(2)}) collective-permute-start(s16[32,2432]{1,0:T(8,128)(2,1)S(1)} %get-tuple-element.65), channel_id=1, source_target_pairs={{0,64},{64,128},{128,192},{192,0},{1,65},{65,129},{129,193},{193,1... | collective-permute-start | bytes 466952 | tf_op jit(solution)/shard_map/ppermute | solution.py:260
  69.0 2.0 %collective-permute-start.10 = (s16[32,2432]{1,0:T(8,128)(2,1)S(1)}, s16[32,2432]{1,0:T(8,128)(2,1)S(1)}, u32[]{:S(2)}, u32[]{:S(2)}) collective-permute-start(s16[32,2432]{1,0:T(8,128)(2,1)S(1)} %get-tuple-element.66), channel_id=1, source_target_pairs={{0,192},{64,0},{128,64},{192,128},{1,193},{65,1},{129,65},{193,129... | collective-permute-start | bytes 466952 | tf_op jit(solution)/shard_map/ppermute | solution.py:260
  71.9 1.2 shard_map.64
  73.1 2.4 %collective-permute-start.8 = (s16[64,2432]{1,0:T(8,128)(2,1)S(1)}, s16[64,2432]{1,0:T(8,128)(2,1)S(1)}, u32[]{:S(2)}, u32[]{:S(2)}) collective-permute-start(s16[64,2432]{1,0:T(8,128)(2,1)S(1)} %get-tuple-element.63.refs_1_), channel_id=1, source_target_pairs={{0,192},{64,0},{128,64},{192,128},{1,193},{65,1},{129,65},{193,129... | collective-permute-start | bytes 933896 | tf_op jit(solution)/shard_map/ppermute | solution.py:260
  76.1 6.3 %collective-permute-done.10.refs_5_ = s16[32,2432]{1,0:T(8,128)(2,1)S(1)} collective-permute-done((s16[32,2432]{1,0:T(8,128)(2,1)S(1)}, s16[32,2432]{1,0:T(8,128)(2,1)S(1)}, u32[]{:S(2)}, u32[]{:S(2)}) %collective-permute-start.10) | collective-permute-done | bytes 155680 | tf_op jit(solution)/shard_map/ppermute | solution.py:260
  82.4 1.2 shard_map.65
  83.5 1.9 %collective-permute-start.12 = (s16[64,2432]{1,0:T(8,128)(2,1)S(1)}, s16[64,2432]{1,0:T(8,128)(2,1)S(1)}, u32[]{:S(2)}, u32[]{:S(2)}) collective-permute-start(s16[64,2432]{1,0:T(8,128)(2,1)S(1)} %get-tuple-element.69.refs_1_), channel_id=1, source_target_pairs={{0,192},{64,0},{128,64},{192,128},{1,193},{65,1},{129,65},{193,129... | collective-permute-start | bytes 933896 | tf_op jit(solution)/shard_map/ppermute | solution.py:260
  86.5 1.2 collective-permute-done.13.refs_1_
  87.7 23.3 %all_to_all.16.refs_0_ = f32[32,8,128]{2,1,0:T(8,128)S(1)} all-to-all(f32[32,8,128]{2,1,0:T(8,128)S(1)} %broadcast_in_dim.8), channel_id=1, replica_groups=mesh['row'=4,'y'=4,'core'=2,'z_lo'=2,'x'=4] {'y','z_lo','x'}, dimensions={0} | all-to-all | bytes 262144 | tf_op jit(solution)/shard_map/all_to_all | solution.py:369
  111.1 2.1 %collective-permute-start.14 = (s16[64,2432]{1,0:T(8,128)(2,1)S(1)}, s16[64,2432]{1,0:T(8,128)(2,1)S(1)}, u32[]{:S(2)}, u32[]{:S(2)}) collective-permute-start(s16[64,2432]{1,0:T(8,128)(2,1)S(1)} %get-tuple-element.75), channel_id=1, source_target_pairs={{0,64},{64,128},{128,192},{192,0},{1,65},{65,129},{129,193},{193,1... | collective-permute-start | bytes 933896 | tf_op jit(solution)/shard_map/ppermute | solution.py:260
  113.2 2.2 %collective-permute-start.15 = (s16[64,2432]{1,0:T(8,128)(2,1)S(1)}, s16[64,2432]{1,0:T(8,128)(2,1)S(1)}, u32[]{:S(2)}, u32[]{:S(2)}) collective-permute-start(s16[64,2432]{1,0:T(8,128)(2,1)S(1)} %get-tuple-element.76), channel_id=1, source_target_pairs={{0,192},{64,0},{128,64},{192,128},{1,193},{65,1},{129,65},{193,129... | collective-permute-start | bytes 933896 | tf_op jit(solution)/shard_map/ppermute | solution.py:260
  115.4 2.4 %collective-permute-start.18 = (f32[8,128]{1,0:T(8,128)S(1)}, f32[8,128]{1,0:T(8,128)S(1)}, u32[]{:S(2)}, u32[]{:S(2)}) collective-permute-start(f32[8,128]{1,0:T(8,128)S(1)} %get-tuple-element.77.refs_6_), channel_id=1, source_target_pairs={{0,128},{64,192},{128,0},{192,64},{1,129},{65,193},{129,1},{193,65... | collective-permute-start | bytes 12296 | tf_op jit(solution)/shard_map/ppermute | solution.py:260
  117.8 1.9 %collective-permute-start.17 = (f32[8,128]{1,0:T(8,128)S(1)}, f32[8,128]{1,0:T(8,128)S(1)}, u32[]{:S(2)}, u32[]{:S(2)}) collective-permute-start(f32[8,128]{1,0:T(8,128)S(1)} %get-tuple-element.77.refs_6_), channel_id=1, source_target_pairs={{0,192},{64,0},{128,64},{192,128},{1,193},{65,1},{129,65},{193,129... | collective-permute-start | bytes 12296 | tf_op jit(solution)/shard_map/ppermute | solution.py:260
  120.7 10.0 %collective-permute-done.18.refs_9_ = f32[8,128]{1,0:T(8,128)S(1)} collective-permute-done((f32[8,128]{1,0:T(8,128)S(1)}, f32[8,128]{1,0:T(8,128)S(1)}, u32[]{:S(2)}, u32[]{:S(2)}) %collective-permute-start.18) | collective-permute-done | bytes 4128 | tf_op jit(solution)/shard_map/ppermute | solution.py:260
  130.7 2.9 %shard_map.69 = (f32[256,1280]{1,0:T(8,128)S(1)}, bf16[256,2432]{1,0:T(8,128)(2,1)}, f32[8,128]{1,0:T(8,128)S(1)}) custom-call(s32[2]{0:T(128)S(1)} %pad_add_fusion.refs_0_, s16[64,2432]{1,0:T(8,128)(2,1)S(1)} %get-tuple-element.69.refs_1_, s16[64,2432]{1,0:T(8,128)(2,1)S(1)} %collective-permute-done.11.refs_2_, ...), custom_call_target="tpu_custom_call" | custom-call | flops 1 | bytes 1 | tf_op jit(solution)/shard_map/pallas_call | solution.py:292
  133.9 2.9 %shard_map.70 = (f32[256,1280]{1,0:T(8,128)S(1)}, bf16[256,2432]{1,0:T(8,128)(2,1)}, f32[8,128]{1,0:T(8,128)S(1)}) custom-call(s32[2]{0:T(128)S(1)} %pad_add_fusion.refs_0_, s16[64,2432]{1,0:T(8,128)(2,1)S(1)} %get-tuple-element.63.refs_1_, s16[64,2432]{1,0:T(8,128)(2,1)S(1)} %collective-permute-done.7.refs_0_.refs_2_, ...), custom_call_target="tpu_custom_call" | custom-call | flops 1 | bytes 1 | tf_op jit(solution)/shard_map/pallas_call | solution.py:292
  137.9 4.9 %all-to-all-start.2 = ((bf16[32,8,1280]{2,1,0:T(8,128)(2,1)}), bf16[32,8,1280]{2,1,0:T(8,128)(2,1)S(1)}, u32[]{:S(2)}, u32[]{:S(2)}) async-start(bf16[32,8,1280]{2,1,0:T(8,128)(2,1)} %bitcast.5), calls=%async_computation.2 | async-start | bytes 1310720 | tf_op jit(solution)/shard_map/all_to_all | solution.py:381
  142.9 1.3 copy-done.12
  144.2 1.3 copy-done.13
  145.5 5.9 %shard_map.72 = (bf16[2374,1280]{1,0:T(8,128)(2,1)}, f32[8,128]{1,0:T(8,128)S(1)}) custom-call(bf16[256,1280]{1,0:T(8,128)(2,1)S(1)} %bitcast.9, bf16[256,1280]{1,0:T(8,128)(2,1)S(1)} %collective-permute-done.2.refs_1_.act_b_ref, bf16[256,2432]{1,0:T(8,128)(2,1)S(1)} %copy-done.13, bf16[256,2432]{1,0:T(8,128)(2,1)S(1)} %copy-done.12), custom_call_target="tpu_custom_call" | custom-call | flops 3111649280 | bytes 1 | tf_op jit(solution)/shard_map/pallas_call | solution.py:386
  151.3 4.4 %all-to-all-done.2.refs_0_ = bf16[32,8,1280]{2,1,0:T(8,128)(2,1)S(1)} async-done(((bf16[32,8,1280]{2,1,0:T(8,128)(2,1)}), bf16[32,8,1280]{2,1,0:T(8,128)(2,1)S(1)}, u32[]{:S(2)}, u32[]{:S(2)}) %all-to-all-start.2) | async-done | bytes 655392 | tf_op jit(solution)/shard_map/all_to_all | solution.py:381
  (69 shorter events, 14.5 us)
Async XLA Ops:
  22.3 13.7 %collective-permute-start.2 = (bf16[256,1280]{1,0:T(8,128)(2,1)S(1)}, bf16[256,1280]{1,0:T(8,128)(2,1)S(1)}, u32[]{:S(2)}, u32[]{:S(2)}) collective-permute-start(bf16[256,1280]{1,0:T(8,128)(2,1)S(1)} %bitcast.7), channel_id=1, source_target_pairs={{0,8},{8,0},{1,9},{9,1},{2,10},{10,2},{3,11},{11,3},{4,12},{12,4},... | collective-permute-start | bytes 1966088 | tf_op jit(solution)/shard_map/ppermute | solution.py:264
  30.6 9.3 %copy-start = (bf16[2432,1280]{1,0:T(8,128)(2,1)}, bf16[2432,1280]{1,0:T(8,128)(2,1)S(1)}, u32[]{:S(2)}) copy-start(bf16[2432,1280]{1,0:T(8,128)(2,1)S(1)} %get-tuple-element.51.refs_2_.refs_11_) | copy-start | bytes 18677764
  30.6 9.3 %copy-start.4 = (f32[64,2432]{1,0:T(8,128)}, f32[64,2432]{1,0:T(8,128)S(1)}, u32[]{:S(2)}) copy-start(f32[64,2432]{1,0:T(8,128)S(1)} %get-tuple-element.46.refs_1_) | copy-start | bytes 1867780
  30.6 25.0 %collective-permute-start = (s16[64,2432]{1,0:T(8,128)(2,1)}, s16[64,2432]{1,0:T(8,128)(2,1)S(1)}, u32[]{:S(2)}, u32[]{:S(2)}) collective-permute-start(s16[64,2432]{1,0:T(8,128)(2,1)} %get-tuple-element.47), channel_id=1, source_target_pairs={{0,64},{64,128},{128,192},{192,0},{1,65},{65,129},{129,193},{193,1... | collective-permute-start | bytes 933896 | tf_op jit(solution)/shard_map/ppermute | solution.py:260
  33.9 22.1 %collective-permute-start.1 = (s16[64,2432]{1,0:T(8,128)(2,1)}, s16[64,2432]{1,0:T(8,128)(2,1)S(1)}, u32[]{:S(2)}, u32[]{:S(2)}) collective-permute-start(s16[64,2432]{1,0:T(8,128)(2,1)} %get-tuple-element.48), channel_id=1, source_target_pairs={{0,192},{64,0},{128,64},{192,128},{1,193},{65,1},{129,65},{193,129... | collective-permute-start | bytes 933896 | tf_op jit(solution)/shard_map/ppermute | solution.py:260
  36.0 9.6 %copy-start.14 = (s32[512,64]{0,1:T(8,128)S(1)}, s32[512,64]{0,1:T(8,128)}, u32[]{:S(2)}) copy-start(s32[512,64]{0,1:T(8,128)} %param.6) | copy-start | bytes 393220
  36.0 9.7 %copy-start.15 = (f32[512,64]{0,1:T(8,128)S(1)}, f32[512,64]{0,1:T(8,128)}, u32[]{:S(2)}) copy-start(f32[512,64]{0,1:T(8,128)} %param.7) | copy-start | bytes 393220
  41.4 21.2 %collective-permute-start.5 = (s16[64,2432]{1,0:T(8,128)(2,1)}, s16[64,2432]{1,0:T(8,128)(2,1)S(1)}, u32[]{:S(2)}, u32[]{:S(2)}) collective-permute-start(s16[64,2432]{1,0:T(8,128)(2,1)} %get-tuple-element.57), channel_id=1, source_target_pairs={{0,64},{64,128},{128,192},{192,0},{1,65},{65,129},{129,193},{193,1... | collective-permute-start | bytes 933896 | tf_op jit(solution)/shard_map/ppermute | solution.py:260
  42.9 23.3 %collective-permute-start.6 = (s16[64,2432]{1,0:T(8,128)(2,1)}, s16[64,2432]{1,0:T(8,128)(2,1)S(1)}, u32[]{:S(2)}, u32[]{:S(2)}) collective-permute-start(s16[64,2432]{1,0:T(8,128)(2,1)} %get-tuple-element.58), channel_id=1, source_target_pairs={{0,192},{64,0},{128,64},{192,128},{1,193},{65,1},{129,65},{193,129... | collective-permute-start | bytes 933896 | tf_op jit(solution)/shard_map/ppermute | solution.py:260
  45.9 20.3 %copy-start.7 = (f32[32,2432]{1,0:T(8,128)S(1)}, f32[32,2432]{1,0:T(8,128)}, u32[]{:S(2)}) copy-start(f32[32,2432]{1,0:T(8,128)} %copy-done.6) | copy-start | bytes 933892
  55.6 16.4 %copy-start.5 = (f32[64,2432]{1,0:T(8,128)S(1)}, f32[64,2432]{1,0:T(8,128)}, u32[]{:S(2)}) copy-start(f32[64,2432]{1,0:T(8,128)} %copy-done.4) | copy-start | bytes 1867780
  56.0 1.0 copy-start.9
  57.9 24.4 %copy-start.3 = (f32[64,2432]{1,0:T(8,128)S(1)}, f32[64,2432]{1,0:T(8,128)}, u32[]{:S(2)}) copy-start(f32[64,2432]{1,0:T(8,128)} %copy-done.2) | copy-start | bytes 1867780
  58.4 13.5 %collective-permute-start.3 = (s16[32,2432]{1,0:T(8,128)(2,1)S(1)}, s16[32,2432]{1,0:T(8,128)(2,1)S(1)}, u32[]{:S(2)}, u32[]{:S(2)}) collective-permute-start(s16[32,2432]{1,0:T(8,128)(2,1)S(1)} %get-tuple-element.55), channel_id=1, source_target_pairs={{0,64},{64,128},{128,192},{192,0},{1,65},{65,129},{129,193},{193,1... | collective-permute-start | bytes 466952 | tf_op jit(solution)/shard_map/ppermute | solution.py:260
  60.6 70.1 %copy-start.1 = (bf16[2432,1280]{1,0:T(8,128)(2,1)S(1)}, bf16[2432,1280]{1,0:T(8,128)(2,1)}, u32[]{:S(2)}) copy-start(bf16[2432,1280]{1,0:T(8,128)(2,1)} %copy-done) | copy-start | bytes 18677764
  60.6 11.3 %collective-permute-start.4 = (s16[32,2432]{1,0:T(8,128)(2,1)S(1)}, s16[32,2432]{1,0:T(8,128)(2,1)S(1)}, u32[]{:S(2)}, u32[]{:S(2)}) collective-permute-start(s16[32,2432]{1,0:T(8,128)(2,1)S(1)} %get-tuple-element.56), channel_id=1, source_target_pairs={{0,192},{64,0},{128,64},{192,128},{1,193},{65,1},{129,65},{193,129... | collective-permute-start | bytes 466952 | tf_op jit(solution)/shard_map/ppermute | solution.py:260
  66.6 9.5 %collective-permute-start.9 = (s16[32,2432]{1,0:T(8,128)(2,1)S(1)}, s16[32,2432]{1,0:T(8,128)(2,1)S(1)}, u32[]{:S(2)}, u32[]{:S(2)}) collective-permute-start(s16[32,2432]{1,0:T(8,128)(2,1)S(1)} %get-tuple-element.65), channel_id=1, source_target_pairs={{0,64},{64,128},{128,192},{192,0},{1,65},{65,129},{129,193},{193,1... | collective-permute-start | bytes 466952 | tf_op jit(solution)/shard_map/ppermute | solution.py:260
  69.0 13.4 %collective-permute-start.10 = (s16[32,2432]{1,0:T(8,128)(2,1)S(1)}, s16[32,2432]{1,0:T(8,128)(2,1)S(1)}, u32[]{:S(2)}, u32[]{:S(2)}) collective-permute-start(s16[32,2432]{1,0:T(8,128)(2,1)S(1)} %get-tuple-element.66), channel_id=1, source_target_pairs={{0,192},{64,0},{128,64},{192,128},{1,193},{65,1},{129,65},{193,129... | collective-permute-start | bytes 466952 | tf_op jit(solution)/shard_map/ppermute | solution.py:260
  73.1 37.9 %collective-permute-start.8 = (s16[64,2432]{1,0:T(8,128)(2,1)S(1)}, s16[64,2432]{1,0:T(8,128)(2,1)S(1)}, u32[]{:S(2)}, u32[]{:S(2)}) collective-permute-start(s16[64,2432]{1,0:T(8,128)(2,1)S(1)} %get-tuple-element.63.refs_1_), channel_id=1, source_target_pairs={{0,192},{64,0},{128,64},{192,128},{1,193},{65,1},{129,65},{193,129... | collective-permute-start | bytes 933896 | tf_op jit(solution)/shard_map/ppermute | solution.py:260
  75.5 35.5 %collective-permute-start.7 = (s16[64,2432]{1,0:T(8,128)(2,1)S(1)}, s16[64,2432]{1,0:T(8,128)(2,1)S(1)}, u32[]{:S(2)}, u32[]{:S(2)}) collective-permute-start(s16[64,2432]{1,0:T(8,128)(2,1)S(1)} %get-tuple-element.63.refs_1_), channel_id=1, source_target_pairs={{0,64},{64,128},{128,192},{192,0},{1,65},{65,129},{129,193},{193,1... | collective-permute-start | bytes 933896 | tf_op jit(solution)/shard_map/ppermute | solution.py:260
  83.5 27.5 %collective-permute-start.12 = (s16[64,2432]{1,0:T(8,128)(2,1)S(1)}, s16[64,2432]{1,0:T(8,128)(2,1)S(1)}, u32[]{:S(2)}, u32[]{:S(2)}) collective-permute-start(s16[64,2432]{1,0:T(8,128)(2,1)S(1)} %get-tuple-element.69.refs_1_), channel_id=1, source_target_pairs={{0,192},{64,0},{128,64},{192,128},{1,193},{65,1},{129,65},{193,129... | collective-permute-start | bytes 933896 | tf_op jit(solution)/shard_map/ppermute | solution.py:260
  85.4 25.6 %collective-permute-start.11 = (s16[64,2432]{1,0:T(8,128)(2,1)S(1)}, s16[64,2432]{1,0:T(8,128)(2,1)S(1)}, u32[]{:S(2)}, u32[]{:S(2)}) collective-permute-start(s16[64,2432]{1,0:T(8,128)(2,1)S(1)} %get-tuple-element.69.refs_1_), channel_id=1, source_target_pairs={{0,64},{64,128},{128,192},{192,0},{1,65},{65,129},{129,193},{193,1... | collective-permute-start | bytes 933896 | tf_op jit(solution)/shard_map/ppermute | solution.py:260
  86.5 1.2 collective-permute-start.13
  111.1 19.6 %collective-permute-start.14 = (s16[64,2432]{1,0:T(8,128)(2,1)S(1)}, s16[64,2432]{1,0:T(8,128)(2,1)S(1)}, u32[]{:S(2)}, u32[]{:S(2)}) collective-permute-start(s16[64,2432]{1,0:T(8,128)(2,1)S(1)} %get-tuple-element.75), channel_id=1, source_target_pairs={{0,64},{64,128},{128,192},{192,0},{1,65},{65,129},{129,193},{193,1... | collective-permute-start | bytes 933896 | tf_op jit(solution)/shard_map/ppermute | solution.py:260
  113.2 17.5 %collective-permute-start.15 = (s16[64,2432]{1,0:T(8,128)(2,1)S(1)}, s16[64,2432]{1,0:T(8,128)(2,1)S(1)}, u32[]{:S(2)}, u32[]{:S(2)}) collective-permute-start(s16[64,2432]{1,0:T(8,128)(2,1)S(1)} %get-tuple-element.76), channel_id=1, source_target_pairs={{0,192},{64,0},{128,64},{192,128},{1,193},{65,1},{129,65},{193,129... | collective-permute-start | bytes 933896 | tf_op jit(solution)/shard_map/ppermute | solution.py:260
  115.4 15.2 %collective-permute-start.18 = (f32[8,128]{1,0:T(8,128)S(1)}, f32[8,128]{1,0:T(8,128)S(1)}, u32[]{:S(2)}, u32[]{:S(2)}) collective-permute-start(f32[8,128]{1,0:T(8,128)S(1)} %get-tuple-element.77.refs_6_), channel_id=1, source_target_pairs={{0,128},{64,192},{128,0},{192,64},{1,129},{65,193},{129,1},{193,65... | collective-permute-start | bytes 12296 | tf_op jit(solution)/shard_map/ppermute | solution.py:260
  117.8 12.9 %collective-permute-start.17 = (f32[8,128]{1,0:T(8,128)S(1)}, f32[8,128]{1,0:T(8,128)S(1)}, u32[]{:S(2)}, u32[]{:S(2)}) collective-permute-start(f32[8,128]{1,0:T(8,128)S(1)} %get-tuple-element.77.refs_6_), channel_id=1, source_target_pairs={{0,192},{64,0},{128,64},{192,128},{1,193},{65,1},{129,65},{193,129... | collective-permute-start | bytes 12296 | tf_op jit(solution)/shard_map/ppermute | solution.py:260
  119.7 11.0 %collective-permute-start.16 = (f32[8,128]{1,0:T(8,128)S(1)}, f32[8,128]{1,0:T(8,128)S(1)}, u32[]{:S(2)}, u32[]{:S(2)}) collective-permute-start(f32[8,128]{1,0:T(8,128)S(1)} %get-tuple-element.77.refs_6_), channel_id=1, source_target_pairs={{0,64},{64,128},{128,192},{192,0},{1,65},{65,129},{129,193},{193,1... | collective-permute-start | bytes 12296 | tf_op jit(solution)/shard_map/ppermute | solution.py:260
  133.6 3.3 %collective-permute-start.19 = (f32[256,1280]{1,0:T(8,128)S(1)}, f32[256,1280]{1,0:T(8,128)S(1)}, u32[]{:S(2)}, u32[]{:S(2)}) collective-permute-start(f32[256,1280]{1,0:T(8,128)S(1)} %get-tuple-element.82), channel_id=1, source_target_pairs={{0,8},{8,0},{1,9},{9,1},{2,10},{10,2},{3,11},{11,3},{4,12},{12,4},... | collective-permute-start | bytes 3932168 | tf_op jit(solution)/shard_map/ppermute | solution.py:264
  137.9 17.8 %all-to-all-start.2 = ((bf16[32,8,1280]{2,1,0:T(8,128)(2,1)}), bf16[32,8,1280]{2,1,0:T(8,128)(2,1)S(1)}, u32[]{:S(2)}, u32[]{:S(2)}) async-start(bf16[32,8,1280]{2,1,0:T(8,128)(2,1)} %bitcast.5), calls=%async_computation.2 | async-start | bytes 1310720 | tf_op jit(solution)/shard_map/all_to_all | solution.py:381
  142.9 1.3 copy-start.12
  144.2 1.3 copy-start.13
  (5 other events, 4.0 us)

commit v4 on v3

--- a/solution.py
+++ b/solution.py
@@ -60,8 +60,8 @@
     rest = rest_ref.shape[0]
     copied = width // rest * rest
     copies = []
-    for i, start in enumerate(range(0, copied, 512)):
-        rows = pl.ds(start, min(512, copied - start))
+    for i, start in enumerate(range(0, copied, 1024)):
+        rows = pl.ds(start, min(1024, copied - start))
         copies.append(pltpu.make_async_copy(weight_hbm.at[rows], weight_ref.at[rows], sems.at[i]))
         copies[-1].start()
     weight_ref[copied : copied + rest, :] = rest_ref[...]
@@ -78,8 +78,9 @@
     quarter, half = tokens // 4, tokens // 8
     padded = acc_ref.shape[1]
     act = act_ref[...]
-    for i, start in enumerate(range(0, padded, 512)):
-        stop = min(start + 512, padded)
+    tile = 1024 if copies else 512
+    for i, start in enumerate(range(0, padded, tile)):
+        stop = min(start + tile, padded)
         if copies:
             copies[i].wait()
         acc_ref[:, start:stop] = lax.dot_general(
@@ -342,7 +343,7 @@
         functools.partial(first_logits_kernel, width),
         part_outs + (((padded, depth), BF16),),
         (places, mine, rest, weight),
-        (acc, pltpu.SemaphoreType.DMA((8,))),
+        (acc, pltpu.SemaphoreType.DMA((3,))),
     )
     one_a = both_ways(parts_a[1], parts_a[2])
     *parts_b, done = call(

time: 158 us -> 158 us (level)
  transfers between devices with their start and end apart: 21 -> 21, of which waited for: 8 -> 9; matrix products, arithmetic and copies ran while one was open for 1% -> 1% of each run, Pallas kernels for 20% -> 20%
where the time goes in v4:
time: 158 us
  blocking collectives  44.6 us (28%)
  starting transfers between devices  40.4 us (26%)
  Pallas kernels  36 us (23%)
  waiting for transfers between devices  25.7 us (16%)
  local copies, waits for them, and re-layouts  9.91 us (6%)
    ppermute x17, starting transfers between devices, ring(): return lax.ppermute(x, 'row', [(i, (i + step) % 4) for i in range(4)])  34.4 us
    pallas_call x14, Pallas kernels, call(): pl.pallas_call(body, out_shape=tuple(((pltpu.HBM if space else pltpu.VMEM...  30.1 us
    all_to_all x1, blocking collectives, local(): lax.all_to_all(jnp.broadcast_to(paired[None], (chips, 8, 128)), CHIP, 0, 0)  23.6 us
    all_to_all x1, blocking collectives, local(): lax.all_to_all(jnp.broadcast_to(activations[None], (chips, own_tokens, de...  20.9 us
    ppermute x17, waiting for transfers between devices, ring(): return lax.ppermute(x, 'row', [(i, (i + step) % 4) for i in range(4)])  20.2 us
    unnamed x35, local copies, waits for them, and re-layouts  8.39 us
    pallas_call x1, Pallas kernels, local(): pl.pallas_call(weight_kernel, out_shape=(pltpu.HBM((width, depth), BF16),...  5.89 us
    all_to_all x1, starting transfers between devices, local(): lax.all_to_all(summed.reshape(chips, own_tokens, depth), CHIP, 0, 0)  5.66 us
  transfers between devices with their start and end apart: 21, of which 9 were waited for; matrix products, arithmetic and copies ran while one was open for 1% of the time, Pallas kernels for 20%

profile of v4, /device:TPU:2, one launch (start us, length us, event | category | flops | bytes accessed | tf_op | source)
XLA Modules:
  0.0 157.6 jit_solution(7678312327871959123)
XLA Ops:
  1.4 20.9 %all_to_all.15 = bf16[32,8,1280]{2,1,0:T(8,128)(2,1)S(1)} all-to-all(bf16[32,8,1280]{2,1,0:T(8,128)(2,1)S(1)} %broadcast_in_dim.6), channel_id=1, replica_groups=mesh['row'=4,'y'=4,'core'=2,'z_lo'=2,'x'=4] {'y','z_lo','x'}, dimensions={0} | all-to-all | bytes 1310720 | tf_op jit(solution)/shard_map/all_to_all | solution.py:279
  23.2 5.9 %shard_map.59 = (f32[64,2432]{1,0:T(8,128)S(1)}, s16[64,2432]{1,0:T(8,128)(2,1)}, s16[64,2432]{1,0:T(8,128)(2,1)}, f32[32,2432]{1,0:T(8,128)S(1)}, f32[32,2432]{...) custom-call(s32[2]{0:T(128)S(1)} %pad_add_fusion.refs_0_, bf16[256,1280]{1,0:T(8,128)(2,1)S(1)} %bitcast.8, ...), custom_call_target="tpu_custom_call" | custom-call | flops 1 | bytes 1 | tf_op jit(solution)/shard_map/pallas_call | solution.py:293
  30.6 3.3 %collective-permute-start = (s16[64,2432]{1,0:T(8,128)(2,1)}, s16[64,2432]{1,0:T(8,128)(2,1)S(1)}, u32[]{:S(2)}, u32[]{:S(2)}) collective-permute-start(s16[64,2432]{1,0:T(8,128)(2,1)} %get-tuple-element.47), channel_id=1, source_target_pairs={{0,64},{64,128},{128,192},{192,0},{1,65},{65,129},{129,193},{193,1... | collective-permute-start | bytes 933896 | tf_op jit(solution)/shard_map/ppermute | solution.py:261
  33.8 2.1 %collective-permute-start.1 = (s16[64,2432]{1,0:T(8,128)(2,1)}, s16[64,2432]{1,0:T(8,128)(2,1)S(1)}, u32[]{:S(2)}, u32[]{:S(2)}) collective-permute-start(s16[64,2432]{1,0:T(8,128)(2,1)} %get-tuple-element.48), channel_id=1, source_target_pairs={{0,192},{64,0},{128,64},{192,128},{1,193},{65,1},{129,65},{193,129... | collective-permute-start | bytes 933896 | tf_op jit(solution)/shard_map/ppermute | solution.py:261
  36.0 3.9 %shard_map.60 = (f32[64,2432]{1,0:T(8,128)S(1)}, s16[64,2432]{1,0:T(8,128)(2,1)}, s16[64,2432]{1,0:T(8,128)(2,1)}, f32[32,2432]{1,0:T(8,128)S(1)}, f32[32,2432]{1,0:T(8,128)S(1)}, /*index=5*/f32[8,128]{1,0:T(8,128)S(1)}) custom-call(s32[2]{0:T(128)S(1)} %pad_add_fusion.refs_0_, bf16[256,1280]{1,0:T(8,128)(2,1)S(1)} %collective-permute-done.2.refs_1_.act_b_ref, ...), custom_call_target="tpu_custom_call" | custom-call | flops 1 | bytes 1 | tf_op jit(solution)/shard_map/pallas_call | solution.py:293
  41.4 1.5 collective-permute-start.5
  42.9 2.7 %collective-permute-start.6 = (s16[64,2432]{1,0:T(8,128)(2,1)}, s16[64,2432]{1,0:T(8,128)(2,1)S(1)}, u32[]{:S(2)}, u32[]{:S(2)}) collective-permute-start(s16[64,2432]{1,0:T(8,128)(2,1)} %get-tuple-element.58), channel_id=1, source_target_pairs={{0,192},{64,0},{128,64},{192,128},{1,193},{65,1},{129,65},{193,129... | collective-permute-start | bytes 933896 | tf_op jit(solution)/shard_map/ppermute | solution.py:261
  45.9 9.6 %shard_map.61 = (f32[512,2432]{1,0:T(8,128)S(1)}, f32[8,128]{1,0:T(8,128)S(1)}) custom-call(s32[2]{0:T(128)S(1)} %pad_add_fusion.1.refs_0_, s32[512,64]{1,0:T(8,128)S(1)} %copy.6.refs_1_, f32[512,64]{1,0:T(8,128)S(1)} %copy.7.refs_2_, f32[8,128]{1,0:T(8,128)S(1)} %get-tuple-element.53.refs_3_), custom_call_target="tpu_custom_call" | custom-call | flops 1 | bytes 1 | tf_op jit(solution)/shard_map/pallas_call | solution.py:293
  58.4 2.2 %collective-permute-start.3 = (s16[32,2432]{1,0:T(8,128)(2,1)S(1)}, s16[32,2432]{1,0:T(8,128)(2,1)S(1)}, u32[]{:S(2)}, u32[]{:S(2)}) collective-permute-start(s16[32,2432]{1,0:T(8,128)(2,1)S(1)} %get-tuple-element.55), channel_id=1, source_target_pairs={{0,64},{64,128},{128,192},{192,0},{1,65},{65,129},{129,193},{193,1... | collective-permute-start | bytes 466952 | tf_op jit(solution)/shard_map/ppermute | solution.py:261
  60.6 2.0 %collective-permute-start.4 = (s16[32,2432]{1,0:T(8,128)(2,1)S(1)}, s16[32,2432]{1,0:T(8,128)(2,1)S(1)}, u32[]{:S(2)}, u32[]{:S(2)}) collective-permute-start(s16[32,2432]{1,0:T(8,128)(2,1)S(1)} %get-tuple-element.56), channel_id=1, source_target_pairs={{0,192},{64,0},{128,64},{192,128},{1,193},{65,1},{129,65},{193,129... | collective-permute-start | bytes 466952 | tf_op jit(solution)/shard_map/ppermute | solution.py:261
  62.6 3.5 %collective-permute-done.6.refs_1_.refs_3_ = s16[64,2432]{1,0:T(8,128)(2,1)S(1)} collective-permute-done((s16[64,2432]{1,0:T(8,128)(2,1)}, s16[64,2432]{1,0:T(8,128)(2,1)S(1)}, u32[]{:S(2)}, u32[]{:S(2)}) %collective-permute-start.6) | collective-permute-done | bytes 311328 | tf_op jit(solution)/shard_map/ppermute | solution.py:261
  66.6 2.4 %collective-permute-start.9 = (s16[32,2432]{1,0:T(8,128)(2,1)S(1)}, s16[32,2432]{1,0:T(8,128)(2,1)S(1)}, u32[]{:S(2)}, u32[]{:S(2)}) collective-permute-start(s16[32,2432]{1,0:T(8,128)(2,1)S(1)} %get-tuple-element.65), channel_id=1, source_target_pairs={{0,64},{64,128},{128,192},{192,0},{1,65},{65,129},{129,193},{193,1... | collective-permute-start | bytes 466952 | tf_op jit(solution)/shard_map/ppermute | solution.py:261
  69.0 2.0 %collective-permute-start.10 = (s16[32,2432]{1,0:T(8,128)(2,1)S(1)}, s16[32,2432]{1,0:T(8,128)(2,1)S(1)}, u32[]{:S(2)}, u32[]{:S(2)}) collective-permute-start(s16[32,2432]{1,0:T(8,128)(2,1)S(1)} %get-tuple-element.66), channel_id=1, source_target_pairs={{0,192},{64,0},{128,64},{192,128},{1,193},{65,1},{129,65},{193,129... | collective-permute-start | bytes 466952 | tf_op jit(solution)/shard_map/ppermute | solution.py:261
  71.9 1.2 shard_map.64
  73.1 2.4 %collective-permute-start.8 = (s16[64,2432]{1,0:T(8,128)(2,1)S(1)}, s16[64,2432]{1,0:T(8,128)(2,1)S(1)}, u32[]{:S(2)}, u32[]{:S(2)}) collective-permute-start(s16[64,2432]{1,0:T(8,128)(2,1)S(1)} %get-tuple-element.63.refs_1_), channel_id=1, source_target_pairs={{0,192},{64,0},{128,64},{192,128},{1,193},{65,1},{129,65},{193,129... | collective-permute-start | bytes 933896 | tf_op jit(solution)/shard_map/ppermute | solution.py:261
  76.1 6.2 %collective-permute-done.10.refs_5_ = s16[32,2432]{1,0:T(8,128)(2,1)S(1)} collective-permute-done((s16[32,2432]{1,0:T(8,128)(2,1)S(1)}, s16[32,2432]{1,0:T(8,128)(2,1)S(1)}, u32[]{:S(2)}, u32[]{:S(2)}) %collective-permute-start.10) | collective-permute-done | bytes 155680 | tf_op jit(solution)/shard_map/ppermute | solution.py:261
  82.3 1.2 shard_map.65
  83.5 2.6 %collective-permute-start.12 = (s16[64,2432]{1,0:T(8,128)(2,1)S(1)}, s16[64,2432]{1,0:T(8,128)(2,1)S(1)}, u32[]{:S(2)}, u32[]{:S(2)}) collective-permute-start(s16[64,2432]{1,0:T(8,128)(2,1)S(1)} %get-tuple-element.69.refs_1_), channel_id=1, source_target_pairs={{0,192},{64,0},{128,64},{192,128},{1,193},{65,1},{129,65},{193,129... | collective-permute-start | bytes 933896 | tf_op jit(solution)/shard_map/ppermute | solution.py:261
  86.5 1.2 collective-permute-done.13.refs_1_
  87.6 23.6 %all_to_all.16.refs_0_ = f32[32,8,128]{2,1,0:T(8,128)S(1)} all-to-all(f32[32,8,128]{2,1,0:T(8,128)S(1)} %broadcast_in_dim.8), channel_id=1, replica_groups=mesh['row'=4,'y'=4,'core'=2,'z_lo'=2,'x'=4] {'y','z_lo','x'}, dimensions={0} | all-to-all | bytes 262144 | tf_op jit(solution)/shard_map/all_to_all | solution.py:370
  111.4 3.7 %collective-permute-start.14 = (s16[64,2432]{1,0:T(8,128)(2,1)S(1)}, s16[64,2432]{1,0:T(8,128)(2,1)S(1)}, u32[]{:S(2)}, u32[]{:S(2)}) collective-permute-start(s16[64,2432]{1,0:T(8,128)(2,1)S(1)} %get-tuple-element.75), channel_id=1, source_target_pairs={{0,64},{64,128},{128,192},{192,0},{1,65},{65,129},{129,193},{193,1... | collective-permute-start | bytes 933896 | tf_op jit(solution)/shard_map/ppermute | solution.py:261
  115.7 3.0 %collective-permute-start.18 = (f32[8,128]{1,0:T(8,128)S(1)}, f32[8,128]{1,0:T(8,128)S(1)}, u32[]{:S(2)}, u32[]{:S(2)}) collective-permute-start(f32[8,128]{1,0:T(8,128)S(1)} %get-tuple-element.77.refs_6_), channel_id=1, source_target_pairs={{0,128},{64,192},{128,0},{192,64},{1,129},{65,193},{129,1},{193,65... | collective-permute-start | bytes 12296 | tf_op jit(solution)/shard_map/ppermute | solution.py:261
  118.8 2.8 %collective-permute-start.17 = (f32[8,128]{1,0:T(8,128)S(1)}, f32[8,128]{1,0:T(8,128)S(1)}, u32[]{:S(2)}, u32[]{:S(2)}) collective-permute-start(f32[8,128]{1,0:T(8,128)S(1)} %get-tuple-element.77.refs_6_), channel_id=1, source_target_pairs={{0,192},{64,0},{128,64},{192,128},{1,193},{65,1},{129,65},{193,129... | collective-permute-start | bytes 12296 | tf_op jit(solution)/shard_map/ppermute | solution.py:261
  121.7 9.0 %collective-permute-done.18.refs_9_ = f32[8,128]{1,0:T(8,128)S(1)} collective-permute-done((f32[8,128]{1,0:T(8,128)S(1)}, f32[8,128]{1,0:T(8,128)S(1)}, u32[]{:S(2)}, u32[]{:S(2)}) %collective-permute-start.18) | collective-permute-done | bytes 4128 | tf_op jit(solution)/shard_map/ppermute | solution.py:261
  130.8 2.9 %shard_map.69 = (f32[256,1280]{1,0:T(8,128)S(1)}, bf16[256,2432]{1,0:T(8,128)(2,1)}, f32[8,128]{1,0:T(8,128)S(1)}) custom-call(s32[2]{0:T(128)S(1)} %pad_add_fusion.refs_0_, s16[64,2432]{1,0:T(8,128)(2,1)S(1)} %get-tuple-element.69.refs_1_, s16[64,2432]{1,0:T(8,128)(2,1)S(1)} %collective-permute-done.11.refs_2_, ...), custom_call_target="tpu_custom_call" | custom-call | flops 1 | bytes 1 | tf_op jit(solution)/shard_map/pallas_call | solution.py:293
  134.0 2.9 %shard_map.70 = (f32[256,1280]{1,0:T(8,128)S(1)}, bf16[256,2432]{1,0:T(8,128)(2,1)}, f32[8,128]{1,0:T(8,128)S(1)}) custom-call(s32[2]{0:T(128)S(1)} %pad_add_fusion.refs_0_, s16[64,2432]{1,0:T(8,128)(2,1)S(1)} %get-tuple-element.63.refs_1_, s16[64,2432]{1,0:T(8,128)(2,1)S(1)} %collective-permute-done.7.refs_0_.refs_2_, ...), custom_call_target="tpu_custom_call" | custom-call | flops 1 | bytes 1 | tf_op jit(solution)/shard_map/pallas_call | solution.py:293
  137.1 1.0 shard_map.71
  138.0 5.7 %all-to-all-start.2 = ((bf16[32,8,1280]{2,1,0:T(8,128)(2,1)}), bf16[32,8,1280]{2,1,0:T(8,128)(2,1)S(1)}, u32[]{:S(2)}, u32[]{:S(2)}) async-start(bf16[32,8,1280]{2,1,0:T(8,128)(2,1)} %bitcast.5), calls=%async_computation.2 | async-start | bytes 1310720 | tf_op jit(solution)/shard_map/all_to_all | solution.py:382
  143.7 1.3 copy-done.12
  145.0 1.3 copy-done.13
  146.3 5.9 %shard_map.72 = (bf16[2374,1280]{1,0:T(8,128)(2,1)}, f32[8,128]{1,0:T(8,128)S(1)}) custom-call(bf16[256,1280]{1,0:T(8,128)(2,1)S(1)} %bitcast.9, bf16[256,1280]{1,0:T(8,128)(2,1)S(1)} %collective-permute-done.2.refs_1_.act_b_ref, bf16[256,2432]{1,0:T(8,128)(2,1)S(1)} %copy-done.13, bf16[256,2432]{1,0:T(8,128)(2,1)S(1)} %copy-done.12), custom_call_target="tpu_custom_call" | custom-call | flops 3111649280 | bytes 1 | tf_op jit(solution)/shard_map/pallas_call | solution.py:387
  152.2 4.2 %all-to-all-done.2.refs_0_ = bf16[32,8,1280]{2,1,0:T(8,128)(2,1)S(1)} async-done(((bf16[32,8,1280]{2,1,0:T(8,128)(2,1)}), bf16[32,8,1280]{2,1,0:T(8,128)(2,1)S(1)}, u32[]{:S(2)}, u32[]{:S(2)}) %all-to-all-start.2) | async-done | bytes 655392 | tf_op jit(solution)/shard_map/all_to_all | solution.py:382
  (69 shorter events, 12.6 us)
Async XLA Ops:
  22.3 13.6 %collective-permute-start.2 = (bf16[256,1280]{1,0:T(8,128)(2,1)S(1)}, bf16[256,1280]{1,0:T(8,128)(2,1)S(1)}, u32[]{:S(2)}, u32[]{:S(2)}) collective-permute-start(bf16[256,1280]{1,0:T(8,128)(2,1)S(1)} %bitcast.7), channel_id=1, source_target_pairs={{0,8},{8,0},{1,9},{9,1},{2,10},{10,2},{3,11},{11,3},{4,12},{12,4},... | collective-permute-start | bytes 1966088 | tf_op jit(solution)/shard_map/ppermute | solution.py:265
  30.6 9.3 %copy-start = (bf16[2432,1280]{1,0:T(8,128)(2,1)}, bf16[2432,1280]{1,0:T(8,128)(2,1)S(1)}, u32[]{:S(2)}) copy-start(bf16[2432,1280]{1,0:T(8,128)(2,1)S(1)} %get-tuple-element.51.refs_2_.refs_11_) | copy-start | bytes 18677764
  30.6 9.3 %copy-start.4 = (f32[64,2432]{1,0:T(8,128)}, f32[64,2432]{1,0:T(8,128)S(1)}, u32[]{:S(2)}) copy-start(f32[64,2432]{1,0:T(8,128)S(1)} %get-tuple-element.46.refs_1_) | copy-start | bytes 1867780
  30.6 25.0 %collective-permute-start = (s16[64,2432]{1,0:T(8,128)(2,1)}, s16[64,2432]{1,0:T(8,128)(2,1)S(1)}, u32[]{:S(2)}, u32[]{:S(2)}) collective-permute-start(s16[64,2432]{1,0:T(8,128)(2,1)} %get-tuple-element.47), channel_id=1, source_target_pairs={{0,64},{64,128},{128,192},{192,0},{1,65},{65,129},{129,193},{193,1... | collective-permute-start | bytes 933896 | tf_op jit(solution)/shard_map/ppermute | solution.py:261
  33.8 22.1 %collective-permute-start.1 = (s16[64,2432]{1,0:T(8,128)(2,1)}, s16[64,2432]{1,0:T(8,128)(2,1)S(1)}, u32[]{:S(2)}, u32[]{:S(2)}) collective-permute-start(s16[64,2432]{1,0:T(8,128)(2,1)} %get-tuple-element.48), channel_id=1, source_target_pairs={{0,192},{64,0},{128,64},{192,128},{1,193},{65,1},{129,65},{193,129... | collective-permute-start | bytes 933896 | tf_op jit(solution)/shard_map/ppermute | solution.py:261
  36.0 9.6 %copy-start.14 = (s32[512,64]{0,1:T(8,128)S(1)}, s32[512,64]{0,1:T(8,128)}, u32[]{:S(2)}) copy-start(s32[512,64]{0,1:T(8,128)} %param.6) | copy-start | bytes 393220
  36.0 9.7 %copy-start.15 = (f32[512,64]{0,1:T(8,128)S(1)}, f32[512,64]{0,1:T(8,128)}, u32[]{:S(2)}) copy-start(f32[512,64]{0,1:T(8,128)} %param.7) | copy-start | bytes 393220
  41.4 21.2 %collective-permute-start.5 = (s16[64,2432]{1,0:T(8,128)(2,1)}, s16[64,2432]{1,0:T(8,128)(2,1)S(1)}, u32[]{:S(2)}, u32[]{:S(2)}) collective-permute-start(s16[64,2432]{1,0:T(8,128)(2,1)} %get-tuple-element.57), channel_id=1, source_target_pairs={{0,64},{64,128},{128,192},{192,0},{1,65},{65,129},{129,193},{193,1... | collective-permute-start | bytes 933896 | tf_op jit(solution)/shard_map/ppermute | solution.py:261
  42.9 23.2 %collective-permute-start.6 = (s16[64,2432]{1,0:T(8,128)(2,1)}, s16[64,2432]{1,0:T(8,128)(2,1)S(1)}, u32[]{:S(2)}, u32[]{:S(2)}) collective-permute-start(s16[64,2432]{1,0:T(8,128)(2,1)} %get-tuple-element.58), channel_id=1, source_target_pairs={{0,192},{64,0},{128,64},{192,128},{1,193},{65,1},{129,65},{193,129... | collective-permute-start | bytes 933896 | tf_op jit(solution)/shard_map/ppermute | solution.py:261
  45.8 20.3 %copy-start.7 = (f32[32,2432]{1,0:T(8,128)S(1)}, f32[32,2432]{1,0:T(8,128)}, u32[]{:S(2)}) copy-start(f32[32,2432]{1,0:T(8,128)} %copy-done.6) | copy-start | bytes 933892
  55.5 16.4 %copy-start.5 = (f32[64,2432]{1,0:T(8,128)S(1)}, f32[64,2432]{1,0:T(8,128)}, u32[]{:S(2)}) copy-start(f32[64,2432]{1,0:T(8,128)} %copy-done.4) | copy-start | bytes 1867780
  56.0 1.0 copy-start.9
  57.9 24.4 %copy-start.3 = (f32[64,2432]{1,0:T(8,128)S(1)}, f32[64,2432]{1,0:T(8,128)}, u32[]{:S(2)}) copy-start(f32[64,2432]{1,0:T(8,128)} %copy-done.2) | copy-start | bytes 1867780
  58.4 13.5 %collective-permute-start.3 = (s16[32,2432]{1,0:T(8,128)(2,1)S(1)}, s16[32,2432]{1,0:T(8,128)(2,1)S(1)}, u32[]{:S(2)}, u32[]{:S(2)}) collective-permute-start(s16[32,2432]{1,0:T(8,128)(2,1)S(1)} %get-tuple-element.55), channel_id=1, source_target_pairs={{0,64},{64,128},{128,192},{192,0},{1,65},{65,129},{129,193},{193,1... | collective-permute-start | bytes 466952 | tf_op jit(solution)/shard_map/ppermute | solution.py:261
  60.6 70.2 %copy-start.1 = (bf16[2432,1280]{1,0:T(8,128)(2,1)S(1)}, bf16[2432,1280]{1,0:T(8,128)(2,1)}, u32[]{:S(2)}) copy-start(bf16[2432,1280]{1,0:T(8,128)(2,1)} %copy-done) | copy-start | bytes 18677764
  60.6 11.3 %collective-permute-start.4 = (s16[32,2432]{1,0:T(8,128)(2,1)S(1)}, s16[32,2432]{1,0:T(8,128)(2,1)S(1)}, u32[]{:S(2)}, u32[]{:S(2)}) collective-permute-start(s16[32,2432]{1,0:T(8,128)(2,1)S(1)} %get-tuple-element.56), channel_id=1, source_target_pairs={{0,192},{64,0},{128,64},{192,128},{1,193},{65,1},{129,65},{193,129... | collective-permute-start | bytes 466952 | tf_op jit(solution)/shard_map/ppermute | solution.py:261
  66.6 9.5 %collective-permute-start.9 = (s16[32,2432]{1,0:T(8,128)(2,1)S(1)}, s16[32,2432]{1,0:T(8,128)(2,1)S(1)}, u32[]{:S(2)}, u32[]{:S(2)}) collective-permute-start(s16[32,2432]{1,0:T(8,128)(2,1)S(1)} %get-tuple-element.65), channel_id=1, source_target_pairs={{0,64},{64,128},{128,192},{192,0},{1,65},{65,129},{129,193},{193,1... | collective-permute-start | bytes 466952 | tf_op jit(solution)/shard_map/ppermute | solution.py:261
  69.0 13.3 %collective-permute-start.10 = (s16[32,2432]{1,0:T(8,128)(2,1)S(1)}, s16[32,2432]{1,0:T(8,128)(2,1)S(1)}, u32[]{:S(2)}, u32[]{:S(2)}) collective-permute-start(s16[32,2432]{1,0:T(8,128)(2,1)S(1)} %get-tuple-element.66), channel_id=1, source_target_pairs={{0,192},{64,0},{128,64},{192,128},{1,193},{65,1},{129,65},{193,129... | collective-permute-start | bytes 466952 | tf_op jit(solution)/shard_map/ppermute | solution.py:261
  73.1 38.2 %collective-permute-start.8 = (s16[64,2432]{1,0:T(8,128)(2,1)S(1)}, s16[64,2432]{1,0:T(8,128)(2,1)S(1)}, u32[]{:S(2)}, u32[]{:S(2)}) collective-permute-start(s16[64,2432]{1,0:T(8,128)(2,1)S(1)} %get-tuple-element.63.refs_1_), channel_id=1, source_target_pairs={{0,192},{64,0},{128,64},{192,128},{1,193},{65,1},{129,65},{193,129... | collective-permute-start | bytes 933896 | tf_op jit(solution)/shard_map/ppermute | solution.py:261
  75.5 35.8 %collective-permute-start.7 = (s16[64,2432]{1,0:T(8,128)(2,1)S(1)}, s16[64,2432]{1,0:T(8,128)(2,1)S(1)}, u32[]{:S(2)}, u32[]{:S(2)}) collective-permute-start(s16[64,2432]{1,0:T(8,128)(2,1)S(1)} %get-tuple-element.63.refs_1_), channel_id=1, source_target_pairs={{0,64},{64,128},{128,192},{192,0},{1,65},{65,129},{129,193},{193,1... | collective-permute-start | bytes 933896 | tf_op jit(solution)/shard_map/ppermute | solution.py:261
  83.5 27.9 %collective-permute-start.12 = (s16[64,2432]{1,0:T(8,128)(2,1)S(1)}, s16[64,2432]{1,0:T(8,128)(2,1)S(1)}, u32[]{:S(2)}, u32[]{:S(2)}) collective-permute-start(s16[64,2432]{1,0:T(8,128)(2,1)S(1)} %get-tuple-element.69.refs_1_), channel_id=1, source_target_pairs={{0,192},{64,0},{128,64},{192,128},{1,193},{65,1},{129,65},{193,129... | collective-permute-start | bytes 933896 | tf_op jit(solution)/shard_map/ppermute | solution.py:261
  86.1 25.2 %collective-permute-start.11 = (s16[64,2432]{1,0:T(8,128)(2,1)S(1)}, s16[64,2432]{1,0:T(8,128)(2,1)S(1)}, u32[]{:S(2)}, u32[]{:S(2)}) collective-permute-start(s16[64,2432]{1,0:T(8,128)(2,1)S(1)} %get-tuple-element.69.refs_1_), channel_id=1, source_target_pairs={{0,64},{64,128},{128,192},{192,0},{1,65},{65,129},{129,193},{193,1... | collective-permute-start | bytes 933896 | tf_op jit(solution)/shard_map/ppermute | solution.py:261
  86.5 1.2 collective-permute-start.13
  111.4 19.4 %collective-permute-start.14 = (s16[64,2432]{1,0:T(8,128)(2,1)S(1)}, s16[64,2432]{1,0:T(8,128)(2,1)S(1)}, u32[]{:S(2)}, u32[]{:S(2)}) collective-permute-start(s16[64,2432]{1,0:T(8,128)(2,1)S(1)} %get-tuple-element.75), channel_id=1, source_target_pairs={{0,64},{64,128},{128,192},{192,0},{1,65},{65,129},{129,193},{193,1... | collective-permute-start | bytes 933896 | tf_op jit(solution)/shard_map/ppermute | solution.py:261
  115.1 15.7 %collective-permute-start.15 = (s16[64,2432]{1,0:T(8,128)(2,1)S(1)}, s16[64,2432]{1,0:T(8,128)(2,1)S(1)}, u32[]{:S(2)}, u32[]{:S(2)}) collective-permute-start(s16[64,2432]{1,0:T(8,128)(2,1)S(1)} %get-tuple-element.76), channel_id=1, source_target_pairs={{0,192},{64,0},{128,64},{192,128},{1,193},{65,1},{129,65},{193,129... | collective-permute-start | bytes 933896 | tf_op jit(solution)/shard_map/ppermute | solution.py:261
  115.7 15.0 %collective-permute-start.18 = (f32[8,128]{1,0:T(8,128)S(1)}, f32[8,128]{1,0:T(8,128)S(1)}, u32[]{:S(2)}, u32[]{:S(2)}) collective-permute-start(f32[8,128]{1,0:T(8,128)S(1)} %get-tuple-element.77.refs_6_), channel_id=1, source_target_pairs={{0,128},{64,192},{128,0},{192,64},{1,129},{65,193},{129,1},{193,65... | collective-permute-start | bytes 12296 | tf_op jit(solution)/shard_map/ppermute | solution.py:261
  118.8 12.0 %collective-permute-start.17 = (f32[8,128]{1,0:T(8,128)S(1)}, f32[8,128]{1,0:T(8,128)S(1)}, u32[]{:S(2)}, u32[]{:S(2)}) collective-permute-start(f32[8,128]{1,0:T(8,128)S(1)} %get-tuple-element.77.refs_6_), channel_id=1, source_target_pairs={{0,192},{64,0},{128,64},{192,128},{1,193},{65,1},{129,65},{193,129... | collective-permute-start | bytes 12296 | tf_op jit(solution)/shard_map/ppermute | solution.py:261
  121.6 9.2 %collective-permute-start.16 = (f32[8,128]{1,0:T(8,128)S(1)}, f32[8,128]{1,0:T(8,128)S(1)}, u32[]{:S(2)}, u32[]{:S(2)}) collective-permute-start(f32[8,128]{1,0:T(8,128)S(1)} %get-tuple-element.77.refs_6_), channel_id=1, source_target_pairs={{0,64},{64,128},{128,192},{192,0},{1,65},{65,129},{129,193},{193,1... | collective-permute-start | bytes 12296 | tf_op jit(solution)/shard_map/ppermute | solution.py:261
  133.7 3.3 %collective-permute-start.19 = (f32[256,1280]{1,0:T(8,128)S(1)}, f32[256,1280]{1,0:T(8,128)S(1)}, u32[]{:S(2)}, u32[]{:S(2)}) collective-permute-start(f32[256,1280]{1,0:T(8,128)S(1)} %get-tuple-element.82), channel_id=1, source_target_pairs={{0,8},{8,0},{1,9},{9,1},{2,10},{10,2},{3,11},{11,3},{4,12},{12,4},... | collective-permute-start | bytes 3932168 | tf_op jit(solution)/shard_map/ppermute | solution.py:265
  138.0 18.4 %all-to-all-start.2 = ((bf16[32,8,1280]{2,1,0:T(8,128)(2,1)}), bf16[32,8,1280]{2,1,0:T(8,128)(2,1)S(1)}, u32[]{:S(2)}, u32[]{:S(2)}) async-start(bf16[32,8,1280]{2,1,0:T(8,128)(2,1)} %bitcast.5), calls=%async_computation.2 | async-start | bytes 1310720 | tf_op jit(solution)/shard_map/all_to_all | solution.py:382
  143.7 1.3 copy-start.12
  145.0 1.3 copy-start.13
  (5 other events, 4.0 us)

commit v5 on v3

--- a/solution.py
+++ b/solution.py
@@ -159,7 +159,8 @@
         return jnp.concatenate([block[n : n + 1, :] for n in range(8)], axis=1)
 
     def group(g, _):
-        rows = pl.ds(pl.multiple_of(g * 8, 8), 8)
+        source = (2 * (g // 8) + place_ref[1]) * 64 + (g % 8) * 8
+        rows = pl.ds(pl.multiple_of(source, 8), 8)
         ids = flat(ids_ref[rows, :]) - place_ref[0]
         value = flat(teacher_ref[rows, :])
         coarse = value.astype(BF16).astype(F32)
@@ -172,6 +173,7 @@
         dense += lax.dot_general(
             jnp.where(here, value - coarse, 0.0).astype(BF16), one_hot, contract, preferred_element_type=F32
         )
+        rows = pl.ds(pl.multiple_of(g * 8, 8), 8)
         for tile in range(tiles):
             block = dense[tile * 8 : tile * 8 + 8, :]
             if tile == tiles - 1:
@@ -179,7 +181,7 @@
             dense_ref[rows, tile * 128 : tile * 128 + 128] = block
         return 0
 
-    lax.fori_loop(0, tokens // 8, group, 0, unroll=8)
+    lax.fori_loop(0, dense_ref.shape[0] // 8, group, 0, unroll=8)
 
 
 def pair_stats_kernel(mine_ref, other_ref, out_ref):
@@ -201,13 +203,13 @@
     chunk = chunk_of(place_ref, which_chunk)
     owner = lax.rem(place_ref[0] + distance, 4)
     count = code.shape[0]
-    quarter = dense_ref.shape[0] // 8
+    quarter = dense_ref.shape[0] // 4
     first = owner * quarter + which * (quarter // 2)
-    token = pl.multiple_of((2 * owner + chunk) * quarter + which * (quarter // 2), quarter // 2)
+    first = pl.multiple_of(first, quarter // 2)
     scale = row_to_column(scale_ref[0:1, :], count, chunk * quarter + which * (quarter // 2))
     student = (code.astype(I32).astype(F32) + CODE_OFFSET) * scale
-    grad = student - LOSS_SCALE * dense_ref[pl.ds(token, count), :]
-    return grad.astype(BF16), pl.multiple_of(first, quarter // 2)
+    grad = student - LOSS_SCALE * dense_ref[pl.ds(first, count), :]
+    return grad.astype(BF16), first
 
 
 def hidden_kernel(
@@ -331,7 +333,7 @@
         return call(
             functools.partial(hidden_kernel, chunk),
             (((tokens, depth), F32), ((tokens, padded), BF16, pltpu.HBM)),
-            (places, own, *received, *codes_far, *scales, dense, weight),
+            (places, own, *received, *codes_far, *scales, (dense_a, dense_b)[chunk], weight),
             after=after,
         )
 
@@ -349,15 +351,19 @@
         functools.partial(logits_kernel, width), part_outs, (places, acts[1], weight), (acc,), (done,)
     )
     one_b = both_ways(parts_b[1], parts_b[2])
-    dense, done = call(
-        functools.partial(teacher_kernel, width),
-        (((2 * tokens, padded), F32),),
-        (jnp.stack([first_col, row]).astype(I32), teacher_ids, teacher_values),
-        (pltpu.VMEM(teacher_values.shape, F32),),
-        (done,),
-    )
+    def teacher(chunk, after):
+        return call(
+            functools.partial(teacher_kernel, width),
+            (((tokens, padded), F32),),
+            (jnp.stack([first_col, chunk]).astype(I32), teacher_ids, teacher_values),
+            (pltpu.VMEM(teacher_values.shape, F32),),
+            after,
+        )
+
+    dense_b, done = teacher(1 - core, (done,))
     *merged_a, done = merge(parts_a, one_a, (done,))
     two_a = both_ways(*merged_a)
+    dense_a, done = teacher(core, (done,))
     *merged_b, done = merge(parts_b, one_b, (done,))
     two_b = both_ways(*merged_b)
     code_a, stats, done = total(0, parts_a, one_a, two_a, jnp.zeros((8, 128), F32), (done,))

time: 158 us -> 158 us (level)
  blocking collectives: 44.2 us -> 47.2 us
  waiting for transfers between devices: 26.8 us -> 24.4 us
    all_to_all x1, blocking collectives: 23.3 us -> 26.3 us  [local(): lax.all_to_all(jnp.broadcast_to(paired[None], (chips, 8, 128)), CHIP, 0, 0)]
    ppermute x17, waiting for transfers between devices: 21.1 us -> 18.9 us  [ring(): return lax.ppermute(x, 'row', [(i, (i + step) % 4) for i in range(4)])]
    pallas_call x14 -> x15, Pallas kernels: 30.2 us -> 30.9 us  [call(): pl.pallas_call(body, out_shape=tuple(((pltpu.HBM if space else pltpu.VMEM...]
  transfers between devices with their start and end apart: 21 -> 21, of which waited for: 8 -> 6; matrix products, arithmetic and copies ran while one was open for 1% -> 1% of each run, Pallas kernels for 20% -> 20%
where the time goes in v5:
time: 158 us
  blocking collectives  47.2 us (30%)
  starting transfers between devices  38.3 us (24%)
  Pallas kernels  36.8 us (23%)
  waiting for transfers between devices  24.4 us (15%)
  local copies, waits for them, and re-layouts  9.92 us (6%)
    ppermute x17, starting transfers between devices, ring(): return lax.ppermute(x, 'row', [(i, (i + step) % 4) for i in range(4)])  33 us
    pallas_call x15, Pallas kernels, call(): pl.pallas_call(body, out_shape=tuple(((pltpu.HBM if space else pltpu.VMEM...  30.9 us
    all_to_all x1, blocking collectives, local(): lax.all_to_all(jnp.broadcast_to(paired[None], (chips, 8, 128)), CHIP, 0, 0)  26.3 us
    all_to_all x1, blocking collectives, local(): lax.all_to_all(jnp.broadcast_to(activations[None], (chips, own_tokens, de...  20.9 us
    ppermute x17, waiting for transfers between devices, ring(): return lax.ppermute(x, 'row', [(i, (i + step) % 4) for i in range(4)])  18.9 us
    unnamed x35, local copies, waits for them, and re-layouts  8.4 us
    pallas_call x1, Pallas kernels, local(): pl.pallas_call(weight_kernel, out_shape=(pltpu.HBM((width, depth), BF16),...  5.89 us
    all_to_all x1, starting transfers between devices, local(): lax.all_to_all(summed.reshape(chips, own_tokens, depth), CHIP, 0, 0)  5.18 us
  transfers between devices with their start and end apart: 21, of which 6 were waited for; matrix products, arithmetic and copies ran while one was open for 1% of the time, Pallas kernels for 20%

profile of v5, /device:TPU:2, one launch (start us, length us, event | category | flops | bytes accessed | tf_op | source)
XLA Modules:
  0.0 157.8 jit_solution(18304492174307886209)
XLA Ops:
  1.4 20.9 %all_to_all.15 = bf16[32,8,1280]{2,1,0:T(8,128)(2,1)S(1)} all-to-all(bf16[32,8,1280]{2,1,0:T(8,128)(2,1)S(1)} %broadcast_in_dim.6), channel_id=1, replica_groups=mesh['row'=4,'y'=4,'core'=2,'z_lo'=2,'x'=4] {'y','z_lo','x'}, dimensions={0} | all-to-all | bytes 1310720 | tf_op jit(solution)/shard_map/all_to_all | solution.py:280
  23.2 6.0 %shard_map.59 = (f32[64,2432]{1,0:T(8,128)S(1)}, s16[64,2432]{1,0:T(8,128)(2,1)}, s16[64,2432]{1,0:T(8,128)(2,1)}, f32[32,2432]{1,0:T(8,128)S(1)}, f32[32,2432]{...) custom-call(s32[2]{0:T(128)S(1)} %pad_add_fusion.refs_0_, bf16[256,1280]{1,0:T(8,128)(2,1)S(1)} %bitcast.9, ...), custom_call_target="tpu_custom_call" | custom-call | flops 1 | bytes 1 | tf_op jit(solution)/shard_map/pallas_call | solution.py:294
  30.6 3.3 %collective-permute-start = (s16[64,2432]{1,0:T(8,128)(2,1)}, s16[64,2432]{1,0:T(8,128)(2,1)S(1)}, u32[]{:S(2)}, u32[]{:S(2)}) collective-permute-start(s16[64,2432]{1,0:T(8,128)(2,1)} %get-tuple-element.49), channel_id=1, source_target_pairs={{0,64},{64,128},{128,192},{192,0},{1,65},{65,129},{129,193},{193,1... | collective-permute-start | bytes 933896 | tf_op jit(solution)/shard_map/ppermute | solution.py:262
  33.9 2.1 %collective-permute-start.1 = (s16[64,2432]{1,0:T(8,128)(2,1)}, s16[64,2432]{1,0:T(8,128)(2,1)S(1)}, u32[]{:S(2)}, u32[]{:S(2)}) collective-permute-start(s16[64,2432]{1,0:T(8,128)(2,1)} %get-tuple-element.50), channel_id=1, source_target_pairs={{0,192},{64,0},{128,64},{192,128},{1,193},{65,1},{129,65},{193,129... | collective-permute-start | bytes 933896 | tf_op jit(solution)/shard_map/ppermute | solution.py:262
  36.0 3.9 %shard_map.60 = (f32[64,2432]{1,0:T(8,128)S(1)}, s16[64,2432]{1,0:T(8,128)(2,1)}, s16[64,2432]{1,0:T(8,128)(2,1)}, f32[32,2432]{1,0:T(8,128)S(1)}, f32[32,2432]{1,0:T(8,128)S(1)}, /*index=5*/f32[8,128]{1,0:T(8,128)S(1)}) custom-call(s32[2]{0:T(128)S(1)} %pad_add_fusion.refs_0_, bf16[256,1280]{1,0:T(8,128)(2,1)S(1)} %collective-permute-done.2.refs_1_.act_b_ref, ...), custom_call_target="tpu_custom_call" | custom-call | flops 1 | bytes 1 | tf_op jit(solution)/shard_map/pallas_call | solution.py:294
  41.5 1.5 collective-permute-start.5
  42.9 2.7 %collective-permute-start.6 = (s16[64,2432]{1,0:T(8,128)(2,1)}, s16[64,2432]{1,0:T(8,128)(2,1)S(1)}, u32[]{:S(2)}, u32[]{:S(2)}) collective-permute-start(s16[64,2432]{1,0:T(8,128)(2,1)} %get-tuple-element.60), channel_id=1, source_target_pairs={{0,192},{64,0},{128,64},{192,128},{1,193},{65,1},{129,65},{193,129... | collective-permute-start | bytes 933896 | tf_op jit(solution)/shard_map/ppermute | solution.py:262
  46.1 5.2 %shard_map.61 = (f32[256,2432]{1,0:T(8,128)S(1)}, f32[8,128]{1,0:T(8,128)S(1)}) custom-call(s32[2]{0:T(128)S(1)} %pad_add_fusion.1.refs_0_, s32[512,64]{1,0:T(8,128)S(1)} %copy.6.refs_1_, f32[512,64]{1,0:T(8,128)S(1)} %copy.7.refs_2_, f32[8,128]{1,0:T(8,128)S(1)} %get-tuple-element.55.refs_3_), custom_call_target="tpu_custom_call" | custom-call | flops 1 | bytes 1 | tf_op jit(solution)/shard_map/pallas_call | solution.py:294
  51.3 4.7 %collective-permute-done.1.refs_1_.refs_3_ = s16[64,2432]{1,0:T(8,128)(2,1)S(1)} collective-permute-done((s16[64,2432]{1,0:T(8,128)(2,1)}, s16[64,2432]{1,0:T(8,128)(2,1)S(1)}, u32[]{:S(2)}, u32[]{:S(2)}) %collective-permute-start.1) | collective-permute-done | bytes 311328 | tf_op jit(solution)/shard_map/ppermute | solution.py:262
  58.4 2.2 %collective-permute-start.3 = (s16[32,2432]{1,0:T(8,128)(2,1)S(1)}, s16[32,2432]{1,0:T(8,128)(2,1)S(1)}, u32[]{:S(2)}, u32[]{:S(2)}) collective-permute-start(s16[32,2432]{1,0:T(8,128)(2,1)S(1)} %get-tuple-element.57), channel_id=1, source_target_pairs={{0,64},{64,128},{128,192},{192,0},{1,65},{65,129},{129,193},{193,1... | collective-permute-start | bytes 466952 | tf_op jit(solution)/shard_map/ppermute | solution.py:262
  60.6 2.0 %collective-permute-start.4 = (s16[32,2432]{1,0:T(8,128)(2,1)S(1)}, s16[32,2432]{1,0:T(8,128)(2,1)S(1)}, u32[]{:S(2)}, u32[]{:S(2)}) collective-permute-start(s16[32,2432]{1,0:T(8,128)(2,1)S(1)} %get-tuple-element.58), channel_id=1, source_target_pairs={{0,192},{64,0},{128,64},{192,128},{1,193},{65,1},{129,65},{193,129... | collective-permute-start | bytes 466952 | tf_op jit(solution)/shard_map/ppermute | solution.py:262
  62.6 5.2 %shard_map.63 = (f32[256,2432]{1,0:T(8,128)S(1)}, f32[8,128]{1,0:T(8,128)S(1)}) custom-call(s32[2]{0:T(128)S(1)} %pad_add_fusion.2.refs_0_, s32[512,64]{1,0:T(8,128)S(1)} %copy.6.refs_1_, f32[512,64]{1,0:T(8,128)S(1)} %copy.7.refs_2_, f32[8,128]{1,0:T(8,128)S(1)} %get-tuple-element.63.refs_3_), custom_call_target="tpu_custom_call" | custom-call | flops 1 | bytes 1 | tf_op jit(solution)/shard_map/pallas_call | solution.py:294
  69.3 3.2 %collective-permute-start.10 = (s16[32,2432]{1,0:T(8,128)(2,1)S(1)}, s16[32,2432]{1,0:T(8,128)(2,1)S(1)}, u32[]{:S(2)}, u32[]{:S(2)}) collective-permute-start(s16[32,2432]{1,0:T(8,128)(2,1)S(1)} %get-tuple-element.69), channel_id=1, source_target_pairs={{0,192},{64,0},{128,64},{192,128},{1,193},{65,1},{129,65},{193,129... | collective-permute-start | bytes 466952 | tf_op jit(solution)/shard_map/ppermute | solution.py:262
  72.5 1.2 shard_map.65
  73.7 1.8 %collective-permute-start.8 = (s16[64,2432]{1,0:T(8,128)(2,1)S(1)}, s16[64,2432]{1,0:T(8,128)(2,1)S(1)}, u32[]{:S(2)}, u32[]{:S(2)}) collective-permute-start(s16[64,2432]{1,0:T(8,128)(2,1)S(1)} %get-tuple-element.66.refs_1_), channel_id=1, source_target_pairs={{0,192},{64,0},{128,64},{192,128},{1,193},{65,1},{129,65},{193,129... | collective-permute-start | bytes 933896 | tf_op jit(solution)/shard_map/ppermute | solution.py:262
  76.7 5.2 %collective-permute-done.10.refs_5_ = s16[32,2432]{1,0:T(8,128)(2,1)S(1)} collective-permute-done((s16[32,2432]{1,0:T(8,128)(2,1)S(1)}, s16[32,2432]{1,0:T(8,128)(2,1)S(1)}, u32[]{:S(2)}, u32[]{:S(2)}) %collective-permute-start.10) | collective-permute-done | bytes 155680 | tf_op jit(solution)/shard_map/ppermute | solution.py:262
  81.9 1.2 shard_map.66
  83.1 2.2 %collective-permute-start.12 = (s16[64,2432]{1,0:T(8,128)(2,1)S(1)}, s16[64,2432]{1,0:T(8,128)(2,1)S(1)}, u32[]{:S(2)}, u32[]{:S(2)}) collective-permute-start(s16[64,2432]{1,0:T(8,128)(2,1)S(1)} %get-tuple-element.72.refs_1_), channel_id=1, source_target_pairs={{0,192},{64,0},{128,64},{192,128},{1,193},{65,1},{129,65},{193,129... | collective-permute-start | bytes 933896 | tf_op jit(solution)/shard_map/ppermute | solution.py:262
  86.1 1.2 collective-permute-done.13.refs_1_
  87.3 26.3 %all_to_all.16.refs_0_ = f32[32,8,128]{2,1,0:T(8,128)S(1)} all-to-all(f32[32,8,128]{2,1,0:T(8,128)S(1)} %broadcast_in_dim.8), channel_id=1, replica_groups=mesh['row'=4,'y'=4,'core'=2,'z_lo'=2,'x'=4] {'y','z_lo','x'}, dimensions={0} | all-to-all | bytes 262144 | tf_op jit(solution)/shard_map/all_to_all | solution.py:375
  113.7 1.9 %collective-permute-start.14 = (s16[64,2432]{1,0:T(8,128)(2,1)S(1)}, s16[64,2432]{1,0:T(8,128)(2,1)S(1)}, u32[]{:S(2)}, u32[]{:S(2)}) collective-permute-start(s16[64,2432]{1,0:T(8,128)(2,1)S(1)} %get-tuple-element.78), channel_id=1, source_target_pairs={{0,64},{64,128},{128,192},{192,0},{1,65},{65,129},{129,193},{193,1... | collective-permute-start | bytes 933896 | tf_op jit(solution)/shard_map/ppermute | solution.py:262
  115.6 2.3 %collective-permute-start.15 = (s16[64,2432]{1,0:T(8,128)(2,1)S(1)}, s16[64,2432]{1,0:T(8,128)(2,1)S(1)}, u32[]{:S(2)}, u32[]{:S(2)}) collective-permute-start(s16[64,2432]{1,0:T(8,128)(2,1)S(1)} %get-tuple-element.79), channel_id=1, source_target_pairs={{0,192},{64,0},{128,64},{192,128},{1,193},{65,1},{129,65},{193,129... | collective-permute-start | bytes 933896 | tf_op jit(solution)/shard_map/ppermute | solution.py:262
  117.9 1.9 %collective-permute-start.18 = (f32[8,128]{1,0:T(8,128)S(1)}, f32[8,128]{1,0:T(8,128)S(1)}, u32[]{:S(2)}, u32[]{:S(2)}) collective-permute-start(f32[8,128]{1,0:T(8,128)S(1)} %get-tuple-element.80.refs_6_), channel_id=1, source_target_pairs={{0,128},{64,192},{128,0},{192,64},{1,129},{65,193},{129,1},{193,65... | collective-permute-start | bytes 12296 | tf_op jit(solution)/shard_map/ppermute | solution.py:262
  119.9 2.3 %collective-permute-start.17 = (f32[8,128]{1,0:T(8,128)S(1)}, f32[8,128]{1,0:T(8,128)S(1)}, u32[]{:S(2)}, u32[]{:S(2)}) collective-permute-start(f32[8,128]{1,0:T(8,128)S(1)} %get-tuple-element.80.refs_6_), channel_id=1, source_target_pairs={{0,192},{64,0},{128,64},{192,128},{1,193},{65,1},{129,65},{193,129... | collective-permute-start | bytes 12296 | tf_op jit(solution)/shard_map/ppermute | solution.py:262
  122.8 8.9 %collective-permute-done.18.refs_9_ = f32[8,128]{1,0:T(8,128)S(1)} collective-permute-done((f32[8,128]{1,0:T(8,128)S(1)}, f32[8,128]{1,0:T(8,128)S(1)}, u32[]{:S(2)}, u32[]{:S(2)}) %collective-permute-start.18) | collective-permute-done | bytes 4128 | tf_op jit(solution)/shard_map/ppermute | solution.py:262
  131.7 2.9 %shard_map.70 = (f32[256,1280]{1,0:T(8,128)S(1)}, bf16[256,2432]{1,0:T(8,128)(2,1)}, f32[8,128]{1,0:T(8,128)S(1)}) custom-call(s32[2]{0:T(128)S(1)} %pad_add_fusion.refs_0_, s16[64,2432]{1,0:T(8,128)(2,1)S(1)} %get-tuple-element.72.refs_1_, s16[64,2432]{1,0:T(8,128)(2,1)S(1)} %collective-permute-done.11.refs_2_, ...), custom_call_target="tpu_custom_call" | custom-call | flops 1 | bytes 1 | tf_op jit(solution)/shard_map/pallas_call | solution.py:294
  134.7 2.9 %shard_map.71 = (f32[256,1280]{1,0:T(8,128)S(1)}, bf16[256,2432]{1,0:T(8,128)(2,1)}, f32[8,128]{1,0:T(8,128)S(1)}) custom-call(s32[2]{0:T(128)S(1)} %pad_add_fusion.refs_0_, s16[64,2432]{1,0:T(8,128)(2,1)S(1)} %get-tuple-element.66.refs_1_, s16[64,2432]{1,0:T(8,128)(2,1)S(1)} %collective-permute-done.7.refs_0_.refs_2_, ...), custom_call_target="tpu_custom_call" | custom-call | flops 1 | bytes 1 | tf_op jit(solution)/shard_map/pallas_call | solution.py:294
  138.7 5.2 %all-to-all-start.2 = ((bf16[32,8,1280]{2,1,0:T(8,128)(2,1)}), bf16[32,8,1280]{2,1,0:T(8,128)(2,1)S(1)}, u32[]{:S(2)}, u32[]{:S(2)}) async-start(bf16[32,8,1280]{2,1,0:T(8,128)(2,1)} %bitcast.6), calls=%async_computation.2 | async-start | bytes 1310720 | tf_op jit(solution)/shard_map/all_to_all | solution.py:387
  143.9 1.3 copy-done.12
  145.2 1.3 copy-done.13
  146.5 5.9 %shard_map.73 = (bf16[2374,1280]{1,0:T(8,128)(2,1)}, f32[8,128]{1,0:T(8,128)S(1)}) custom-call(bf16[256,1280]{1,0:T(8,128)(2,1)S(1)} %bitcast.10, bf16[256,1280]{1,0:T(8,128)(2,1)S(1)} %collective-permute-done.2.refs_1_.act_b_ref, bf16[256,2432]{1,0:T(8,128)(2,1)S(1)} %copy-done.13, bf16[256,2432]{1,0:T(8,128)(2,1)S(1)} %copy-done.12), custom_call_target="tpu_custom_call" | custom-call | flops 3111649280 | bytes 1 | tf_op jit(solution)/shard_map/pallas_call | solution.py:392
  152.4 4.2 %all-to-all-done.2.refs_0_ = bf16[32,8,1280]{2,1,0:T(8,128)(2,1)S(1)} async-done(((bf16[32,8,1280]{2,1,0:T(8,128)(2,1)}), bf16[32,8,1280]{2,1,0:T(8,128)(2,1)S(1)}, u32[]{:S(2)}, u32[]{:S(2)}) %all-to-all-start.2) | async-done | bytes 655392 | tf_op jit(solution)/shard_map/all_to_all | solution.py:387
  (71 shorter events, 14.0 us)
Async XLA Ops:
  22.3 13.7 %collective-permute-start.2 = (bf16[256,1280]{1,0:T(8,128)(2,1)S(1)}, bf16[256,1280]{1,0:T(8,128)(2,1)S(1)}, u32[]{:S(2)}, u32[]{:S(2)}) collective-permute-start(bf16[256,1280]{1,0:T(8,128)(2,1)S(1)} %bitcast.8), channel_id=1, source_target_pairs={{0,8},{8,0},{1,9},{9,1},{2,10},{10,2},{3,11},{11,3},{4,12},{12,4},... | collective-permute-start | bytes 1966088 | tf_op jit(solution)/shard_map/ppermute | solution.py:266
  30.6 9.3 %copy-start = (bf16[2432,1280]{1,0:T(8,128)(2,1)}, bf16[2432,1280]{1,0:T(8,128)(2,1)S(1)}, u32[]{:S(2)}) copy-start(bf16[2432,1280]{1,0:T(8,128)(2,1)S(1)} %get-tuple-element.53.refs_2_.refs_11_) | copy-start | bytes 18677764
  30.6 9.3 %copy-start.4 = (f32[64,2432]{1,0:T(8,128)}, f32[64,2432]{1,0:T(8,128)S(1)}, u32[]{:S(2)}) copy-start(f32[64,2432]{1,0:T(8,128)S(1)} %get-tuple-element.48.refs_1_) | copy-start | bytes 1867780
  30.6 20.7 %collective-permute-start = (s16[64,2432]{1,0:T(8,128)(2,1)}, s16[64,2432]{1,0:T(8,128)(2,1)S(1)}, u32[]{:S(2)}, u32[]{:S(2)}) collective-permute-start(s16[64,2432]{1,0:T(8,128)(2,1)} %get-tuple-element.49), channel_id=1, source_target_pairs={{0,64},{64,128},{128,192},{192,0},{1,65},{65,129},{129,193},{193,1... | collective-permute-start | bytes 933896 | tf_op jit(solution)/shard_map/ppermute | solution.py:262
  33.9 22.1 %collective-permute-start.1 = (s16[64,2432]{1,0:T(8,128)(2,1)}, s16[64,2432]{1,0:T(8,128)(2,1)S(1)}, u32[]{:S(2)}, u32[]{:S(2)}) collective-permute-start(s16[64,2432]{1,0:T(8,128)(2,1)} %get-tuple-element.50), channel_id=1, source_target_pairs={{0,192},{64,0},{128,64},{192,128},{1,193},{65,1},{129,65},{193,129... | collective-permute-start | bytes 933896 | tf_op jit(solution)/shard_map/ppermute | solution.py:262
  36.0 9.6 %copy-start.14 = (s32[512,64]{0,1:T(8,128)S(1)}, s32[512,64]{0,1:T(8,128)}, u32[]{:S(2)}) copy-start(s32[512,64]{0,1:T(8,128)} %param.6) | copy-start | bytes 393220
  36.0 9.7 %copy-start.15 = (f32[512,64]{0,1:T(8,128)S(1)}, f32[512,64]{0,1:T(8,128)}, u32[]{:S(2)}) copy-start(f32[512,64]{0,1:T(8,128)} %param.7) | copy-start | bytes 393220
  41.5 26.3 %collective-permute-start.5 = (s16[64,2432]{1,0:T(8,128)(2,1)}, s16[64,2432]{1,0:T(8,128)(2,1)S(1)}, u32[]{:S(2)}, u32[]{:S(2)}) collective-permute-start(s16[64,2432]{1,0:T(8,128)(2,1)} %get-tuple-element.59), channel_id=1, source_target_pairs={{0,64},{64,128},{128,192},{192,0},{1,65},{65,129},{129,193},{193,1... | collective-permute-start | bytes 933896 | tf_op jit(solution)/shard_map/ppermute | solution.py:262
  42.9 24.9 %collective-permute-start.6 = (s16[64,2432]{1,0:T(8,128)(2,1)}, s16[64,2432]{1,0:T(8,128)(2,1)S(1)}, u32[]{:S(2)}, u32[]{:S(2)}) collective-permute-start(s16[64,2432]{1,0:T(8,128)(2,1)} %get-tuple-element.60), channel_id=1, source_target_pairs={{0,192},{64,0},{128,64},{192,128},{1,193},{65,1},{129,65},{193,129... | collective-permute-start | bytes 933896 | tf_op jit(solution)/shard_map/ppermute | solution.py:262
  45.9 21.9 %copy-start.7 = (f32[32,2432]{1,0:T(8,128)S(1)}, f32[32,2432]{1,0:T(8,128)}, u32[]{:S(2)}) copy-start(f32[32,2432]{1,0:T(8,128)} %copy-done.6) | copy-start | bytes 933892
  45.9 26.6 %copy-start.5 = (f32[64,2432]{1,0:T(8,128)S(1)}, f32[64,2432]{1,0:T(8,128)}, u32[]{:S(2)}) copy-start(f32[64,2432]{1,0:T(8,128)} %copy-done.4) | copy-start | bytes 1867780
  46.1 35.9 %copy-start.3 = (f32[64,2432]{1,0:T(8,128)S(1)}, f32[64,2432]{1,0:T(8,128)}, u32[]{:S(2)}) copy-start(f32[64,2432]{1,0:T(8,128)} %copy-done.2) | copy-start | bytes 1867780
  56.0 1.0 copy-start.9
  58.4 14.1 %collective-permute-start.3 = (s16[32,2432]{1,0:T(8,128)(2,1)S(1)}, s16[32,2432]{1,0:T(8,128)(2,1)S(1)}, u32[]{:S(2)}, u32[]{:S(2)}) collective-permute-start(s16[32,2432]{1,0:T(8,128)(2,1)S(1)} %get-tuple-element.57), channel_id=1, source_target_pairs={{0,64},{64,128},{128,192},{192,0},{1,65},{65,129},{129,193},{193,1... | collective-permute-start | bytes 466952 | tf_op jit(solution)/shard_map/ppermute | solution.py:262
  60.6 11.9 %collective-permute-start.4 = (s16[32,2432]{1,0:T(8,128)(2,1)S(1)}, s16[32,2432]{1,0:T(8,128)(2,1)S(1)}, u32[]{:S(2)}, u32[]{:S(2)}) collective-permute-start(s16[32,2432]{1,0:T(8,128)(2,1)S(1)} %get-tuple-element.58), channel_id=1, source_target_pairs={{0,192},{64,0},{128,64},{192,128},{1,193},{65,1},{129,65},{193,129... | collective-permute-start | bytes 466952 | tf_op jit(solution)/shard_map/ppermute | solution.py:262
  62.6 69.1 %copy-start.1 = (bf16[2432,1280]{1,0:T(8,128)(2,1)S(1)}, bf16[2432,1280]{1,0:T(8,128)(2,1)}, u32[]{:S(2)}) copy-start(bf16[2432,1280]{1,0:T(8,128)(2,1)} %copy-done) | copy-start | bytes 18677764
  68.3 8.4 %collective-permute-start.9 = (s16[32,2432]{1,0:T(8,128)(2,1)S(1)}, s16[32,2432]{1,0:T(8,128)(2,1)S(1)}, u32[]{:S(2)}, u32[]{:S(2)}) collective-permute-start(s16[32,2432]{1,0:T(8,128)(2,1)S(1)} %get-tuple-element.68), channel_id=1, source_target_pairs={{0,64},{64,128},{128,192},{192,0},{1,65},{65,129},{129,193},{193,1... | collective-permute-start | bytes 466952 | tf_op jit(solution)/shard_map/ppermute | solution.py:262
  69.3 12.6 %collective-permute-start.10 = (s16[32,2432]{1,0:T(8,128)(2,1)S(1)}, s16[32,2432]{1,0:T(8,128)(2,1)S(1)}, u32[]{:S(2)}, u32[]{:S(2)}) collective-permute-start(s16[32,2432]{1,0:T(8,128)(2,1)S(1)} %get-tuple-element.69), channel_id=1, source_target_pairs={{0,192},{64,0},{128,64},{192,128},{1,193},{65,1},{129,65},{193,129... | collective-permute-start | bytes 466952 | tf_op jit(solution)/shard_map/ppermute | solution.py:262
  73.7 39.9 %collective-permute-start.8 = (s16[64,2432]{1,0:T(8,128)(2,1)S(1)}, s16[64,2432]{1,0:T(8,128)(2,1)S(1)}, u32[]{:S(2)}, u32[]{:S(2)}) collective-permute-start(s16[64,2432]{1,0:T(8,128)(2,1)S(1)} %get-tuple-element.66.refs_1_), channel_id=1, source_target_pairs={{0,192},{64,0},{128,64},{192,128},{1,193},{65,1},{129,65},{193,129... | collective-permute-start | bytes 933896 | tf_op jit(solution)/shard_map/ppermute | solution.py:262
  75.5 38.1 %collective-permute-start.7 = (s16[64,2432]{1,0:T(8,128)(2,1)S(1)}, s16[64,2432]{1,0:T(8,128)(2,1)S(1)}, u32[]{:S(2)}, u32[]{:S(2)}) collective-permute-start(s16[64,2432]{1,0:T(8,128)(2,1)S(1)} %get-tuple-element.66.refs_1_), channel_id=1, source_target_pairs={{0,64},{64,128},{128,192},{192,0},{1,65},{65,129},{129,193},{193,1... | collective-permute-start | bytes 933896 | tf_op jit(solution)/shard_map/ppermute | solution.py:262
  83.1 30.5 %collective-permute-start.12 = (s16[64,2432]{1,0:T(8,128)(2,1)S(1)}, s16[64,2432]{1,0:T(8,128)(2,1)S(1)}, u32[]{:S(2)}, u32[]{:S(2)}) collective-permute-start(s16[64,2432]{1,0:T(8,128)(2,1)S(1)} %get-tuple-element.72.refs_1_), channel_id=1, source_target_pairs={{0,192},{64,0},{128,64},{192,128},{1,193},{65,1},{129,65},{193,129... | collective-permute-start | bytes 933896 | tf_op jit(solution)/shard_map/ppermute | solution.py:262
  85.3 28.3 %collective-permute-start.11 = (s16[64,2432]{1,0:T(8,128)(2,1)S(1)}, s16[64,2432]{1,0:T(8,128)(2,1)S(1)}, u32[]{:S(2)}, u32[]{:S(2)}) collective-permute-start(s16[64,2432]{1,0:T(8,128)(2,1)S(1)} %get-tuple-element.72.refs_1_), channel_id=1, source_target_pairs={{0,64},{64,128},{128,192},{192,0},{1,65},{65,129},{129,193},{193,1... | collective-permute-start | bytes 933896 | tf_op jit(solution)/shard_map/ppermute | solution.py:262
  86.1 1.2 collective-permute-start.13
  113.7 18.0 %collective-permute-start.14 = (s16[64,2432]{1,0:T(8,128)(2,1)S(1)}, s16[64,2432]{1,0:T(8,128)(2,1)S(1)}, u32[]{:S(2)}, u32[]{:S(2)}) collective-permute-start(s16[64,2432]{1,0:T(8,128)(2,1)S(1)} %get-tuple-element.78), channel_id=1, source_target_pairs={{0,64},{64,128},{128,192},{192,0},{1,65},{65,129},{129,193},{193,1... | collective-permute-start | bytes 933896 | tf_op jit(solution)/shard_map/ppermute | solution.py:262
  115.6 16.1 %collective-permute-start.15 = (s16[64,2432]{1,0:T(8,128)(2,1)S(1)}, s16[64,2432]{1,0:T(8,128)(2,1)S(1)}, u32[]{:S(2)}, u32[]{:S(2)}) collective-permute-start(s16[64,2432]{1,0:T(8,128)(2,1)S(1)} %get-tuple-element.79), channel_id=1, source_target_pairs={{0,192},{64,0},{128,64},{192,128},{1,193},{65,1},{129,65},{193,129... | collective-permute-start | bytes 933896 | tf_op jit(solution)/shard_map/ppermute | solution.py:262
  117.9 13.8 %collective-permute-start.18 = (f32[8,128]{1,0:T(8,128)S(1)}, f32[8,128]{1,0:T(8,128)S(1)}, u32[]{:S(2)}, u32[]{:S(2)}) collective-permute-start(f32[8,128]{1,0:T(8,128)S(1)} %get-tuple-element.80.refs_6_), channel_id=1, source_target_pairs={{0,128},{64,192},{128,0},{192,64},{1,129},{65,193},{129,1},{193,65... | collective-permute-start | bytes 12296 | tf_op jit(solution)/shard_map/ppermute | solution.py:262
  119.9 11.8 %collective-permute-start.17 = (f32[8,128]{1,0:T(8,128)S(1)}, f32[8,128]{1,0:T(8,128)S(1)}, u32[]{:S(2)}, u32[]{:S(2)}) collective-permute-start(f32[8,128]{1,0:T(8,128)S(1)} %get-tuple-element.80.refs_6_), channel_id=1, source_target_pairs={{0,192},{64,0},{128,64},{192,128},{1,193},{65,1},{129,65},{193,129... | collective-permute-start | bytes 12296 | tf_op jit(solution)/shard_map/ppermute | solution.py:262
  122.1 9.6 %collective-permute-start.16 = (f32[8,128]{1,0:T(8,128)S(1)}, f32[8,128]{1,0:T(8,128)S(1)}, u32[]{:S(2)}, u32[]{:S(2)}) collective-permute-start(f32[8,128]{1,0:T(8,128)S(1)} %get-tuple-element.80.refs_6_), channel_id=1, source_target_pairs={{0,64},{64,128},{128,192},{192,0},{1,65},{65,129},{129,193},{193,1... | collective-permute-start | bytes 12296 | tf_op jit(solution)/shard_map/ppermute | solution.py:262
  134.6 3.1 %collective-permute-start.19 = (f32[256,1280]{1,0:T(8,128)S(1)}, f32[256,1280]{1,0:T(8,128)S(1)}, u32[]{:S(2)}, u32[]{:S(2)}) collective-permute-start(f32[256,1280]{1,0:T(8,128)S(1)} %get-tuple-element.86), channel_id=1, source_target_pairs={{0,8},{8,0},{1,9},{9,1},{2,10},{10,2},{3,11},{11,3},{4,12},{12,4},... | collective-permute-start | bytes 3932168 | tf_op jit(solution)/shard_map/ppermute | solution.py:266
  138.7 17.9 %all-to-all-start.2 = ((bf16[32,8,1280]{2,1,0:T(8,128)(2,1)}), bf16[32,8,1280]{2,1,0:T(8,128)(2,1)S(1)}, u32[]{:S(2)}, u32[]{:S(2)}) async-start(bf16[32,8,1280]{2,1,0:T(8,128)(2,1)} %bitcast.6), calls=%async_computation.2 | async-start | bytes 1310720 | tf_op jit(solution)/shard_map/all_to_all | solution.py:387
  143.9 1.3 copy-start.12
  145.2 1.3 copy-start.13
  (5 other events, 4.0 us)
